TPU v7x, 256 devices: a whole 4x4x8 slice. The times are simulated.
256 devices in a mesh: blk: 128 (over z, x, y_lo, core), rep: 2 (over y_hi).
Axes of the slice: x: 4, y: 4 (y_hi: 2, y_lo: 2; y = y_hi * 2 + y_lo), z: 8, core: 2. Of those that a mesh axis runs over, the one named last changes fastest.
Arguments:
- audio_embed: bfloat16 [65536, 512], P(('rep', 'blk')), parts along dimension 0, may hold values from -1.2 to 1.2
- text_embed: bfloat16 [65536, 512], P(('rep', 'blk')), parts along dimension 0, may hold values from -1.2 to 1.2
- audio_head: bfloat16 [512, 512], replicated, may hold values from -0.25 to 0.25
- text_head: bfloat16 [512, 512], replicated, may hold values from -0.25 to 0.25
- audio_lse: bfloat16 [65536], P(('rep', 'blk')), parts along dimension 0, as said below
- text_lse: bfloat16 [65536], P(('rep', 'blk')), parts along dimension 0, as said below
Outputs:
- audio_input_grad: bfloat16 [65536, 512], P(('rep', 'blk')), parts along dimension 0
- text_input_grad: bfloat16 [65536, 512], P(('rep', 'blk')), parts along dimension 0
- audio_head_grad: float32 [1024, 512], P('rep'), parts along dimension 0
- text_head_grad: float32 [1024, 512], P('rep'), parts along dimension 0
There are 2 independent parts, one for each index of `rep`. A program takes and returns all parts, laid end to end along the dimension named above; an argument that names none is the same for every part. Nothing has to cross between parts.
Inputs may be any that keep to these rules, and one draw needn't show every extreme that they name: Each entry of audio_lse lies between log(8192) - 1.5 and log(8192) + 1.0. Each entry of text_lse lies between log(8192) - 1.5 and log(8192) + 1.0.
All inputs are finite; a program needn't handle non-finite values.
Results may differ from a plain program's by a relative error of at most 0.015.
Values may be sent and summed in bfloat16 or wider, within the bound.
No kernel may reach another device: no remote copies, remote signals or barrier semaphores. Data moves between devices by JAX's collectives and lax.ppermute only.
A program may use at most 64 MiB of HBM per device.

v0:
```python
import jax
import jax.numpy as jnp
from jax import lax
from jax.sharding import PartitionSpec as P

logit_scale = 14.2857143


def from_behind(value, axis, steps):
    count = lax.axis_size(axis)
    pairs = [(source, (source + steps) % count) for source in range(count)]
    return lax.ppermute(value, axis, pairs)


def unit_rows(embed, head):
    projected = jnp.dot(embed, head, preferred_element_type=jnp.float32)
    norm_rows = jnp.sqrt(jnp.sum(projected * projected, axis=1, keepdims=True) + 1e-06)
    return (projected / norm_rows, norm_rows)


def tile_weights(left_z, left_lse, right_z, right_lse, diagonal):
    scores = logit_scale * lax.dot_general(
        left_z, right_z, (((1,), (1,)), ((), ())), preferred_element_type=jnp.float32
    )
    mixed = 0.5 * (
        jnp.exp(scores - left_lse.astype(jnp.float32)[:, None])
        + jnp.exp(scores - right_lse.astype(jnp.float32)[None, :])
    )
    return (mixed - diagonal).astype(jnp.bfloat16)


def left_product(weights, right_z):
    return logit_scale * jnp.dot(weights, right_z, preferred_element_type=jnp.float32)


def right_product(weights, left_z):
    return logit_scale * lax.dot_general(
        weights, left_z, (((0,), (0,)), ((), ())), preferred_element_type=jnp.float32
    )


def head_backward(embed, head, unit, norm_rows, grad):
    dproj = ((grad - unit * jnp.sum(unit * grad, axis=1, keepdims=True)) / norm_rows).astype(
        jnp.bfloat16
    )
    input_grad = lax.dot_general(
        dproj, head, (((1,), (1,)), ((), ())), preferred_element_type=jnp.float32
    ).astype(jnp.bfloat16)
    head_sum = lax.dot_general(
        embed, dproj, (((0,), (0,)), ((), ())), preferred_element_type=jnp.float32
    )
    return (input_grad, head_sum)


def local(audio_embed, text_embed, audio_head, text_head, audio_lse, text_lse):
    row_count = audio_embed.shape[0]
    width_blk = lax.axis_size("blk")
    window_len = width_blk // 4
    audio_unit, audio_norm = unit_rows(audio_embed, audio_head)
    text_unit, text_norm = unit_rows(text_embed, text_head)
    audio_z = audio_unit.astype(jnp.bfloat16)
    text_z = text_unit.astype(jnp.bfloat16)
    identity = jnp.eye(row_count, dtype=jnp.float32)
    nothing = jnp.zeros((row_count, row_count), jnp.float32)
    first = tile_weights(audio_z, audio_lse, text_z, text_lse, identity)
    audio_grad = left_product(first, text_z)
    text_acc = right_product(first, audio_z)

    def advance(step, state):
        cur_text, cur_tlse, cur_audio, cur_alse, acc, agrad = state
        cur_text, cur_tlse = from_behind((cur_text, cur_tlse), "blk", -1)
        weights = tile_weights(audio_z, audio_lse, cur_text, cur_tlse, nothing)
        agrad = agrad + left_product(weights, cur_text)
        acc = from_behind(acc, "blk", -1)
        acc = acc + right_product(weights, audio_z)
        return (cur_text, cur_tlse, cur_audio, cur_alse, acc, agrad)

    start_state = (text_z, text_lse, audio_z, audio_lse, text_acc, audio_grad)
    final_state = lax.fori_loop(1, window_len, advance, start_state)
    audio_grad = final_state[5]
    text_grad = from_behind(final_state[4].astype(jnp.bfloat16), "blk", window_len - 1).astype(
        jnp.float32
    )
    audio_input_grad, audio_sum = head_backward(
        audio_embed, audio_head, audio_unit, audio_norm, audio_grad
    )
    text_input_grad, text_sum = head_backward(
        text_embed, text_head, text_unit, text_norm, text_grad
    )
    audio_total, text_total = lax.psum((audio_sum, text_sum), "blk")
    batch_rows = row_count * width_blk
    return (audio_input_grad, text_input_grad, audio_total / batch_rows, text_total / batch_rows)


def solution(mesh):
    placed = (
        P(("rep", "blk"), None),
        P(("rep", "blk"), None),
        P(),
        P(),
        P(("rep", "blk")),
        P(("rep", "blk")),
    )
    return jax.shard_map(
        local,
        mesh=mesh,
        in_specs=placed,
        out_specs=(
            P(("rep", "blk"), None),
            P(("rep", "blk"), None),
            P("rep", None),
            P("rep", None),
        ),
        check_vma=False,
    )
```

profile of v0, /device:TPU:1, one launch (start us, length us, event | category | flops | bytes accessed | tf_op | source)
XLA Modules:
  0.0 1664.4 jit_solution(11369958277092596169)
XLA Ops:
  12.2 535.0 %while.16 = (s32[]{:T(128)}, bf16[256,512]{1,0:T(8,128)(2,1)S(1)}, bf16[256]{0:T(256)(128)(2,1)S(1)}, f32[256,512]{1,0:T(8,128)}, f32[256,512]{1,0:T(8,128)S(1)}...) while((s32[]{:T(128)}, bf16[256,512]{1,0:T(8,128)(2,1)S(1)}, ...), condition=%wide.region_3.0_spmd, body=%wide.region_2.0_spmd.sunk | while | flops 202244608 | bytes 7217357 | solution.py:79
  15.4 6.8 collective-permute-start.2
  26.8 6.7 collective-permute-start
  44.1 6.7 collective-permute-start
  61.5 6.7 collective-permute-start
  78.8 6.6 collective-permute-start
  96.2 6.7 collective-permute-start
  113.5 6.7 collective-permute-start
  130.9 6.6 collective-permute-start
  148.2 6.7 collective-permute-start
  165.6 6.7 collective-permute-start
  182.9 6.6 collective-permute-start
  200.3 6.7 collective-permute-start
  217.6 6.7 collective-permute-start
  235.0 6.6 collective-permute-start
  252.3 6.7 collective-permute-start
  269.7 6.7 collective-permute-start
  287.0 6.6 collective-permute-start
  304.3 6.7 collective-permute-start
  321.7 6.7 collective-permute-start
  356.4 6.7 collective-permute-start
  373.7 6.7 collective-permute-start
  391.1 6.6 collective-permute-start
  408.4 6.7 collective-permute-start
  425.8 6.7 collective-permute-start
  443.1 6.6 collective-permute-start
  460.5 6.7 collective-permute-start
  477.8 6.7 collective-permute-start
  512.5 6.7 collective-permute-start
  529.9 6.7 collective-permute-start
  550.8 7.5 collective-permute-done.3
  562.9 1090.6 %all-reduce.3.cloned.1.call-done = (f32[512,512]{0,1:T(8,128)}, f32[512,512]{0,1:T(8,128)}) async-done(((f32[512,512]{0,1:T(8,128)}, f32[512,512]{0,1:T(8,128)}), (f32[512,512]{0,1:T(8,128)}, f32[512,512]{0,1:T(8,128)})) %all-reduce.3.cloned.1.call-update) | async-done | bytes 2097168 | tf_op jit(solution)/shard_map/psum | solution.py:90
  (417 shorter events, 358.0 us)
Async XLA Ops:
  7.2 1646.3 %all-reduce.3.cloned.1.call-start = ((), (), s32[]{:S(2)}) async-start(), calls=%async_computation | async-start | bytes 4194304 | tf_op jit(solution)/shard_map/psum | solution.py:90
  12.2 13.0 collective-permute-start
  26.8 15.7 collective-permute-start
  44.1 15.7 collective-permute-start
  61.5 15.7 collective-permute-start
  78.8 15.7 collective-permute-start
  96.2 15.7 collective-permute-start
  113.5 15.7 collective-permute-start
  130.9 15.7 collective-permute-start
  148.2 15.7 collective-permute-start
  165.6 15.7 collective-permute-start
  182.9 15.7 collective-permute-start
  200.3 15.7 collective-permute-start
  217.6 15.7 collective-permute-start
  235.0 15.7 collective-permute-start
  252.3 15.7 collective-permute-start
  269.7 15.7 collective-permute-start
  287.0 15.7 collective-permute-start
  304.3 15.7 collective-permute-start
  321.7 15.7 collective-permute-start
  339.1 15.7 collective-permute-start
  356.4 15.7 collective-permute-start
  373.7 15.7 collective-permute-start
  391.1 15.7 collective-permute-start
  408.4 15.7 collective-permute-start
  425.8 15.7 collective-permute-start
  443.1 15.7 collective-permute-start
  460.5 15.7 collective-permute-start
  477.8 15.7 collective-permute-start
  495.2 15.7 collective-permute-start
  512.5 15.7 collective-permute-start
  529.9 15.7 collective-permute-start
  (71 other events, 410.7 us)
Sparse Core Ops, SparseCore 0:
  560.9 1092.4 all-reduce.2
where the time goes:
time: 1670 us; the launch traced here: 1660 us
  waiting for transfers between devices  1190 us (71%)
  starting transfers between devices  394 us (24%)
  matrix products  57 us (3%)
    psum x1, waiting for transfers between devices, local(): audio_total, text_total = lax.psum((audio_sum, text_sum), 'blk')  1090 us
    ppermute x94, starting transfers between devices, from_behind(): return lax.ppermute(value, axis, pairs)  394 us
    ppermute x94, waiting for transfers between devices, from_behind(): return lax.ppermute(value, axis, pairs)  97.8 us
    dot_general x32, matrix products, right_product(): lax.dot_general(weights, left_z, (((0,), (0,)), ((), ())), preferred_elem...  33.5 us
  transfers between devices with their start and end apart: 95, of which 33 were waited for; matrix products, arithmetic and copies ran while one was open for 1% of the time, Pallas kernels for 0%

commit v1 on v0

v1 whole, which is shorter than its diff:
```python
import functools

import jax
import jax.numpy as jnp
from jax import lax
from jax.experimental import pallas as pl
from jax.experimental.pallas import tpu as pltpu
from jax.sharding import Mesh, PartitionSpec as P

logit_scale = 14.2857143
log2_e = 1.4426950408889634
PAD = 16

BF = jnp.bfloat16
F32 = jnp.float32
XY = ("x", "yl")


def shift(value, axis, steps):
    count = lax.axis_size(axis)
    return lax.ppermute(value, axis, [(i, (i + steps) % count) for i in range(count)])


def exchange(value, axis):
    return lax.all_to_all(value, axis, split_axis=0, concat_axis=0, tiled=True)


def dot_nn(a, b):
    return jnp.dot(a, b, preferred_element_type=F32)


def dot_nt(a, b):
    return lax.dot_general(a, b, (((1,), (1,)), ((), ())), preferred_element_type=F32)


def dot_tn(a, b):
    return lax.dot_general(a, b, (((0,), (0,)), ((), ())), preferred_element_type=F32)


def tiles_kernel(inv_rows, sel_ref, *refs):
    audio = refs[:5]
    text = refs[5:13]
    ha_ref, ht_ref = refs[13:15]
    da_ref, dt_ref, head_ref = refs[15:18]
    za, zat, zt, ua, ut, na, nt, ea, eb, ga, gt = refs[18:]
    rows, width = za.shape[1], za.shape[2]

    for i in range(5):
        p = dot_nn(audio[i][:rows, :], ha_ref[...])
        inv = lax.rsqrt(jnp.sum(p * p, axis=1, keepdims=True) + 1e-06)
        u = p * inv
        z = u.astype(BF)
        ua[i] = u
        za[i] = z
        zat[i] = z.T
        na[i] = jnp.broadcast_to(inv, na.shape[1:])
        lse = audio[i][rows : rows + PAD, :rows].astype(F32)[0:1, :]
        half = 0.5 * jnp.exp(-lse)
        ea[i] = jnp.broadcast_to(half, (ea.shape[2], rows)).T
    for j in range(4):
        for plane in range(2):
            block = text[4 * plane + j]
            cols = slice(plane * rows, (plane + 1) * rows)
            p = dot_nt(ht_ref[...], block[:rows, :])
            inv = lax.rsqrt(jnp.sum(p * p, axis=0, keepdims=True) + 1e-06)
            u = p * inv
            ut[j, :, cols] = u
            zt[j, :, cols] = u.astype(BF)
            nt[j, :, cols] = jnp.broadcast_to(inv, (8, rows))
            lse = block[rows : rows + PAD, :rows].astype(F32)[0:1, :]
            eb[j, :, cols] = jnp.broadcast_to(0.5 * jnp.exp(-lse), (8, rows))

    ga[...] = jnp.zeros_like(ga)
    row_id = lax.broadcasted_iota(jnp.int32, (rows, 2 * rows), 0)
    col_id = lax.broadcasted_iota(jnp.int32, (rows, 2 * rows), 1)
    eye = (row_id == col_id).astype(F32)

    def chunk(j, carry):
        columns = zt[j]
        col_scale = eb[j, 0:1, :]
        own = sel_ref[j]
        acc = None
        for r in range(4):
            i = own if r == 0 else r + 1
            s = dot_nn(za[i], columns)
            e = jnp.exp2(s * (logit_scale * log2_e))
            row_scale = ea[i]
            scale = jnp.concatenate([row_scale] * (2 * rows // row_scale.shape[1]), axis=1)
            w = e * (scale + col_scale)
            if r == 0:
                w = w - eye * jnp.where(j == 0, 1.0, 0.0)
            w = w.astype(BF)
            ga[i] += dot_nt(w, columns)
            part = dot_nn(zat[i], w)
            acc = part if acc is None else acc + part
        gt[j] = acc
        return carry

    lax.fori_loop(0, 4, chunk, 0)

    head = None
    for i in range(5):
        g = ga[i]
        u = ua[i]
        along = jnp.sum(u * g, axis=1, keepdims=True)
        d = ((g - u * along) * (na[i][:, 0:1] * logit_scale)).astype(BF)
        da_ref[i] = d
        part = dot_tn(audio[i][:rows, :], d)
        head = part if head is None else head + part
    head_ref[0] = (head * inv_rows).astype(BF)
    head = None
    for j in range(4):
        g = gt[j]
        u = ut[j]
        along = jnp.sum(u * g, axis=0, keepdims=True)
        d = ((g - u * along) * (nt[j, 0:1, :] * logit_scale)).astype(BF)
        for plane in range(2):
            part_d = d[:, plane * rows : (plane + 1) * rows]
            dt_ref[2 * j + plane] = part_d
            part = dot_nn(part_d, text[4 * plane + j][:rows, :])
            head = part if head is None else head + part
    head_ref[1] = (head * inv_rows).T.astype(BF)


def tiles(sel, audio, text, audio_head, text_head_t, batch_rows):
    rows, width = audio[0].shape[0] - PAD, audio[0].shape[1]
    lanes = min(128, rows)
    vmem = pl.BlockSpec(memory_space=pltpu.VMEM)
    return pl.pallas_call(
        functools.partial(tiles_kernel, 1.0 / batch_rows),
        out_shape=(
            jax.ShapeDtypeStruct((5, rows, width), BF),
            jax.ShapeDtypeStruct((8, width, rows), BF),
            jax.ShapeDtypeStruct((2, width, width), BF),
        ),
        in_specs=[pl.BlockSpec(memory_space=pltpu.SMEM)] + [vmem] * 15,
        out_specs=(vmem, vmem, vmem),
        scratch_shapes=[
            pltpu.VMEM((5, rows, width), BF),
            pltpu.VMEM((5, width, rows), BF),
            pltpu.VMEM((4, width, 2 * rows), BF),
            pltpu.VMEM((5, rows, width), F32),
            pltpu.VMEM((4, width, 2 * rows), F32),
            pltpu.VMEM((5, rows, lanes), F32),
            pltpu.VMEM((4, 8, 2 * rows), F32),
            pltpu.VMEM((5, rows, lanes), F32),
            pltpu.VMEM((4, 8, 2 * rows), F32),
            pltpu.VMEM((5, rows, width), F32),
            pltpu.VMEM((4, width, 2 * rows), F32),
        ],
        compiler_params=pltpu.CompilerParams(vmem_limit_bytes=48 * 1024 * 1024),
        cost_estimate=pl.CostEstimate(
            flops=12_000_000_000, bytes_accessed=9_000_000, transcendentals=2_100_000
        ),
    )(sel, *audio, *text, audio_head, text_head_t)


def packed(embed, lse):
    extra = jnp.pad(lse[None, :], ((0, PAD - 1), (0, embed.shape[1] - lse.shape[0])))
    return jnp.concatenate([embed, extra], axis=0)


def summed(parts):
    return jnp.sum(parts.astype(F32), axis=0)


def head_total(head):
    core = lax.axis_index("c")
    width = head.shape[1]
    keep = lax.dynamic_index_in_dim(head, core, 0, keepdims=False)
    send = lax.dynamic_index_in_dim(head, 1 - core, 0, keepdims=False)
    mine = (keep.astype(F32) + shift(send, "c", 1).astype(F32)).astype(BF)
    part = summed(exchange(mine, XY).reshape(8, width // 8, width)).astype(BF)
    part = summed(exchange(part, "z").reshape(8, width // 64, width)).astype(BF)
    part = exchange(jnp.broadcast_to(part[None], (8,) + part.shape).reshape(width // 8, width), "z")
    part = exchange(jnp.broadcast_to(part[None], (8,) + part.shape).reshape(width, width), XY)
    other = shift(part, "c", 1)
    first = jnp.where(core == 0, part, other).astype(F32)
    second = jnp.where(core == 0, other, part).astype(F32)
    return first, second


def local(audio_embed, text_embed, audio_head, text_head, audio_lse, text_lse):
    rows = audio_embed.shape[0]
    blocks = lax.axis_size(("z", "x", "yl", "c"))
    x = lax.axis_index("x")
    yl = lax.axis_index("yl")
    core = lax.axis_index("c")

    a_own = packed(audio_embed, audio_lse)
    t_own = packed(text_embed, text_lse)
    t_next = shift(t_own, "z", -1)
    a_prev = shift(a_own, "z", 1)
    t_y = shift(t_own, "yl", 1)
    t_next, a_prev, t_y = lax.optimization_barrier((t_next, a_prev, t_y))
    t_next_y = shift(t_next, "yl", 1)
    a_x = [shift(jnp.where(x + s < 4, a_own, a_prev), "x", s) for s in (1, 2, 3)]
    here = [t_own, t_y]
    here += [shift(v, "c", 1) for v in here]
    ahead = [t_next, t_next_y]
    ahead += [shift(v, "c", 1) for v in ahead]

    behind = [jnp.int32(0), (yl == 1).astype(jnp.int32), (core == 1).astype(jnp.int32), (yl == 1).astype(jnp.int32)]
    da, dt, head = tiles(
        jnp.stack(behind), [a_own, a_prev] + a_x, here + ahead, audio_head, text_head.T, rows * blocks
    )

    audio_total, text_total = head_total(head)

    dt_mine, dt_send = dt[:4], dt[4:]
    dt_sum = (dt_mine.astype(F32) + shift(dt_send, "c", 1).astype(F32)).astype(BF)
    dt_pair = dt_sum[:2].astype(F32) + shift(dt_sum[2:], "yl", 1).astype(F32)
    dt_full = dt_pair[0] + shift(dt_pair[1].astype(BF), "z", 1).astype(F32)
    text_input = lax.dot_general(
        dt_full.astype(BF), text_head, (((0,), (1,)), ((), ())), preferred_element_type=F32
    ).astype(BF)

    back = [shift(da[1 + s], "x", -s).astype(F32) for s in (1, 2, 3)]
    here_sum, behind_sum = da[0].astype(F32), da[1].astype(F32)
    for s in (1, 2, 3):
        wrapped = x + s >= 4
        here_sum = here_sum + jnp.where(wrapped, 0.0, back[s - 1])
        behind_sum = behind_sum + jnp.where(wrapped, back[s - 1], 0.0)
    da_full = here_sum + shift(behind_sum.astype(BF), "z", -1).astype(F32)
    audio_input = dot_nt(da_full.astype(BF), audio_head).astype(BF)
    return audio_input, text_input, audio_total, text_total


def solution(mesh):
    sizes = (8, 4, 2, 2, mesh.shape["rep"])
    grid = Mesh(mesh.devices.reshape(sizes), ("z", "x", "yl", "c", "rep"))
    every = ("rep", "z", "x", "yl", "c")
    return jax.shard_map(
        local,
        mesh=grid,
        in_specs=(P(every, None), P(every, None), P(), P(), P(every), P(every)),
        out_specs=(P(every, None), P(every, None), P("rep", None), P("rep", None)),
        check_vma=False,
    )
```

time: 1670 us -> 128 us (0.08)
  waiting for transfers between devices: 1190 us -> 30.8 us
  starting transfers between devices: 394 us -> 50.9 us
  matrix products: 57 us -> 4.37 us
  Pallas kernels: 0 us -> 17 us
    psum x1 -> x0, waiting for transfers between devices: 1090 us -> none  [local(): audio_total, text_total = lax.psum((audio_sum, text_sum), 'blk')]
    ppermute x94 -> x20, starting transfers between devices: 394 us -> 35.5 us  [shift(): lax.ppermute(value, axis, [(i, (i + steps) % count) for i in range(count)])]
    ppermute x94 -> x20, waiting for transfers between devices: 97.8 us -> 15.3 us  [shift(): lax.ppermute(value, axis, [(i, (i + steps) % count) for i in range(count)])]
    dot_general x102 -> x2, matrix products: 57 us -> 4.37 us  [the longest x1 2.36 us: dot_nt(): lax.dot_general(a, b, (((1,), (1,)), ((), ())), preferred_element_type=F32)]
    pallas_call x0 -> x1, Pallas kernels: none -> 17 us  [tiles(): pl.pallas_call(functools.partial(tiles_kernel, 1.0 / batch_rows), out_sha...]
  transfers between devices with their start and end apart: 95 -> 24, of which waited for: 33 -> 10; matrix products, arithmetic and copies ran while one was open for 1% -> 16% of each run, Pallas kernels for 0% -> 0%
where the time goes in v1:
time: 128 us; the launch traced here: 127 us
  starting transfers between devices  50.9 us (40%)
  waiting for transfers between devices  30.8 us (24%)
  Pallas kernels  17 us (13%)
  other arithmetic  12.1 us (9%)
  local copies, waits for them, and re-layouts  10.9 us (9%)
  matrix products  4.37 us (3%)
    ppermute x20, starting transfers between devices, shift(): lax.ppermute(value, axis, [(i, (i + steps) % count) for i in range(count)])  35.5 us
    pallas_call x1, Pallas kernels, tiles(): pl.pallas_call(functools.partial(tiles_kernel, 1.0 / batch_rows), out_sha...  17 us
    all_to_all x4, waiting for transfers between devices, exchange(): return lax.all_to_all(value, axis, split_axis=0, concat_axis=0, tiled=True)  15.6 us
    all_to_all x4, starting transfers between devices, exchange(): return lax.all_to_all(value, axis, split_axis=0, concat_axis=0, tiled=True)  15.4 us
    ppermute x20, waiting for transfers between devices, shift(): lax.ppermute(value, axis, [(i, (i + steps) % count) for i in range(count)])  15.3 us
    unnamed x19, local copies, waits for them, and re-layouts  4.14 us
  transfers between devices with their start and end apart: 24, of which 10 were waited for; matrix products, arithmetic and copies ran while one was open for 16% of the time, Pallas kernels for 0%

profile of v1, /device:TPU:1, one launch (start us, length us, event | category | flops | bytes accessed | tf_op | source)
XLA Modules:
  0.0 126.9 jit_solution(5982058029728571180)
XLA Ops:
  2.3 6.5 %collective-permute-start = (bf16[272,512]{1,0:T(8,128)(2,1)S(1)}, bf16[272,512]{1,0:T(8,128)(2,1)S(1)}, u32[]{:S(2)}, u32[]{:S(2)}) collective-permute-start(bf16[272,512]{1,0:T(8,128)(2,1)S(1)} %fusion.15.refs_5_), channel_id=1, source_target_pairs={{0,224},{32,0},{64,32},{96,64},{128,96},{160,128},{192,160},{224,1... | collective-permute-start | bytes 835592 | tf_op jit(solution)/shard_map/ppermute | solution.py:21
  8.8 1.3 %collective-permute-start.2 = (bf16[272,512]{1,0:T(8,128)(2,1)S(1)}, bf16[272,512]{1,0:T(8,128)(2,1)S(1)}, u32[]{:S(2)}, u32[]{:S(2)}) collective-permute-start(bf16[272,512]{1,0:T(8,128)(2,1)S(1)} %fusion.15.refs_5_), channel_id=1, source_target_pairs={{0,4},{4,0},{1,5},{5,1},{2,6},{6,2},{3,7},{7,3},{8,12},{12,8},{9,1... | collective-permute-start | bytes 835592 | tf_op jit(solution)/shard_map/ppermute | solution.py:21
  11.8 1.3 %collective-permute-start.6 = (bf16[272,512]{1,0:T(8,128)(2,1)S(1)}, bf16[272,512]{1,0:T(8,128)(2,1)S(1)}, u32[]{:S(2)}, u32[]{:S(2)}) collective-permute-start(bf16[272,512]{1,0:T(8,128)(2,1)S(1)} %fusion.15.refs_5_), channel_id=1, source_target_pairs={{0,2},{2,0},{1,3},{3,1},{4,6},{6,4},{5,7},{7,5},{8,10},{10,8},{9,1... | collective-permute-start | bytes 835592 | tf_op jit(solution)/shard_map/ppermute | solution.py:21
  14.1 1.9 %collective-permute-done.2.refs_6_ = bf16[272,512]{1,0:T(8,128)(2,1)S(1)} collective-permute-done((bf16[272,512]{1,0:T(8,128)(2,1)S(1)}, bf16[272,512]{1,0:T(8,128)(2,1)S(1)}, u32[]{:S(2)}, u32[]{:S(2)}) %collective-permute-start.2) | collective-permute-done | bytes 278560 | tf_op jit(solution)/shard_map/ppermute | solution.py:21
  16.0 3.9 %collective-permute-done.1.refs_1_ = bf16[272,512]{1,0:T(8,128)(2,1)S(1)} collective-permute-done((bf16[272,512]{1,0:T(8,128)(2,1)S(1)}, bf16[272,512]{1,0:T(8,128)(2,1)S(1)}, u32[]{:S(2)}, u32[]{:S(2)}) %collective-permute-start.1) | collective-permute-done | bytes 278560 | tf_op jit(solution)/shard_map/ppermute | solution.py:21
  19.9 1.9 %broadcast_select_fusion = (bf16[272,512]{1,0:T(8,128)(2,1)}, bf16[272,512]{1,0:T(8,128)(2,1)}, bf16[272,512]{1,0:T(8,128)(2,1)S(1)}) fusion(bf16[272,512]{1,0:T(8,128)(2,1)S(1)} %collective-permute-done.1.refs_1_, pred[]{:T(512)S(6)} %lt.18, bf16[1,256]{1,0:T(2,128)(2,1)S(1)} %broadcast_in_dim.30, bf16[256,512]{1,0:T(8,128)(2,1)} %param.6, pred[]{:T(512)S(6)} %lt.17, ...), kind=kLoop, calls=%fused_computation.33 | loop fusion | flops 1253376 | bytes 1376771 | tf_op jit(solution)/shard_map/jit(_where)/select_n | solution.py:197
  21.8 1.2 collective-permute-start.3
  23.2 2.7 %collective-permute-start.9 = (bf16[272,512]{1,0:T(8,128)(2,1)S(1)}, bf16[272,512]{1,0:T(8,128)(2,1)}, u32[]{:S(2)}, u32[]{:S(2)}) collective-permute-start(bf16[272,512]{1,0:T(8,128)(2,1)S(1)} %collective-permute-done.refs_9_), channel_id=1, source_target_pairs={{0,2},{2,0},{1,3},{3,1},{4,6},{6,4},{5,7},{7,5},{8,10},{10,8},{9,1... | collective-permute-start | bytes 835592 | tf_op jit(solution)/shard_map/ppermute | solution.py:21
  25.9 2.5 %collective-permute-start.4 = (bf16[272,512]{1,0:T(8,128)(2,1)}, bf16[272,512]{1,0:T(8,128)(2,1)}, u32[]{:S(2)}, u32[]{:S(2)}) collective-permute-start(bf16[272,512]{1,0:T(8,128)(2,1)} %get-tuple-element.22), channel_id=1, source_target_pairs={{0,16},{8,24},{16,0},{24,8},{1,17},{9,25},{17,1},{25,9},{2,18},{10... | collective-permute-start | bytes 835592 | tf_op jit(solution)/shard_map/ppermute | solution.py:21
  29.5 3.9 %collective-permute-start.7 = (bf16[272,512]{1,0:T(8,128)(2,1)S(1)}, bf16[272,512]{1,0:T(8,128)(2,1)}, u32[]{:S(2)}, u32[]{:S(2)}) collective-permute-start(bf16[272,512]{1,0:T(8,128)(2,1)S(1)} %collective-permute-done.2.refs_6_), channel_id=1, source_target_pairs={{0,2},{2,0},{1,3},{3,1},{4,6},{6,4},{5,7},{7,5},{8,10},{10,8},{9,1... | collective-permute-start | bytes 835592 | tf_op jit(solution)/shard_map/ppermute | solution.py:21
  33.8 1.3 copy.11
  35.1 1.3 %collective-permute-done.4.refs_3_ = bf16[272,512]{1,0:T(8,128)(2,1)} collective-permute-done((bf16[272,512]{1,0:T(8,128)(2,1)}, bf16[272,512]{1,0:T(8,128)(2,1)}, u32[]{:S(2)}, u32[]{:S(2)}) %collective-permute-start.4) | collective-permute-done | bytes 278560 | tf_op jit(solution)/shard_map/ppermute | solution.py:21
  36.4 4.7 %collective-permute-done.5.refs_4_ = bf16[272,512]{1,0:T(8,128)(2,1)} collective-permute-done((bf16[272,512]{1,0:T(8,128)(2,1)}, bf16[272,512]{1,0:T(8,128)(2,1)}, u32[]{:S(2)}, u32[]{:S(2)}) %collective-permute-start.5) | collective-permute-done | bytes 278560 | tf_op jit(solution)/shard_map/ppermute | solution.py:21
  44.0 17.0 %shard_map.93 = (bf16[5,256,512]{2,1,0:T(8,128)(2,1)}, bf16[8,512,256]{2,1,0:T(8,128)(2,1)}, bf16[2,512,512]{2,1,0:T(8,128)(2,1)S(1)}) custom-call(s32[4]{0:T(128)S(1)} %add_convert_fusion.1.sel_ref, bf16[272,512]{1,0:T(8,128)(2,1)S(1)} %fusion.14.refs_0_, bf16[272,512]{1,0:T(8,128)(2,1)S(1)} %collective-permute-done.1.refs_1_, ...), custom_call_target="tpu_custom_call" | custom-call | flops 12000000000 | bytes 9000000 | tf_op jit(solution)/shard_map/pallas_call | solution.py:129
  61.0 1.3 %slice.40 = bf16[4,512,256]{2,1,0:T(8,128)(2,1)S(1)} slice(bf16[8,512,256]{2,1,0:T(8,128)(2,1)} %get-tuple-element.14), slice={[4:8], [0:512], [0:256]} | slice | bytes 2097152 | tf_op jit(solution)/shard_map/slice | solution.py:210
  64.1 2.4 %collective-permute-done.18 = bf16[512,512]{1,0:T(8,128)(2,1)S(1)} collective-permute-done((bf16[512,512]{1,0:T(8,128)(2,1)}, bf16[512,512]{1,0:T(8,128)(2,1)S(1)}, u32[]{:S(2)}, u32[]{:S(2)}) %collective-permute-start.18) | collective-permute-done | bytes 524320 | tf_op jit(solution)/shard_map/ppermute | solution.py:21
  67.4 5.0 %all-to-all-start = ((bf16[8,64,512]{2,1,0:T(8,128)(2,1)}), bf16[8,64,512]{2,1,0:T(8,128)(2,1)S(1)}, u32[]{:S(2)}, u32[]{:S(2)}) async-start(bf16[8,64,512]{2,1,0:T(8,128)(2,1)} %bitcast.12), calls=%async_computation | async-start | bytes 1048576 | tf_op jit(solution)/shard_map/all_to_all | solution.py:25
  72.4 1.9 %add_convert_fusion = bf16[4,512,256]{2,1,0:T(8,128)(2,1)S(1)} fusion(bf16[4,512,256]{2,1,0:T(8,128)(2,1)} %collective-permute-done.15, bf16[8,512,256]{2,1,0:T(8,128)(2,1)} %get-tuple-element.14), kind=kLoop, calls=%fused_computation | loop fusion | flops 2097152 | bytes 3145728 | tf_op jit(solution)/shard_map/convert_element_type | solution.py:211
  75.2 1.5 %collective-permute-start.16 = (bf16[2,512,256]{2,1,0:T(8,128)(2,1)}, bf16[2,512,256]{2,1,0:T(8,128)(2,1)}, u32[]{:S(2)}, u32[]{:S(2)}) collective-permute-start(bf16[2,512,256]{2,1,0:T(8,128)(2,1)} %slice.46), channel_id=1, source_target_pairs={{0,4},{4,0},{1,5},{5,1},{2,6},{6,2},{3,7},{7,3},{8,12},{12,8},{9,1... | collective-permute-start | bytes 1572872 | tf_op jit(solution)/shard_map/ppermute | solution.py:21
  77.5 2.4 %collective-permute-start.11 = (bf16[256,512]{1,0:T(8,128)(2,1)}, bf16[256,512]{1,0:T(8,128)(2,1)}, u32[]{:S(2)}, u32[]{:S(2)}) collective-permute-start(bf16[256,512]{1,0:T(8,128)(2,1)} %get-tuple-element.18), channel_id=1, source_target_pairs={{0,24},{8,0},{16,8},{24,16},{1,25},{9,1},{17,9},{25,17},{2,26},{10... | collective-permute-start | bytes 786440 | tf_op jit(solution)/shard_map/ppermute | solution.py:21
  82.3 3.4 %all-to-all-start.1 = ((bf16[8,8,512]{2,1,0:T(8,128)(2,1)}), bf16[8,8,512]{2,1,0:T(8,128)(2,1)S(1)}, u32[]{:S(2)}, u32[]{:S(2)}) async-start(bf16[8,8,512]{2,1,0:T(8,128)(2,1)} %bitcast.13), calls=%async_computation.1 | async-start | bytes 131072 | tf_op jit(solution)/shard_map/all_to_all | solution.py:25
  85.7 7.1 %all-to-all-done.1 = bf16[8,8,512]{2,1,0:T(8,128)(2,1)S(1)} async-done(((bf16[8,8,512]{2,1,0:T(8,128)(2,1)}), bf16[8,8,512]{2,1,0:T(8,128)(2,1)S(1)}, u32[]{:S(2)}, u32[]{:S(2)}) %all-to-all-start.1) | async-done | bytes 65568 | tf_op jit(solution)/shard_map/all_to_all | solution.py:25
  93.5 3.6 %all-to-all-start.2 = ((bf16[8,8,512]{2,1,0:T(8,128)(2,1)}), bf16[8,8,512]{2,1,0:T(8,128)(2,1)S(1)}, u32[]{:S(2)}, u32[]{:S(2)}) async-start(bf16[8,8,512]{2,1,0:T(8,128)(2,1)} %broadcast_in_dim.33), calls=%async_computation.2 | async-start | bytes 131072 | tf_op jit(solution)/shard_map/all_to_all | solution.py:25
  97.1 2.0 %fusion.11 = bf16[256,512]{1,0:T(8,128)(2,1)} fusion(bf16[256,512]{1,0:T(8,128)(2,1)} %collective-permute-done.11, bf16[256,512]{1,0:T(8,128)(2,1)} %collective-permute-done.12, bf16[256,512]{1,0:T(8,128)(2,1)} %collective-permute-done.13, bf16[5,256,512]{2,1,0:T(8,128)(2,1)S(1)} %copy-done.8, pred[]{:T(512)S(6)} %ge.11, pred[]{:T(512)S(6)} %ge.10, pred[]{:T(512)S(6)} %ge.9), kind=kLoop, calls=%fused_computation.23 | loop fusion | flops 1441792 | bytes 1310723 | tf_op jit(solution)/shard_map/convert_element_type | solution.py:224
  99.1 2.4 %collective-permute-start.14 = (bf16[256,512]{1,0:T(8,128)(2,1)}, bf16[256,512]{1,0:T(8,128)(2,1)}, u32[]{:S(2)}, u32[]{:S(2)}) collective-permute-start(bf16[256,512]{1,0:T(8,128)(2,1)} %fusion.11), channel_id=1, source_target_pairs={{0,224},{32,0},{64,32},{96,64},{128,96},{160,128},{192,160},{224,1... | collective-permute-start | bytes 786440 | tf_op jit(solution)/shard_map/ppermute | solution.py:21
  101.5 2.5 %all-to-all-done.2 = bf16[8,8,512]{2,1,0:T(8,128)(2,1)S(1)} async-done(((bf16[8,8,512]{2,1,0:T(8,128)(2,1)}), bf16[8,8,512]{2,1,0:T(8,128)(2,1)S(1)}, u32[]{:S(2)}, u32[]{:S(2)}) %all-to-all-start.2) | async-done | bytes 65568 | tf_op jit(solution)/shard_map/all_to_all | solution.py:25
  104.9 3.5 %all-to-all-start.3 = ((bf16[8,64,512]{2,1,0:T(8,128)(2,1)}), bf16[8,64,512]{2,1,0:T(8,128)(2,1)S(1)}, u32[]{:S(2)}, u32[]{:S(2)}) async-start(bf16[8,64,512]{2,1,0:T(8,128)(2,1)} %broadcast_in_dim.35), calls=%async_computation.3 | async-start | bytes 1048576 | tf_op jit(solution)/shard_map/all_to_all | solution.py:25
  109.9 5.4 %all-to-all-done.3 = bf16[8,64,512]{2,1,0:T(8,128)(2,1)S(1)} async-done(((bf16[8,64,512]{2,1,0:T(8,128)(2,1)}), bf16[8,64,512]{2,1,0:T(8,128)(2,1)S(1)}, u32[]{:S(2)}, u32[]{:S(2)}) %all-to-all-start.3) | async-done | bytes 524320 | tf_op jit(solution)/shard_map/all_to_all | solution.py:25
  115.3 5.7 %collective-permute-start.19 = (bf16[512,512]{1,0:T(8,128)(2,1)S(1)}, bf16[512,512]{1,0:T(8,128)(2,1)S(1)}, u32[]{:S(2)}, u32[]{:S(2)}) collective-permute-start(bf16[512,512]{1,0:T(8,128)(2,1)S(1)} %bitcast.41), channel_id=1, source_target_pairs={{0,2},{2,0},{1,3},{3,1},{4,6},{6,4},{5,7},{7,5},{8,10},{10,8},{9,1... | collective-permute-start | bytes 1572872 | tf_op jit(solution)/shard_map/ppermute | solution.py:21
  121.0 2.4 %convolution_convert_fusion.1 = bf16[256,512]{1,0:T(8,128)(2,1)} fusion(bf16[512,512]{1,0:T(8,128)(2,1)S(1)} %copy-done, bf16[256,512]{1,0:T(8,128)(2,1)} %collective-permute-done.11, bf16[256,512]{1,0:T(8,128)(2,1)} %collective-permute-done.12, bf16[256,512]{1,0:T(8,128)(2,1)} %collective-permute-done.13, bf16[256,512]{1,0:T(8,128)(2,1)} %collective-permute-done.14, ...), kind=kOutput, calls=%fused_computation.2 | convolution fusion | flops 136052736 | bytes 2097155 | tf_op jit(solution)/shard_map/dot_general | solution.py:33
  123.4 2.0 %convolution_convert_fusion = bf16[256,512]{1,0:T(8,128)(2,1)} fusion(bf16[512,512]{1,0:T(8,128)(2,1)S(1)} %copy-done.7, f32[2,512,256]{2,1,0:T(8,128)S(1)} %convert_add_fusion.1, bf16[512,256]{1,0:T(8,128)(2,1)} %collective-permute-done.17), kind=kOutput, calls=%fused_computation.1 | convolution fusion | flops 134742016 | bytes 1572864 | tf_op jit(solution)/shard_map/dot_general | solution.py:214
  125.4 1.5 %select_convert_fusion = (f32[512,512]{1,0:T(8,128)}, f32[512,512]{1,0:T(8,128)}) fusion(bf16[512,512]{1,0:T(8,128)(2,1)S(1)} %collective-permute-done.19, pred[]{:T(512)S(6)} %eq.13, bf16[8,64,512]{2,1,0:T(8,128)(2,1)S(1)} %all-to-all-done.3), kind=kLoop, calls=%fused_computation.28 | loop fusion | flops 1048576 | bytes 3145729 | tf_op jit(solution)/shard_map/convert_element_type | solution.py:179
  (58 shorter events, 18.9 us)
Async XLA Ops:
  0.6 40.5 %copy-start = (bf16[512,512]{1,0:T(8,128)(2,1)S(1)}, bf16[512,512]{1,0:T(8,128)(2,1)}, u32[]{:S(2)}) copy-start(bf16[512,512]{1,0:T(8,128)(2,1)} %refs_13_.1) | copy-start | bytes 1572868
  2.3 11.8 %collective-permute-start = (bf16[272,512]{1,0:T(8,128)(2,1)S(1)}, bf16[272,512]{1,0:T(8,128)(2,1)S(1)}, u32[]{:S(2)}, u32[]{:S(2)}) collective-permute-start(bf16[272,512]{1,0:T(8,128)(2,1)S(1)} %fusion.15.refs_5_), channel_id=1, source_target_pairs={{0,224},{32,0},{64,32},{96,64},{128,96},{160,128},{192,160},{224,1... | collective-permute-start | bytes 835592 | tf_op jit(solution)/shard_map/ppermute | solution.py:21
  8.8 7.2 %collective-permute-start.2 = (bf16[272,512]{1,0:T(8,128)(2,1)S(1)}, bf16[272,512]{1,0:T(8,128)(2,1)S(1)}, u32[]{:S(2)}, u32[]{:S(2)}) collective-permute-start(bf16[272,512]{1,0:T(8,128)(2,1)S(1)} %fusion.15.refs_5_), channel_id=1, source_target_pairs={{0,4},{4,0},{1,5},{5,1},{2,6},{6,2},{3,7},{7,3},{8,12},{12,8},{9,1... | collective-permute-start | bytes 835592 | tf_op jit(solution)/shard_map/ppermute | solution.py:21
  11.7 8.2 %collective-permute-start.1 = (bf16[272,512]{1,0:T(8,128)(2,1)S(1)}, bf16[272,512]{1,0:T(8,128)(2,1)S(1)}, u32[]{:S(2)}, u32[]{:S(2)}) collective-permute-start(bf16[272,512]{1,0:T(8,128)(2,1)S(1)} %fusion.14.refs_0_), channel_id=1, source_target_pairs={{0,32},{32,64},{64,96},{96,128},{128,160},{160,192},{192,224},{224... | collective-permute-start | bytes 835592 | tf_op jit(solution)/shard_map/ppermute | solution.py:21
  11.8 16.6 %collective-permute-start.6 = (bf16[272,512]{1,0:T(8,128)(2,1)S(1)}, bf16[272,512]{1,0:T(8,128)(2,1)S(1)}, u32[]{:S(2)}, u32[]{:S(2)}) collective-permute-start(bf16[272,512]{1,0:T(8,128)(2,1)S(1)} %fusion.15.refs_5_), channel_id=1, source_target_pairs={{0,2},{2,0},{1,3},{3,1},{4,6},{6,4},{5,7},{7,5},{8,10},{10,8},{9,1... | collective-permute-start | bytes 835592 | tf_op jit(solution)/shard_map/ppermute | solution.py:21
  21.8 7.7 %collective-permute-start.3 = (bf16[272,512]{1,0:T(8,128)(2,1)S(1)}, bf16[272,512]{1,0:T(8,128)(2,1)S(1)}, u32[]{:S(2)}, u32[]{:S(2)}) collective-permute-start(bf16[272,512]{1,0:T(8,128)(2,1)S(1)} %get-tuple-element.23), channel_id=1, source_target_pairs={{0,8},{8,16},{16,24},{24,0},{1,9},{9,17},{17,25},{25,1},{2,10},{10... | collective-permute-start | bytes 835592 | tf_op jit(solution)/shard_map/ppermute | solution.py:21
  23.0 10.4 %collective-permute-start.8 = (bf16[272,512]{1,0:T(8,128)(2,1)S(1)}, bf16[272,512]{1,0:T(8,128)(2,1)S(1)}, u32[]{:S(2)}, u32[]{:S(2)}) collective-permute-start(bf16[272,512]{1,0:T(8,128)(2,1)S(1)} %collective-permute-done.refs_9_), channel_id=1, source_target_pairs={{0,4},{4,0},{1,5},{5,1},{2,6},{6,2},{3,7},{7,3},{8,12},{12,8},{9,1... | collective-permute-start | bytes 835592 | tf_op jit(solution)/shard_map/ppermute | solution.py:21
  23.2 17.9 %collective-permute-start.9 = (bf16[272,512]{1,0:T(8,128)(2,1)S(1)}, bf16[272,512]{1,0:T(8,128)(2,1)}, u32[]{:S(2)}, u32[]{:S(2)}) collective-permute-start(bf16[272,512]{1,0:T(8,128)(2,1)S(1)} %collective-permute-done.refs_9_), channel_id=1, source_target_pairs={{0,2},{2,0},{1,3},{3,1},{4,6},{6,4},{5,7},{7,5},{8,10},{10,8},{9,1... | collective-permute-start | bytes 835592 | tf_op jit(solution)/shard_map/ppermute | solution.py:21
  25.9 10.5 %collective-permute-start.4 = (bf16[272,512]{1,0:T(8,128)(2,1)}, bf16[272,512]{1,0:T(8,128)(2,1)}, u32[]{:S(2)}, u32[]{:S(2)}) collective-permute-start(bf16[272,512]{1,0:T(8,128)(2,1)} %get-tuple-element.22), channel_id=1, source_target_pairs={{0,16},{8,24},{16,0},{24,8},{1,17},{9,25},{17,1},{25,9},{2,18},{10... | collective-permute-start | bytes 835592 | tf_op jit(solution)/shard_map/ppermute | solution.py:21
  28.4 12.8 %copy-start.1 = (bf16[272,512]{1,0:T(8,128)(2,1)}, bf16[272,512]{1,0:T(8,128)(2,1)S(1)}, u32[]{:S(2)}) copy-start(bf16[272,512]{1,0:T(8,128)(2,1)S(1)} %collective-permute-done.6.refs_7_) | copy-start | bytes 835588
  28.4 12.7 %collective-permute-start.5 = (bf16[272,512]{1,0:T(8,128)(2,1)}, bf16[272,512]{1,0:T(8,128)(2,1)}, u32[]{:S(2)}, u32[]{:S(2)}) collective-permute-start(bf16[272,512]{1,0:T(8,128)(2,1)} %get-tuple-element.21), channel_id=1, source_target_pairs={{0,24},{8,0},{16,8},{24,16},{1,25},{9,1},{17,9},{25,17},{2,26},{10... | collective-permute-start | bytes 835592 | tf_op jit(solution)/shard_map/ppermute | solution.py:21
  29.5 11.6 %copy-start.3 = (bf16[272,512]{1,0:T(8,128)(2,1)}, bf16[272,512]{1,0:T(8,128)(2,1)S(1)}, u32[]{:S(2)}) copy-start(bf16[272,512]{1,0:T(8,128)(2,1)S(1)} %collective-permute-done.3.refs_2_) | copy-start | bytes 835588
  29.5 11.6 %collective-permute-start.7 = (bf16[272,512]{1,0:T(8,128)(2,1)S(1)}, bf16[272,512]{1,0:T(8,128)(2,1)}, u32[]{:S(2)}, u32[]{:S(2)}) collective-permute-start(bf16[272,512]{1,0:T(8,128)(2,1)S(1)} %collective-permute-done.2.refs_6_), channel_id=1, source_target_pairs={{0,2},{2,0},{1,3},{3,1},{4,6},{6,4},{5,7},{7,5},{8,10},{10,8},{9,1... | collective-permute-start | bytes 835592 | tf_op jit(solution)/shard_map/ppermute | solution.py:21
  33.5 7.7 %copy-start.5 = (bf16[272,512]{1,0:T(8,128)(2,1)}, bf16[272,512]{1,0:T(8,128)(2,1)S(1)}, u32[]{:S(2)}) copy-start(bf16[272,512]{1,0:T(8,128)(2,1)S(1)} %collective-permute-done.8.refs_10_) | copy-start | bytes 835588
  33.5 7.7 %collective-permute-start.10 = (bf16[272,512]{1,0:T(8,128)(2,1)S(1)}, bf16[272,512]{1,0:T(8,128)(2,1)}, u32[]{:S(2)}, u32[]{:S(2)}) collective-permute-start(bf16[272,512]{1,0:T(8,128)(2,1)S(1)} %collective-permute-done.8.refs_10_), channel_id=1, source_target_pairs={{0,2},{2,0},{1,3},{3,1},{4,6},{6,4},{5,7},{7,5},{8,10},{10,8},{9,1... | collective-permute-start | bytes 835592 | tf_op jit(solution)/shard_map/ppermute | solution.py:21
  41.2 1.0 copy-start.2
  42.1 1.0 copy-start.4
  62.3 10.1 %collective-permute-start.15 = (bf16[4,512,256]{2,1,0:T(8,128)(2,1)S(1)}, bf16[4,512,256]{2,1,0:T(8,128)(2,1)}, u32[]{:S(2)}, u32[]{:S(2)}) collective-permute-start(bf16[4,512,256]{2,1,0:T(8,128)(2,1)S(1)} %slice.40), channel_id=1, source_target_pairs={{0,2},{2,0},{1,3},{3,1},{4,6},{6,4},{5,7},{7,5},{8,10},{10,8},{9,1... | collective-permute-start | bytes 3145736 | tf_op jit(solution)/shard_map/ppermute | solution.py:21
  64.1 2.4 %collective-permute-start.18 = (bf16[512,512]{1,0:T(8,128)(2,1)}, bf16[512,512]{1,0:T(8,128)(2,1)S(1)}, u32[]{:S(2)}, u32[]{:S(2)}) collective-permute-start(bf16[512,512]{1,0:T(8,128)(2,1)} %dynamic-slice_bitcast_fusion), channel_id=1, source_target_pairs={{0,2},{2,0},{1,3},{3,1},{4,6},{6,4},{5,7},{7,5},{8,10},{10,8},{9,1... | collective-permute-start | bytes 1572872 | tf_op jit(solution)/shard_map/ppermute | solution.py:21
  67.4 14.2 %all-to-all-start = ((bf16[8,64,512]{2,1,0:T(8,128)(2,1)}), bf16[8,64,512]{2,1,0:T(8,128)(2,1)S(1)}, u32[]{:S(2)}, u32[]{:S(2)}) async-start(bf16[8,64,512]{2,1,0:T(8,128)(2,1)} %bitcast.12), calls=%async_computation | async-start | bytes 1048576 | tf_op jit(solution)/shard_map/all_to_all | solution.py:25
  72.4 4.2 %copy-start.8 = (bf16[5,256,512]{2,1,0:T(8,128)(2,1)S(1)}, bf16[5,256,512]{2,1,0:T(8,128)(2,1)}, u32[]{:S(2)}) copy-start(bf16[5,256,512]{2,1,0:T(8,128)(2,1)} %get-tuple-element.13) | copy-start | bytes 3932164
  75.2 33.2 %collective-permute-start.16 = (bf16[2,512,256]{2,1,0:T(8,128)(2,1)}, bf16[2,512,256]{2,1,0:T(8,128)(2,1)}, u32[]{:S(2)}, u32[]{:S(2)}) collective-permute-start(bf16[2,512,256]{2,1,0:T(8,128)(2,1)} %slice.46), channel_id=1, source_target_pairs={{0,4},{4,0},{1,5},{5,1},{2,6},{6,2},{3,7},{7,3},{8,12},{12,8},{9,1... | collective-permute-start | bytes 1572872 | tf_op jit(solution)/shard_map/ppermute | solution.py:21
  77.5 19.6 %collective-permute-start.11 = (bf16[256,512]{1,0:T(8,128)(2,1)}, bf16[256,512]{1,0:T(8,128)(2,1)}, u32[]{:S(2)}, u32[]{:S(2)}) collective-permute-start(bf16[256,512]{1,0:T(8,128)(2,1)} %get-tuple-element.18), channel_id=1, source_target_pairs={{0,24},{8,0},{16,8},{24,16},{1,25},{9,1},{17,9},{25,17},{2,26},{10... | collective-permute-start | bytes 786440 | tf_op jit(solution)/shard_map/ppermute | solution.py:21
  79.9 17.2 %collective-permute-start.12 = (bf16[256,512]{1,0:T(8,128)(2,1)}, bf16[256,512]{1,0:T(8,128)(2,1)}, u32[]{:S(2)}, u32[]{:S(2)}) collective-permute-start(bf16[256,512]{1,0:T(8,128)(2,1)} %get-tuple-element.17), channel_id=1, source_target_pairs={{0,16},{8,24},{16,0},{24,8},{1,17},{9,25},{17,1},{25,9},{2,18},{10... | collective-permute-start | bytes 786440 | tf_op jit(solution)/shard_map/ppermute | solution.py:21
  80.5 16.6 %collective-permute-start.13 = (bf16[256,512]{1,0:T(8,128)(2,1)}, bf16[256,512]{1,0:T(8,128)(2,1)}, u32[]{:S(2)}, u32[]{:S(2)}) collective-permute-start(bf16[256,512]{1,0:T(8,128)(2,1)} %get-tuple-element.16), channel_id=1, source_target_pairs={{0,8},{8,16},{16,24},{24,0},{1,9},{9,17},{17,25},{25,1},{2,10},{10... | collective-permute-start | bytes 786440 | tf_op jit(solution)/shard_map/ppermute | solution.py:21
  82.3 10.5 %all-to-all-start.1 = ((bf16[8,8,512]{2,1,0:T(8,128)(2,1)}), bf16[8,8,512]{2,1,0:T(8,128)(2,1)S(1)}, u32[]{:S(2)}, u32[]{:S(2)}) async-start(bf16[8,8,512]{2,1,0:T(8,128)(2,1)} %bitcast.13), calls=%async_computation.1 | async-start | bytes 131072 | tf_op jit(solution)/shard_map/all_to_all | solution.py:25
  93.5 10.5 %all-to-all-start.2 = ((bf16[8,8,512]{2,1,0:T(8,128)(2,1)}), bf16[8,8,512]{2,1,0:T(8,128)(2,1)S(1)}, u32[]{:S(2)}, u32[]{:S(2)}) async-start(bf16[8,8,512]{2,1,0:T(8,128)(2,1)} %broadcast_in_dim.33), calls=%async_computation.2 | async-start | bytes 131072 | tf_op jit(solution)/shard_map/all_to_all | solution.py:25
  99.1 21.9 %collective-permute-start.14 = (bf16[256,512]{1,0:T(8,128)(2,1)}, bf16[256,512]{1,0:T(8,128)(2,1)}, u32[]{:S(2)}, u32[]{:S(2)}) collective-permute-start(bf16[256,512]{1,0:T(8,128)(2,1)} %fusion.11), channel_id=1, source_target_pairs={{0,224},{32,0},{64,32},{96,64},{128,96},{160,128},{192,160},{224,1... | collective-permute-start | bytes 786440 | tf_op jit(solution)/shard_map/ppermute | solution.py:21
  104.9 10.4 %all-to-all-start.3 = ((bf16[8,64,512]{2,1,0:T(8,128)(2,1)}), bf16[8,64,512]{2,1,0:T(8,128)(2,1)S(1)}, u32[]{:S(2)}, u32[]{:S(2)}) async-start(bf16[8,64,512]{2,1,0:T(8,128)(2,1)} %broadcast_in_dim.35), calls=%async_computation.3 | async-start | bytes 1048576 | tf_op jit(solution)/shard_map/all_to_all | solution.py:25
  109.5 13.9 %copy-start.7 = (bf16[512,512]{1,0:T(8,128)(2,1)S(1)}, bf16[512,512]{1,0:T(8,128)(2,1)}, u32[]{:S(2)}) copy-start(bf16[512,512]{1,0:T(8,128)(2,1)} %param.9) | copy-start | bytes 1572868
  109.6 13.8 %collective-permute-start.17 = (bf16[512,256]{1,0:T(8,128)(2,1)S(1)}, bf16[512,256]{1,0:T(8,128)(2,1)}, u32[]{:S(2)}, u32[]{:S(2)}) collective-permute-start(bf16[512,256]{1,0:T(8,128)(2,1)S(1)} %fusion.17), channel_id=1, source_target_pairs={{0,32},{32,64},{64,96},{96,128},{128,160},{160,192},{192,224},{224... | collective-permute-start | bytes 786440 | tf_op jit(solution)/shard_map/ppermute | solution.py:21
  115.3 10.1 %collective-permute-start.19 = (bf16[512,512]{1,0:T(8,128)(2,1)S(1)}, bf16[512,512]{1,0:T(8,128)(2,1)S(1)}, u32[]{:S(2)}, u32[]{:S(2)}) collective-permute-start(bf16[512,512]{1,0:T(8,128)(2,1)S(1)} %bitcast.41), channel_id=1, source_target_pairs={{0,2},{2,0},{1,3},{3,1},{4,6},{6,4},{5,7},{7,5},{8,10},{10,8},{9,1... | collective-permute-start | bytes 1572872 | tf_op jit(solution)/shard_map/ppermute | solution.py:21
  (1 other events, 1.0 us)

commit v2 on v1

--- a/solution.py
+++ b/solution.py
@@ -37,13 +37,14 @@
     return lax.dot_general(a, b, (((0,), (0,)), ((), ())), preferred_element_type=F32)
 
 
-def tiles_kernel(inv_rows, sel_ref, *refs):
-    audio = refs[:5]
-    text = refs[5:13]
-    ha_ref, ht_ref = refs[13:15]
-    da_ref, dt_ref, head_ref = refs[15:18]
+def tiles_kernel(inv_rows, where_ref, *refs):
+    audio_x, audio_prev = refs[:2]
+    text = refs[2:10]
+    ha_ref, ht_ref = refs[10:12]
+    dx_ref, dp_ref, mine_ref, send_ref, keep_head, send_head = refs[12:18]
     za, zat, zt, ua, ut, na, nt, ea, eb, ga, gt = refs[18:]
     rows, width = za.shape[1], za.shape[2]
+    audio = [audio_x.at[i] for i in range(4)] + [audio_prev]
 
     for i in range(5):
         p = dot_nn(audio[i][:rows, :], ha_ref[...])
@@ -74,14 +75,14 @@
     row_id = lax.broadcasted_iota(jnp.int32, (rows, 2 * rows), 0)
     col_id = lax.broadcasted_iota(jnp.int32, (rows, 2 * rows), 1)
     eye = (row_id == col_id).astype(F32)
+    place = where_ref[4]
 
     def chunk(j, carry):
         columns = zt[j]
         col_scale = eb[j, 0:1, :]
-        own = sel_ref[j]
         acc = None
         for r in range(4):
-            i = own if r == 0 else r + 1
+            i = where_ref[j] if r == 0 else lax.rem(place + r, 4)
             s = dot_nn(za[i], columns)
             e = jnp.exp2(s * (logit_scale * log2_e))
             row_scale = ea[i]
@@ -98,43 +99,61 @@
 
     lax.fori_loop(0, 4, chunk, 0)
 
-    head = None
+    head_a = None
     for i in range(5):
         g = ga[i]
         u = ua[i]
         along = jnp.sum(u * g, axis=1, keepdims=True)
         d = ((g - u * along) * (na[i][:, 0:1] * logit_scale)).astype(BF)
-        da_ref[i] = d
+        if i < 4:
+            dx_ref[i] = d
+        else:
+            dp_ref[...] = d
         part = dot_tn(audio[i][:rows, :], d)
-        head = part if head is None else head + part
-    head_ref[0] = (head * inv_rows).astype(BF)
-    head = None
+        head_a = part if head_a is None else head_a + part
+    head_a = (head_a * inv_rows).astype(BF)
+    head_t = None
     for j in range(4):
         g = gt[j]
         u = ut[j]
         along = jnp.sum(u * g, axis=0, keepdims=True)
         d = ((g - u * along) * (nt[j, 0:1, :] * logit_scale)).astype(BF)
+        out = mine_ref if j < 2 else send_ref
         for plane in range(2):
             part_d = d[:, plane * rows : (plane + 1) * rows]
-            dt_ref[2 * j + plane] = part_d
+            out[2 * (j % 2) + plane] = part_d
             part = dot_nn(part_d, text[4 * plane + j][:rows, :])
-            head = part if head is None else head + part
-    head_ref[1] = (head * inv_rows).T.astype(BF)
-
-
-def tiles(sel, audio, text, audio_head, text_head_t, batch_rows):
-    rows, width = audio[0].shape[0] - PAD, audio[0].shape[1]
+            head_t = part if head_t is None else head_t + part
+    head_t = (head_t * inv_rows).T.astype(BF)
+    core = where_ref[5]
+
+    @pl.when(core == 0)
+    def _():
+        keep_head[...] = head_a
+        send_head[...] = head_t
+
+    @pl.when(core == 1)
+    def _():
+        keep_head[...] = head_t
+        send_head[...] = head_a
+
+
+def tiles(where, audio_x, audio_prev, text, audio_head, text_head_t, batch_rows):
+    rows, width = audio_prev.shape[0] - PAD, audio_prev.shape[1]
     lanes = min(128, rows)
     vmem = pl.BlockSpec(memory_space=pltpu.VMEM)
     return pl.pallas_call(
         functools.partial(tiles_kernel, 1.0 / batch_rows),
         out_shape=(
-            jax.ShapeDtypeStruct((5, rows, width), BF),
-            jax.ShapeDtypeStruct((8, width, rows), BF),
-            jax.ShapeDtypeStruct((2, width, width), BF),
+            jax.ShapeDtypeStruct((4, rows, width), BF),
+            jax.ShapeDtypeStruct((rows, width), BF),
+            jax.ShapeDtypeStruct((4, width, rows), BF),
+            jax.ShapeDtypeStruct((4, width, rows), BF),
+            jax.ShapeDtypeStruct((width, width), BF),
+            jax.ShapeDtypeStruct((width, width), BF),
         ),
-        in_specs=[pl.BlockSpec(memory_space=pltpu.SMEM)] + [vmem] * 15,
-        out_specs=(vmem, vmem, vmem),
+        in_specs=[pl.BlockSpec(memory_space=pltpu.SMEM)] + [vmem] * 12,
+        out_specs=(vmem,) * 6,
         scratch_shapes=[
             pltpu.VMEM((5, rows, width), BF),
             pltpu.VMEM((5, width, rows), BF),
@@ -148,11 +167,11 @@
             pltpu.VMEM((5, rows, width), F32),
             pltpu.VMEM((4, width, 2 * rows), F32),
         ],
-        compiler_params=pltpu.CompilerParams(vmem_limit_bytes=48 * 1024 * 1024),
+        compiler_params=pltpu.CompilerParams(vmem_limit_bytes=36 * 1024 * 1024),
         cost_estimate=pl.CostEstimate(
             flops=12_000_000_000, bytes_accessed=9_000_000, transcendentals=2_100_000
         ),
-    )(sel, *audio, *text, audio_head, text_head_t)
+    )(where, audio_x, audio_prev, *text, audio_head, text_head_t)
 
 
 def packed(embed, lse):
@@ -164,20 +183,25 @@
     return jnp.sum(parts.astype(F32), axis=0)
 
 
-def head_total(head):
-    core = lax.axis_index("c")
-    width = head.shape[1]
-    keep = lax.dynamic_index_in_dim(head, core, 0, keepdims=False)
-    send = lax.dynamic_index_in_dim(head, 1 - core, 0, keepdims=False)
+def repeated(part, count):
+    wide = jnp.broadcast_to(part[None], (count,) + part.shape)
+    return wide.reshape(count * part.shape[0], part.shape[1])
+
+
+def head_total(keep, send, other_work):
+    width = keep.shape[0]
     mine = (keep.astype(F32) + shift(send, "c", 1).astype(F32)).astype(BF)
     part = summed(exchange(mine, XY).reshape(8, width // 8, width)).astype(BF)
-    part = summed(exchange(part, "z").reshape(8, width // 64, width)).astype(BF)
-    part = exchange(jnp.broadcast_to(part[None], (8,) + part.shape).reshape(width // 8, width), "z")
-    part = exchange(jnp.broadcast_to(part[None], (8,) + part.shape).reshape(width, width), XY)
+    near = [shift(part, "z", s).astype(F32) for s in (1, -1, -2)]
+    part = (part.astype(F32) + near[0] + near[1] + near[2]).astype(BF)
+    part = (part.astype(F32) + shift(part, "z", 4).astype(F32)).astype(BF)
+    part = exchange(repeated(part, 8), XY)
+    part, *other_work = lax.optimization_barrier((part, *other_work))
     other = shift(part, "c", 1)
+    core = lax.axis_index("c")
     first = jnp.where(core == 0, part, other).astype(F32)
     second = jnp.where(core == 0, other, part).astype(F32)
-    return first, second
+    return first, second, *other_work
 
 
 def local(audio_embed, text_embed, audio_head, text_head, audio_lse, text_lse):
@@ -189,25 +213,24 @@
 
     a_own = packed(audio_embed, audio_lse)
     t_own = packed(text_embed, text_lse)
+    a_prev = shift(a_own, "z", 1)
     t_next = shift(t_own, "z", -1)
-    a_prev = shift(a_own, "z", 1)
     t_y = shift(t_own, "yl", 1)
     t_next, a_prev, t_y = lax.optimization_barrier((t_next, a_prev, t_y))
+    for_x = jnp.concatenate([jnp.where(x <= d, a_own, a_prev) for d in range(4)], axis=0)
+    audio_x = exchange(for_x, "x").reshape((4,) + a_own.shape)
     t_next_y = shift(t_next, "yl", 1)
-    a_x = [shift(jnp.where(x + s < 4, a_own, a_prev), "x", s) for s in (1, 2, 3)]
     here = [t_own, t_y]
     here += [shift(v, "c", 1) for v in here]
     ahead = [t_next, t_next_y]
     ahead += [shift(v, "c", 1) for v in ahead]
 
-    behind = [jnp.int32(0), (yl == 1).astype(jnp.int32), (core == 1).astype(jnp.int32), (yl == 1).astype(jnp.int32)]
-    da, dt, head = tiles(
-        jnp.stack(behind), [a_own, a_prev] + a_x, here + ahead, audio_head, text_head.T, rows * blocks
+    high_y, high_c = yl == 1, core == 1
+    where = [x, jnp.where(high_y, 4, x), jnp.where(high_c, 4, x), jnp.where(high_y, 4, x), x, core]
+    dx, dp, dt_mine, dt_send, keep, send = tiles(
+        jnp.stack(where), audio_x, a_prev, here + ahead, audio_head, text_head.T, rows * blocks
     )
 
-    audio_total, text_total = head_total(head)
-
-    dt_mine, dt_send = dt[:4], dt[4:]
     dt_sum = (dt_mine.astype(F32) + shift(dt_send, "c", 1).astype(F32)).astype(BF)
     dt_pair = dt_sum[:2].astype(F32) + shift(dt_sum[2:], "yl", 1).astype(F32)
     dt_full = dt_pair[0] + shift(dt_pair[1].astype(BF), "z", 1).astype(F32)
@@ -215,14 +238,14 @@
         dt_full.astype(BF), text_head, (((0,), (1,)), ((), ())), preferred_element_type=F32
     ).astype(BF)
 
-    back = [shift(da[1 + s], "x", -s).astype(F32) for s in (1, 2, 3)]
-    here_sum, behind_sum = da[0].astype(F32), da[1].astype(F32)
-    for s in (1, 2, 3):
-        wrapped = x + s >= 4
-        here_sum = here_sum + jnp.where(wrapped, 0.0, back[s - 1])
-        behind_sum = behind_sum + jnp.where(wrapped, back[s - 1], 0.0)
+    back = exchange(dx.reshape(4 * rows, -1), "x").reshape(dx.shape).astype(F32)
+    ahead_x = (jnp.arange(4) >= x)[:, None, None]
+    here_sum = jnp.sum(jnp.where(ahead_x, back, 0.0), axis=0)
+    behind_sum = dp.astype(F32) + jnp.sum(jnp.where(ahead_x, 0.0, back), axis=0)
     da_full = here_sum + shift(behind_sum.astype(BF), "z", -1).astype(F32)
     audio_input = dot_nt(da_full.astype(BF), audio_head).astype(BF)
+
+    audio_total, text_total, audio_input, text_input = head_total(keep, send, (audio_input, text_input))
     return audio_input, text_input, audio_total, text_total
 
 

time: 128 us -> 136 us (1.062)
  waiting for transfers between devices: 30.8 us -> 38.4 us
  other arithmetic: 12.1 us -> 14.8 us
  matrix products: 4.37 us -> 2.1 us
    all_to_all x4, waiting for transfers between devices: 15.6 us -> 21.5 us  [exchange(): return lax.all_to_all(value, axis, split_axis=0, concat_axis=0, tiled=True)]
    unnamed x19 -> x35, local copies, waits for them, and re-layouts: 4.14 us -> 8.63 us
    reduce_sum x0 -> x1, other arithmetic: none -> 2.59 us  [local(): behind_sum = dp.astype(F32) + jnp.sum(jnp.where(ahead_x, 0.0, back), axis=0)]
    squeeze x2 -> x0, local copies, waits for them, and re-layouts: 1.72 us -> none  [the longest x1 0.9 us: local(): back = [shift(da[1 + s], 'x', -s).astype(F32) for s in (1, 2, 3)]]
    select_n x1, other arithmetic: 1.89 us -> 0.2 us  [local(): jnp.where(x <= d, a_own, a_prev)]
    ppermute x20 -> x18, waiting for transfers between devices: 15.3 us -> 16.9 us  [shift(): lax.ppermute(value, axis, [(i, (i + steps) % count) for i in range(count)])]
    ppermute x20 -> x18, starting transfers between devices: 35.5 us -> 34.3 us  [shift(): lax.ppermute(value, axis, [(i, (i + steps) % count) for i in range(count)])]
  transfers between devices with their start and end apart: 24 -> 22, of which waited for: 10 -> 11; matrix products, arithmetic and copies ran while one was open for 16% -> 12% of each run, Pallas kernels for 0% -> 0%
where the time goes in v2:
time: 136 us; the launch traced here: 135 us
  starting transfers between devices  51 us (38%)
  waiting for transfers between devices  38.4 us (28%)
  Pallas kernels  17.3 us (13%)
  other arithmetic  14.8 us (11%)
  local copies, waits for them, and re-layouts  11 us (8%)
  matrix products  2.1 us (2%)
    ppermute x18, starting transfers between devices, shift(): lax.ppermute(value, axis, [(i, (i + steps) % count) for i in range(count)])  34.3 us
    all_to_all x4, waiting for transfers between devices, exchange(): return lax.all_to_all(value, axis, split_axis=0, concat_axis=0, tiled=True)  21.5 us
    pallas_call x1, Pallas kernels, tiles(): pl.pallas_call(functools.partial(tiles_kernel, 1.0 / batch_rows), out_sha...  17.3 us
    ppermute x18, waiting for transfers between devices, shift(): lax.ppermute(value, axis, [(i, (i + steps) % count) for i in range(count)])  16.9 us
    all_to_all x4, starting transfers between devices, exchange(): return lax.all_to_all(value, axis, split_axis=0, concat_axis=0, tiled=True)  16.7 us
    unnamed x35, local copies, waits for them, and re-layouts  8.63 us
  transfers between devices with their start and end apart: 22, of which 11 were waited for; matrix products, arithmetic and copies ran while one was open for 12% of the time, Pallas kernels for 0%

profile of v2, /device:TPU:1, one launch (start us, length us, event | category | flops | bytes accessed | tf_op | source)
XLA Modules:
  0.0 135.4 jit_solution(13733889472742237454)
XLA Ops:
  2.3 2.5 %collective-permute-start.1 = (bf16[272,512]{1,0:T(8,128)(2,1)S(1)}, bf16[272,512]{1,0:T(8,128)(2,1)S(1)}, u32[]{:S(2)}, u32[]{:S(2)}) collective-permute-start(bf16[272,512]{1,0:T(8,128)(2,1)S(1)} %fusion.6), channel_id=1, source_target_pairs={{0,32},{32,64},{64,96},{96,128},{128,160},{160,192},{192,224},{224... | collective-permute-start | bytes 835592 | tf_op jit(solution)/shard_map/ppermute | solution.py:21
  6.5 1.4 %collective-permute-start.2 = (bf16[272,512]{1,0:T(8,128)(2,1)S(1)}, bf16[272,512]{1,0:T(8,128)(2,1)S(1)}, u32[]{:S(2)}, u32[]{:S(2)}) collective-permute-start(bf16[272,512]{1,0:T(8,128)(2,1)S(1)} %fusion.7.refs_2_), channel_id=1, source_target_pairs={{0,4},{4,0},{1,5},{5,1},{2,6},{6,2},{3,7},{7,3},{8,12},{12,8},{9,1... | collective-permute-start | bytes 835592 | tf_op jit(solution)/shard_map/ppermute | solution.py:21
  7.9 4.0 %collective-permute-start = (bf16[272,512]{1,0:T(8,128)(2,1)S(1)}, bf16[272,512]{1,0:T(8,128)(2,1)S(1)}, u32[]{:S(2)}, u32[]{:S(2)}) collective-permute-start(bf16[272,512]{1,0:T(8,128)(2,1)S(1)} %fusion.7.refs_2_), channel_id=1, source_target_pairs={{0,224},{32,0},{64,32},{96,64},{128,96},{160,128},{192,160},{224,1... | collective-permute-start | bytes 835592 | tf_op jit(solution)/shard_map/ppermute | solution.py:21
  11.8 3.3 %collective-permute-done.1.refs_1_ = bf16[272,512]{1,0:T(8,128)(2,1)S(1)} collective-permute-done((bf16[272,512]{1,0:T(8,128)(2,1)S(1)}, bf16[272,512]{1,0:T(8,128)(2,1)S(1)}, u32[]{:S(2)}, u32[]{:S(2)}) %collective-permute-start.1) | collective-permute-done | bytes 278560 | tf_op jit(solution)/shard_map/ppermute | solution.py:21
  15.2 1.7 %collective-permute-done.refs_6_ = bf16[272,512]{1,0:T(8,128)(2,1)S(1)} collective-permute-done((bf16[272,512]{1,0:T(8,128)(2,1)S(1)}, bf16[272,512]{1,0:T(8,128)(2,1)S(1)}, u32[]{:S(2)}, u32[]{:S(2)}) %collective-permute-start) | collective-permute-done | bytes 278560 | tf_op jit(solution)/shard_map/ppermute | solution.py:21
  17.1 1.1 pad_maximum_fusion
  18.1 4.1 %all-to-all-start = ((bf16[4,272,512]{2,1,0:T(8,128)(2,1)}), bf16[4,272,512]{2,1,0:T(8,128)(2,1)S(1)}, u32[]{:S(2)}, u32[]{:S(2)}) async-start(bf16[4,272,512]{2,1,0:T(8,128)(2,1)} %bitcast.20), calls=%async_computation | async-start | bytes 2228224 | tf_op jit(solution)/shard_map/all_to_all | solution.py:25
  22.5 2.4 %collective-permute-start.3 = (bf16[272,512]{1,0:T(8,128)(2,1)S(1)}, bf16[272,512]{1,0:T(8,128)(2,1)}, u32[]{:S(2)}, u32[]{:S(2)}) collective-permute-start(bf16[272,512]{1,0:T(8,128)(2,1)S(1)} %fusion.7.refs_2_), channel_id=1, source_target_pairs={{0,2},{2,0},{1,3},{3,1},{4,6},{6,4},{5,7},{7,5},{8,10},{10,8},{9,1... | collective-permute-start | bytes 835592 | tf_op jit(solution)/shard_map/ppermute | solution.py:21
  25.4 2.9 %collective-permute-done.5.refs_7_ = bf16[272,512]{1,0:T(8,128)(2,1)S(1)} collective-permute-done((bf16[272,512]{1,0:T(8,128)(2,1)S(1)}, bf16[272,512]{1,0:T(8,128)(2,1)S(1)}, u32[]{:S(2)}, u32[]{:S(2)}) %collective-permute-start.5) | collective-permute-done | bytes 278560 | tf_op jit(solution)/shard_map/ppermute | solution.py:21
  28.3 3.1 %collective-permute-start.7 = (bf16[272,512]{1,0:T(8,128)(2,1)S(1)}, bf16[272,512]{1,0:T(8,128)(2,1)}, u32[]{:S(2)}, u32[]{:S(2)}) collective-permute-start(bf16[272,512]{1,0:T(8,128)(2,1)S(1)} %collective-permute-done.5.refs_7_), channel_id=1, source_target_pairs={{0,2},{2,0},{1,3},{3,1},{4,6},{6,4},{5,7},{7,5},{8,10},{10,8},{9,1... | collective-permute-start | bytes 835592 | tf_op jit(solution)/shard_map/ppermute | solution.py:21
  31.4 2.0 %copy.10 = bf16[512,512]{0,1:T(8,128)(2,1)} copy(bf16[512,512]{1,0:T(8,128)(2,1)} %param.9) | data formatting | bytes 1048576 | tf_op args[3]
  33.5 2.5 %all-to-all-done.refs_0_ = bf16[4,272,512]{2,1,0:T(8,128)(2,1)S(1)} async-done(((bf16[4,272,512]{2,1,0:T(8,128)(2,1)}), bf16[4,272,512]{2,1,0:T(8,128)(2,1)S(1)}, u32[]{:S(2)}, u32[]{:S(2)}) %all-to-all-start) | async-done | bytes 1114144 | tf_op jit(solution)/shard_map/all_to_all | solution.py:25
  40.9 17.3 %shard_map.93 = (bf16[4,256,512]{2,1,0:T(8,128)(2,1)}, bf16[256,512]{1,0:T(8,128)(2,1)S(1)}, bf16[4,512,256]{2,1,0:T(8,128)(2,1)S(1)}, bf16[4,512,256]{2,1,0:T(8...) custom-call(s32[6]{0:T(128)S(1)} %stack.21.where_ref, ...), custom_call_target="tpu_custom_call" | custom-call | flops 12000000000 | bytes 9000000 | tf_op jit(solution)/shard_map/pallas_call | solution.py:145
  59.8 2.9 %collective-permute-start.8 = (bf16[512,512]{1,0:T(8,128)(2,1)}, bf16[512,512]{1,0:T(8,128)(2,1)}, u32[]{:S(2)}, u32[]{:S(2)}) collective-permute-start(bf16[512,512]{1,0:T(8,128)(2,1)} %get-tuple-element.20), channel_id=1, source_target_pairs={{0,2},{2,0},{1,3},{3,1},{4,6},{6,4},{5,7},{7,5},{8,10},{10,8},{9,1... | collective-permute-start | bytes 1572872 | tf_op jit(solution)/shard_map/ppermute | solution.py:21
  62.7 4.2 %all-to-all-start.3 = ((bf16[4,256,512]{2,1,0:T(8,128)(2,1)}), bf16[4,256,512]{2,1,0:T(8,128)(2,1)}, u32[]{:S(2)}, u32[]{:S(2)}) async-start(bf16[4,256,512]{2,1,0:T(8,128)(2,1)} %get-tuple-element.21), calls=%async_computation.3 | async-start | bytes 2097152 | tf_op jit(solution)/shard_map/all_to_all | solution.py:25
  67.2 2.0 %add_convert_fusion.1 = bf16[512,512]{1,0:T(8,128)(2,1)} fusion(bf16[512,512]{1,0:T(8,128)(2,1)} %collective-permute-done.8, bf16[512,512]{1,0:T(8,128)(2,1)S(1)} %get-tuple-element.19), kind=kLoop, calls=%fused_computation.9 | loop fusion | flops 1048576 | bytes 1572864 | tf_op jit(solution)/shard_map/convert_element_type | solution.py:193
  69.2 13.0 %all-to-all-done.3 = bf16[4,256,512]{2,1,0:T(8,128)(2,1)} async-done(((bf16[4,256,512]{2,1,0:T(8,128)(2,1)}), bf16[4,256,512]{2,1,0:T(8,128)(2,1)}, u32[]{:S(2)}, u32[]{:S(2)}) %all-to-all-start.3) | async-done | bytes 1048608 | tf_op jit(solution)/shard_map/all_to_all | solution.py:25
  82.1 4.1 %all-to-all-start.1 = ((bf16[8,64,512]{2,1,0:T(8,128)(2,1)}), bf16[8,64,512]{2,1,0:T(8,128)(2,1)}, u32[]{:S(2)}, u32[]{:S(2)}) async-start(bf16[8,64,512]{2,1,0:T(8,128)(2,1)} %bitcast.21), calls=%async_computation.1 | async-start | bytes 1048576 | tf_op jit(solution)/shard_map/all_to_all | solution.py:25
  86.3 2.6 %fusion.1 = (f32[256,512]{1,0:T(8,128)}, f32[256,512]{1,0:T(8,128)S(1)}) fusion(bf16[4,256,512]{2,1,0:T(8,128)(2,1)} %all-to-all-done.3, pred[4]{0:T(512)(128)(4,1)S(1)} %iota_compare_fusion.1), kind=kLoop, calls=%fused_computation.3 | loop fusion | flops 2359296 | bytes 2097156 | tf_op jit(solution)/shard_map/reduce_sum | solution.py:244
  88.9 6.1 %all-to-all-done.1 = bf16[8,64,512]{2,1,0:T(8,128)(2,1)} async-done(((bf16[8,64,512]{2,1,0:T(8,128)(2,1)}), bf16[8,64,512]{2,1,0:T(8,128)(2,1)}, u32[]{:S(2)}, u32[]{:S(2)}) %all-to-all-start.1) | async-done | bytes 524320 | tf_op jit(solution)/shard_map/all_to_all | solution.py:25
  95.0 1.1 reduce_sum.30
  96.1 3.3 %collective-permute-start.11 = (bf16[64,512]{1,0:T(8,128)(2,1)S(1)}, bf16[64,512]{1,0:T(8,128)(2,1)S(1)}, u32[]{:S(2)}, u32[]{:S(2)}) collective-permute-start(bf16[64,512]{1,0:T(8,128)(2,1)S(1)} %reduce_sum.30), channel_id=1, source_target_pairs={{0,192},{32,224},{64,0},{96,32},{128,64},{160,96},{192,128},{224,1... | collective-permute-start | bytes 196616 | tf_op jit(solution)/shard_map/ppermute | solution.py:21
  100.9 1.5 %add_convert_fusion = bf16[4,512,256]{2,1,0:T(8,128)(2,1)S(1)} fusion(bf16[4,512,256]{2,1,0:T(8,128)(2,1)} %collective-permute-done.14, bf16[4,512,256]{2,1,0:T(8,128)(2,1)S(1)} %get-tuple-element.23), kind=kLoop, calls=%fused_computation.4 | loop fusion | flops 2097152 | bytes 3145728 | tf_op jit(solution)/shard_map/convert_element_type | solution.py:234
  104.5 3.4 %collective-permute-start.12 = (bf16[64,512]{1,0:T(8,128)(2,1)S(1)}, bf16[64,512]{1,0:T(8,128)(2,1)S(1)}, u32[]{:S(2)}, u32[]{:S(2)}) collective-permute-start(bf16[64,512]{1,0:T(8,128)(2,1)S(1)} %add_convert_fusion.6), channel_id=1, source_target_pairs={{0,128},{32,160},{64,192},{96,224},{128,0},{160,32},{192,64},{224,... | collective-permute-start | bytes 196616 | tf_op jit(solution)/shard_map/ppermute | solution.py:21
  108.6 1.5 %collective-permute-start.13 = (bf16[256,512]{1,0:T(8,128)(2,1)}, bf16[256,512]{1,0:T(8,128)(2,1)S(1)}, u32[]{:S(2)}, u32[]{:S(2)}) collective-permute-start(bf16[256,512]{1,0:T(8,128)(2,1)} %add_convert_fusion.3), channel_id=1, source_target_pairs={{0,224},{32,0},{64,32},{96,64},{128,96},{160,128},{192,160},{224,1... | collective-permute-start | bytes 786440 | tf_op jit(solution)/shard_map/ppermute | solution.py:21
  110.1 1.4 %collective-permute-done.12 = bf16[64,512]{1,0:T(8,128)(2,1)S(1)} collective-permute-done((bf16[64,512]{1,0:T(8,128)(2,1)S(1)}, bf16[64,512]{1,0:T(8,128)(2,1)S(1)}, u32[]{:S(2)}, u32[]{:S(2)}) %collective-permute-start.12) | collective-permute-done | bytes 65568 | tf_op jit(solution)/shard_map/ppermute | solution.py:21
  112.5 4.2 %all-to-all-start.2 = ((bf16[8,64,512]{2,1,0:T(8,128)(2,1)}), bf16[8,64,512]{2,1,0:T(8,128)(2,1)}, u32[]{:S(2)}, u32[]{:S(2)}) async-start(bf16[8,64,512]{2,1,0:T(8,128)(2,1)} %broadcast_in_dim.35), calls=%async_computation.2 | async-start | bytes 1048576 | tf_op jit(solution)/shard_map/all_to_all | solution.py:25
  116.6 1.1 convert_add_fusion
  119.5 4.8 %collective-permute-done.16 = bf16[512,256]{1,0:T(8,128)(2,1)S(1)} collective-permute-done((bf16[512,256]{1,0:T(8,128)(2,1)S(1)}, bf16[512,256]{1,0:T(8,128)(2,1)S(1)}, u32[]{:S(2)}, u32[]{:S(2)}) %collective-permute-start.16) | collective-permute-done | bytes 262176 | tf_op jit(solution)/shard_map/ppermute | solution.py:21
  125.4 5.7 %collective-permute-start.17 = (bf16[512,512]{1,0:T(8,128)(2,1)}, bf16[512,512]{1,0:T(8,128)(2,1)S(1)}, u32[]{:S(2)}, u32[]{:S(2)}) collective-permute-start(bf16[512,512]{1,0:T(8,128)(2,1)} %bitcast.7), channel_id=1, source_target_pairs={{0,2},{2,0},{1,3},{3,1},{4,6},{6,4},{5,7},{7,5},{8,10},{10,8},{9,1... | collective-permute-start | bytes 1572872 | tf_op jit(solution)/shard_map/ppermute | solution.py:21
  131.1 1.7 %collective-permute-done.17 = bf16[512,512]{1,0:T(8,128)(2,1)S(1)} collective-permute-done((bf16[512,512]{1,0:T(8,128)(2,1)}, bf16[512,512]{1,0:T(8,128)(2,1)S(1)}, u32[]{:S(2)}, u32[]{:S(2)}) %collective-permute-start.17) | collective-permute-done | bytes 524320 | tf_op jit(solution)/shard_map/ppermute | solution.py:21
  132.9 2.5 %select_convert_fusion = (f32[512,512]{1,0:T(8,128)}, f32[512,512]{1,0:T(8,128)}) fusion(bf16[512,512]{1,0:T(8,128)(2,1)S(1)} %collective-permute-done.17, bf16[512,512]{1,0:T(8,128)(2,1)} %bitcast.7, pred[]{:T(512)S(6)} %eq.12), kind=kLoop, calls=%fused_computation.17 | loop fusion | flops 1048576 | bytes 3145729 | tf_op jit(solution)/shard_map/convert_element_type | solution.py:203
  (70 shorter events, 19.1 us)
Async XLA Ops:
  0.6 16.2 %copy-start.16 = (bf16[256,512]{1,0:T(8,128)(2,1)S(1)}, bf16[256,512]{1,0:T(8,128)(2,1)}, u32[]{:S(2)}) copy-start(bf16[256,512]{1,0:T(8,128)(2,1)} %param.6) | copy-start | bytes 786436
  2.3 12.9 %collective-permute-start.1 = (bf16[272,512]{1,0:T(8,128)(2,1)S(1)}, bf16[272,512]{1,0:T(8,128)(2,1)S(1)}, u32[]{:S(2)}, u32[]{:S(2)}) collective-permute-start(bf16[272,512]{1,0:T(8,128)(2,1)S(1)} %fusion.6), channel_id=1, source_target_pairs={{0,32},{32,64},{64,96},{96,128},{128,160},{160,192},{192,224},{224... | collective-permute-start | bytes 835592 | tf_op jit(solution)/shard_map/ppermute | solution.py:21
  6.5 16.0 %copy-start.2 = (bf16[272,512]{1,0:T(8,128)(2,1)}, bf16[272,512]{1,0:T(8,128)(2,1)S(1)}, u32[]{:S(2)}) copy-start(bf16[272,512]{1,0:T(8,128)(2,1)S(1)} %fusion.7.refs_2_) | copy-start | bytes 835588
  6.5 8.7 %collective-permute-start.2 = (bf16[272,512]{1,0:T(8,128)(2,1)S(1)}, bf16[272,512]{1,0:T(8,128)(2,1)S(1)}, u32[]{:S(2)}, u32[]{:S(2)}) collective-permute-start(bf16[272,512]{1,0:T(8,128)(2,1)S(1)} %fusion.7.refs_2_), channel_id=1, source_target_pairs={{0,4},{4,0},{1,5},{5,1},{2,6},{6,2},{3,7},{7,3},{8,12},{12,8},{9,1... | collective-permute-start | bytes 835592 | tf_op jit(solution)/shard_map/ppermute | solution.py:21
  7.9 9.0 %collective-permute-start = (bf16[272,512]{1,0:T(8,128)(2,1)S(1)}, bf16[272,512]{1,0:T(8,128)(2,1)S(1)}, u32[]{:S(2)}, u32[]{:S(2)}) collective-permute-start(bf16[272,512]{1,0:T(8,128)(2,1)S(1)} %fusion.7.refs_2_), channel_id=1, source_target_pairs={{0,224},{32,0},{64,32},{96,64},{128,96},{160,128},{192,160},{224,1... | collective-permute-start | bytes 835592 | tf_op jit(solution)/shard_map/ppermute | solution.py:21
  15.2 9.8 %copy-start.8 = (bf16[272,512]{1,0:T(8,128)(2,1)}, bf16[272,512]{1,0:T(8,128)(2,1)S(1)}, u32[]{:S(2)}) copy-start(bf16[272,512]{1,0:T(8,128)(2,1)S(1)} %collective-permute-done.2.refs_3_) | copy-start | bytes 835588
  16.9 8.0 %copy-start.10 = (bf16[272,512]{1,0:T(8,128)(2,1)}, bf16[272,512]{1,0:T(8,128)(2,1)S(1)}, u32[]{:S(2)}) copy-start(bf16[272,512]{1,0:T(8,128)(2,1)S(1)} %collective-permute-done.refs_6_) | copy-start | bytes 835588
  18.1 17.8 %copy-start = (bf16[512,512]{1,0:T(8,128)(2,1)S(1)}, bf16[512,512]{1,0:T(8,128)(2,1)}, u32[]{:S(2)}) copy-start(bf16[512,512]{1,0:T(8,128)(2,1)} %refs_10_.1) | copy-start | bytes 1572868
  18.1 17.8 %all-to-all-start = ((bf16[4,272,512]{2,1,0:T(8,128)(2,1)}), bf16[4,272,512]{2,1,0:T(8,128)(2,1)S(1)}, u32[]{:S(2)}, u32[]{:S(2)}) async-start(bf16[4,272,512]{2,1,0:T(8,128)(2,1)} %bitcast.20), calls=%async_computation | async-start | bytes 2228224 | tf_op jit(solution)/shard_map/all_to_all | solution.py:25
  22.3 6.0 %collective-permute-start.5 = (bf16[272,512]{1,0:T(8,128)(2,1)S(1)}, bf16[272,512]{1,0:T(8,128)(2,1)S(1)}, u32[]{:S(2)}, u32[]{:S(2)}) collective-permute-start(bf16[272,512]{1,0:T(8,128)(2,1)S(1)} %collective-permute-done.refs_6_), channel_id=1, source_target_pairs={{0,4},{4,0},{1,5},{5,1},{2,6},{6,2},{3,7},{7,3},{8,12},{12,8},{9,1... | collective-permute-start | bytes 835592 | tf_op jit(solution)/shard_map/ppermute | solution.py:21
  22.5 11.0 %collective-permute-start.3 = (bf16[272,512]{1,0:T(8,128)(2,1)S(1)}, bf16[272,512]{1,0:T(8,128)(2,1)}, u32[]{:S(2)}, u32[]{:S(2)}) collective-permute-start(bf16[272,512]{1,0:T(8,128)(2,1)S(1)} %fusion.7.refs_2_), channel_id=1, source_target_pairs={{0,2},{2,0},{1,3},{3,1},{4,6},{6,4},{5,7},{7,5},{8,10},{10,8},{9,1... | collective-permute-start | bytes 835592 | tf_op jit(solution)/shard_map/ppermute | solution.py:21
  24.9 8.6 %collective-permute-start.6 = (bf16[272,512]{1,0:T(8,128)(2,1)S(1)}, bf16[272,512]{1,0:T(8,128)(2,1)}, u32[]{:S(2)}, u32[]{:S(2)}) collective-permute-start(bf16[272,512]{1,0:T(8,128)(2,1)S(1)} %collective-permute-done.refs_6_), channel_id=1, source_target_pairs={{0,2},{2,0},{1,3},{3,1},{4,6},{6,4},{5,7},{7,5},{8,10},{10,8},{9,1... | collective-permute-start | bytes 835592 | tf_op jit(solution)/shard_map/ppermute | solution.py:21
  25.0 8.5 %collective-permute-start.4 = (bf16[272,512]{1,0:T(8,128)(2,1)S(1)}, bf16[272,512]{1,0:T(8,128)(2,1)}, u32[]{:S(2)}, u32[]{:S(2)}) collective-permute-start(bf16[272,512]{1,0:T(8,128)(2,1)S(1)} %collective-permute-done.2.refs_3_), channel_id=1, source_target_pairs={{0,2},{2,0},{1,3},{3,1},{4,6},{6,4},{5,7},{7,5},{8,10},{10,8},{9,1... | collective-permute-start | bytes 835592 | tf_op jit(solution)/shard_map/ppermute | solution.py:21
  28.3 7.7 %copy-start.12 = (bf16[272,512]{1,0:T(8,128)(2,1)}, bf16[272,512]{1,0:T(8,128)(2,1)S(1)}, u32[]{:S(2)}) copy-start(bf16[272,512]{1,0:T(8,128)(2,1)S(1)} %collective-permute-done.5.refs_7_) | copy-start | bytes 835588
  28.3 5.2 %collective-permute-start.7 = (bf16[272,512]{1,0:T(8,128)(2,1)S(1)}, bf16[272,512]{1,0:T(8,128)(2,1)}, u32[]{:S(2)}, u32[]{:S(2)}) collective-permute-start(bf16[272,512]{1,0:T(8,128)(2,1)S(1)} %collective-permute-done.5.refs_7_), channel_id=1, source_target_pairs={{0,2},{2,0},{1,3},{3,1},{4,6},{6,4},{5,7},{7,5},{8,10},{10,8},{9,1... | collective-permute-start | bytes 835592 | tf_op jit(solution)/shard_map/ppermute | solution.py:21
  59.8 7.2 %copy-start.7 = (bf16[4,512,256]{2,1,0:T(8,128)(2,1)S(1)}, bf16[4,512,256]{2,1,0:T(8,128)(2,1)}, u32[]{:S(2)}) copy-start(bf16[4,512,256]{2,1,0:T(8,128)(2,1)} %copy-done.6) | copy-start | bytes 3145732
  59.8 7.4 %collective-permute-start.8 = (bf16[512,512]{1,0:T(8,128)(2,1)}, bf16[512,512]{1,0:T(8,128)(2,1)}, u32[]{:S(2)}, u32[]{:S(2)}) collective-permute-start(bf16[512,512]{1,0:T(8,128)(2,1)} %get-tuple-element.20), channel_id=1, source_target_pairs={{0,2},{2,0},{1,3},{3,1},{4,6},{6,4},{5,7},{7,5},{8,10},{10,8},{9,1... | collective-permute-start | bytes 1572872 | tf_op jit(solution)/shard_map/ppermute | solution.py:21
  62.7 19.4 %all-to-all-start.3 = ((bf16[4,256,512]{2,1,0:T(8,128)(2,1)}), bf16[4,256,512]{2,1,0:T(8,128)(2,1)}, u32[]{:S(2)}, u32[]{:S(2)}) async-start(bf16[4,256,512]{2,1,0:T(8,128)(2,1)} %get-tuple-element.21), calls=%async_computation.3 | async-start | bytes 2097152 | tf_op jit(solution)/shard_map/all_to_all | solution.py:25
  67.0 33.9 %collective-permute-start.14 = (bf16[4,512,256]{2,1,0:T(8,128)(2,1)S(1)}, bf16[4,512,256]{2,1,0:T(8,128)(2,1)}, u32[]{:S(2)}, u32[]{:S(2)}) collective-permute-start(bf16[4,512,256]{2,1,0:T(8,128)(2,1)S(1)} %copy-done.7), channel_id=1, source_target_pairs={{0,2},{2,0},{1,3},{3,1},{4,6},{6,4},{5,7},{7,5},{8,10},{10,8},{9,1... | collective-permute-start | bytes 3145736 | tf_op jit(solution)/shard_map/ppermute | solution.py:21
  82.1 12.9 %all-to-all-start.1 = ((bf16[8,64,512]{2,1,0:T(8,128)(2,1)}), bf16[8,64,512]{2,1,0:T(8,128)(2,1)}, u32[]{:S(2)}, u32[]{:S(2)}) async-start(bf16[8,64,512]{2,1,0:T(8,128)(2,1)} %bitcast.21), calls=%async_computation.1 | async-start | bytes 1048576 | tf_op jit(solution)/shard_map/all_to_all | solution.py:25
  96.1 7.4 %collective-permute-start.11 = (bf16[64,512]{1,0:T(8,128)(2,1)S(1)}, bf16[64,512]{1,0:T(8,128)(2,1)S(1)}, u32[]{:S(2)}, u32[]{:S(2)}) collective-permute-start(bf16[64,512]{1,0:T(8,128)(2,1)S(1)} %reduce_sum.30), channel_id=1, source_target_pairs={{0,192},{32,224},{64,0},{96,32},{128,64},{160,96},{192,128},{224,1... | collective-permute-start | bytes 196616 | tf_op jit(solution)/shard_map/ppermute | solution.py:21
  99.4 4.4 %collective-permute-start.10 = (bf16[64,512]{1,0:T(8,128)(2,1)S(1)}, bf16[64,512]{1,0:T(8,128)(2,1)S(1)}, u32[]{:S(2)}, u32[]{:S(2)}) collective-permute-start(bf16[64,512]{1,0:T(8,128)(2,1)S(1)} %reduce_sum.30), channel_id=1, source_target_pairs={{0,224},{32,0},{64,32},{96,64},{128,96},{160,128},{192,160},{224,1... | collective-permute-start | bytes 196616 | tf_op jit(solution)/shard_map/ppermute | solution.py:21
  100.1 4.3 %collective-permute-start.9 = (bf16[64,512]{1,0:T(8,128)(2,1)S(1)}, bf16[64,512]{1,0:T(8,128)(2,1)S(1)}, u32[]{:S(2)}, u32[]{:S(2)}) collective-permute-start(bf16[64,512]{1,0:T(8,128)(2,1)S(1)} %reduce_sum.30), channel_id=1, source_target_pairs={{0,32},{32,64},{64,96},{96,128},{128,160},{160,192},{192,224},{224... | collective-permute-start | bytes 196616 | tf_op jit(solution)/shard_map/ppermute | solution.py:21
  102.4 5.5 %copy-start.5 = (bf16[256,512]{1,0:T(8,128)(2,1)S(1)}, bf16[256,512]{1,0:T(8,128)(2,1)}, u32[]{:S(2)}) copy-start(bf16[256,512]{1,0:T(8,128)(2,1)} %copy-done.4) | copy-start | bytes 786436
  102.4 5.5 %copy-start.15 = (f32[256,512]{1,0:T(8,128)S(1)}, f32[256,512]{1,0:T(8,128)}, u32[]{:S(2)}) copy-start(f32[256,512]{1,0:T(8,128)} %get-tuple-element.28) | copy-start | bytes 1572868
  102.4 14.2 %collective-permute-start.15 = (bf16[2,512,256]{2,1,0:T(8,128)(2,1)S(1)}, bf16[2,512,256]{2,1,0:T(8,128)(2,1)}, u32[]{:S(2)}, u32[]{:S(2)}) collective-permute-start(bf16[2,512,256]{2,1,0:T(8,128)(2,1)S(1)} %slice.18), channel_id=1, source_target_pairs={{0,4},{4,0},{1,5},{5,1},{2,6},{6,2},{3,7},{7,3},{8,12},{12,8},{9,1... | collective-permute-start | bytes 1572872 | tf_op jit(solution)/shard_map/ppermute | solution.py:21
  104.5 7.1 %collective-permute-start.12 = (bf16[64,512]{1,0:T(8,128)(2,1)S(1)}, bf16[64,512]{1,0:T(8,128)(2,1)S(1)}, u32[]{:S(2)}, u32[]{:S(2)}) collective-permute-start(bf16[64,512]{1,0:T(8,128)(2,1)S(1)} %add_convert_fusion.6), channel_id=1, source_target_pairs={{0,128},{32,160},{64,192},{96,224},{128,0},{160,32},{192,64},{224,... | collective-permute-start | bytes 196616 | tf_op jit(solution)/shard_map/ppermute | solution.py:21
  108.6 9.8 %collective-permute-start.13 = (bf16[256,512]{1,0:T(8,128)(2,1)}, bf16[256,512]{1,0:T(8,128)(2,1)S(1)}, u32[]{:S(2)}, u32[]{:S(2)}) collective-permute-start(bf16[256,512]{1,0:T(8,128)(2,1)} %add_convert_fusion.3), channel_id=1, source_target_pairs={{0,224},{32,0},{64,32},{96,64},{128,96},{160,128},{192,160},{224,1... | collective-permute-start | bytes 786440 | tf_op jit(solution)/shard_map/ppermute | solution.py:21
  112.5 12.9 %all-to-all-start.2 = ((bf16[8,64,512]{2,1,0:T(8,128)(2,1)}), bf16[8,64,512]{2,1,0:T(8,128)(2,1)}, u32[]{:S(2)}, u32[]{:S(2)}) async-start(bf16[8,64,512]{2,1,0:T(8,128)(2,1)} %broadcast_in_dim.35), calls=%async_computation.2 | async-start | bytes 1048576 | tf_op jit(solution)/shard_map/all_to_all | solution.py:25
  117.8 6.6 %copy-start.14 = (bf16[512,512]{1,0:T(8,128)(2,1)S(1)}, bf16[512,512]{1,0:T(8,128)(2,1)}, u32[]{:S(2)}) copy-start(bf16[512,512]{1,0:T(8,128)(2,1)} %param.9) | copy-start | bytes 1572868
  117.8 6.5 %collective-permute-start.16 = (bf16[512,256]{1,0:T(8,128)(2,1)S(1)}, bf16[512,256]{1,0:T(8,128)(2,1)S(1)}, u32[]{:S(2)}, u32[]{:S(2)}) collective-permute-start(bf16[512,256]{1,0:T(8,128)(2,1)S(1)} %fusion.9), channel_id=1, source_target_pairs={{0,32},{32,64},{64,96},{96,128},{128,160},{160,192},{192,224},{224... | collective-permute-start | bytes 786440 | tf_op jit(solution)/shard_map/ppermute | solution.py:21
  125.4 7.5 %collective-permute-start.17 = (bf16[512,512]{1,0:T(8,128)(2,1)}, bf16[512,512]{1,0:T(8,128)(2,1)S(1)}, u32[]{:S(2)}, u32[]{:S(2)}) collective-permute-start(bf16[512,512]{1,0:T(8,128)(2,1)} %bitcast.7), channel_id=1, source_target_pairs={{0,2},{2,0},{1,3},{3,1},{4,6},{6,4},{5,7},{7,5},{8,10},{10,8},{9,1... | collective-permute-start | bytes 1572872 | tf_op jit(solution)/shard_map/ppermute | solution.py:21
  (7 other events, 6.5 us)

commit v3 on v0

v3 whole, which is shorter than its diff:
```python
import functools

import jax
import jax.numpy as jnp
from jax import lax
from jax.experimental import pallas as pl
from jax.experimental.pallas import tpu as pltpu
from jax.sharding import Mesh, PartitionSpec as P

logit_scale = 14.2857143
log2_e = 1.4426950408889634
PAD = 16

BF = jnp.bfloat16
F32 = jnp.float32
XY = ("x", "yl")


def shift(value, axis, steps):
    count = lax.axis_size(axis)
    return lax.ppermute(value, axis, [(i, (i + steps) % count) for i in range(count)])


def exchange(value, axis):
    return lax.all_to_all(value, axis, split_axis=0, concat_axis=0, tiled=True)


def dot_nn(a, b):
    return jnp.dot(a, b, preferred_element_type=F32)


def dot_nt(a, b):
    return lax.dot_general(a, b, (((1,), (1,)), ((), ())), preferred_element_type=F32)


def tiles_kernel(inv_rows, where_ref, *refs):
    audio_hbm = refs[:5]
    text_hbm = refs[5:13]
    ha_hbm, ht_hbm = refs[13:15]
    da_hbm = refs[15:20]
    mine_hbm, send_hbm, keep_hbm, give_hbm = refs[20:24]
    (ae, al, te, tl, ha, ht, za, zat, zt, ua, ut, na, nt, ea, eb, ga, gt) = refs[24:41]
    (da, dt, keep, give, in_sem, out_sem) = refs[41:]
    width = ha.shape[0]
    rows = ae.shape[0] // 5
    core = where_ref[4]

    def span(first, count=1):
        return slice(first * rows, (first + count) * rows)

    def fetch(block, values, lse, at):
        return [
            (block.at[0:rows, :], values.at[span(at), :]),
            (block.at[rows : rows + PAD, :], lse.at[at]),
        ]

    copies = [(ha_hbm, ha), (ht_hbm, ht)]
    copies += fetch(audio_hbm[0], ae, al, 0)
    for j in range(4):
        for plane in range(2):
            copies += fetch(text_hbm[4 * plane + j], te, tl, 2 * j + plane)
    for i in range(1, 5):
        copies += fetch(audio_hbm[i], ae, al, i)
    copies = [pltpu.make_async_copy(s, d, in_sem.at[i]) for i, (s, d) in enumerate(copies)]
    for c in copies:
        c.start()
    for c in copies[:2]:
        c.wait()
    ha[...] = ha[...].T
    ht[...] = ht[...].T

    def project(head, embeds, cols, u_ref, z_ref, n_ref):
        p = dot_nt(head[...], embeds[cols, :])
        inv = lax.rsqrt(jnp.sum(p * p, axis=0, keepdims=True) + 1e-06)
        u = p * inv
        z = u.astype(BF)
        u_ref[:, cols] = u
        z_ref[:, cols] = z
        n_ref[:, cols] = jnp.broadcast_to(inv, (8, u.shape[1]))
        return z

    def half_exp(lse):
        return 0.5 * jnp.exp(-lse[:, :rows].astype(F32)[0:1, :])

    def audio_block(i):
        z = project(ha, ae, span(i), ua, zat, na)
        za[span(i), :] = z.T
        ea[span(i), :] = jnp.broadcast_to(half_exp(al[i]), (ea.shape[1], rows)).T

    def text_chunk(j):
        project(ht, te, span(2 * j, 2), ut, zt, nt)
        for b in (2 * j, 2 * j + 1):
            eb[:, span(b)] = jnp.broadcast_to(half_exp(tl[b]), (8, rows))

    row_id = lax.broadcasted_iota(jnp.int32, (rows, rows), 0)
    col_id = lax.broadcasted_iota(jnp.int32, (rows, rows), 1)
    eye = (row_id == col_id).astype(F32)

    def tile(j):
        cols = span(2 * j, 2)
        at = pl.ds(pl.multiple_of(where_ref[j] * rows, rows), 4 * rows) if j else span(0, 4)
        z = zt[:, cols]
        e = jnp.exp2(dot_nn(za[at, :], z) * (logit_scale * log2_e))
        row_scale = ea[at, :]
        scale = jnp.concatenate([row_scale] * (2 * rows // row_scale.shape[1]), axis=1)
        w = e * (scale + eb[0:1, cols])
        if j == 0:
            corner = jnp.concatenate([w[:rows, :rows] - eye, w[:rows, rows:]], axis=1)
            w = jnp.concatenate([corner, w[rows:]], axis=0)
        w = w.astype(BF)
        if j == 0:
            ga[:, at] = dot_nt(z, w)
            ga[:, span(4)] = jnp.zeros((width, rows), F32)
        else:
            ga[:, at] += dot_nt(z, w)
        gt[:, cols] = dot_nn(zat[:, at], w)

    for c in copies[2:4]:
        c.wait()
    audio_block(0)
    for c in copies[4:20]:
        c.wait()
    for j in range(4):
        text_chunk(j)
    for c in copies[20:]:
        c.wait()
    for i in range(1, 5):
        audio_block(i)
    for j in range(4):
        tile(j)

    def finish(g_ref, u_ref, n_ref, d_ref, cols):
        g = g_ref[:, cols]
        u = u_ref[:, cols]
        along = jnp.sum(u * g, axis=0, keepdims=True)
        d_ref[:, cols] = ((g - u * along) * (n_ref[0:1, cols] * logit_scale)).astype(BF)

    for j in range(4):
        finish(gt, ut, nt, dt, span(2 * j, 2))
    for i in range(5):
        finish(ga, ua, na, da, span(i))
    outs = [(dt.at[:, span(b)], (mine_hbm if b < 4 else send_hbm).at[b % 4]) for b in range(8)]
    outs += [(da.at[:, span(i)], da_hbm[i]) for i in range(5)]
    outs = [pltpu.make_async_copy(s, d, out_sem.at[i]) for i, (s, d) in enumerate(outs)]
    for c in outs:
        c.start()
    head_t = (dot_nn(dt[...], te[...]) * inv_rows).astype(BF).T
    head_a = (dot_nn(da[...], ae[...]) * inv_rows).astype(BF).T

    @pl.when(core == 0)
    def _():
        keep[...] = head_a
        give[...] = head_t

    @pl.when(core == 1)
    def _():
        keep[...] = head_t
        give[...] = head_a

    last = [(give, give_hbm), (keep, keep_hbm)]
    last = [pltpu.make_async_copy(s, d, out_sem.at[13 + i]) for i, (s, d) in enumerate(last)]
    for c in last:
        c.start()
    for c in outs + last:
        c.wait()


def tiles(where, audio, text, audio_head, text_head, batch_rows):
    rows, width = audio[0].shape[0] - PAD, audio[0].shape[1]
    lanes = min(128, rows)
    anywhere = pl.BlockSpec(memory_space=pl.ANY)
    vmem = pltpu.VMEM
    shape = jax.ShapeDtypeStruct
    return pl.pallas_call(
        functools.partial(tiles_kernel, 1.0 / batch_rows),
        out_shape=(shape((width, rows), BF),) * 5
        + (
            shape((4, width, rows), BF),
            shape((4, width, rows), BF),
            shape((width, width), BF),
            shape((width, width), BF),
        ),
        in_specs=[pl.BlockSpec(memory_space=pltpu.SMEM)] + [anywhere] * 15,
        out_specs=(anywhere,) * 9,
        scratch_shapes=[
            vmem((5 * rows, width), BF),
            vmem((5, PAD, width), BF),
            vmem((8 * rows, width), BF),
            vmem((8, PAD, width), BF),
            vmem((width, width), BF),
            vmem((width, width), BF),
            vmem((5 * rows, width), BF),
            vmem((width, 5 * rows), BF),
            vmem((width, 8 * rows), BF),
            vmem((width, 5 * rows), F32),
            vmem((width, 8 * rows), F32),
            vmem((8, 5 * rows), F32),
            vmem((8, 8 * rows), F32),
            vmem((5 * rows, lanes), F32),
            vmem((8, 8 * rows), F32),
            vmem((width, 5 * rows), F32),
            vmem((width, 8 * rows), F32),
            vmem((width, 5 * rows), BF),
            vmem((width, 8 * rows), BF),
            vmem((width, width), BF),
            vmem((width, width), BF),
            pltpu.SemaphoreType.DMA((28,)),
            pltpu.SemaphoreType.DMA((15,)),
        ],
        compiler_params=pltpu.CompilerParams(vmem_limit_bytes=60 * 1024 * 1024),
        cost_estimate=pl.CostEstimate(
            flops=12_000_000_000, bytes_accessed=9_000_000, transcendentals=2_100_000
        ),
    )(where, *audio, *text, audio_head, text_head)


def packed(embed, lse):
    extra = jnp.pad(lse, ((0, PAD - 1), (0, embed.shape[1] - lse.shape[1])))
    return jnp.concatenate([embed, extra], axis=0)


def diagonal_shift(value, steps):
    count = lax.axis_size("z")
    pairs = [(2 * z + y, 2 * ((z + steps) % count) + 1 - y) for z in range(count) for y in (0, 1)]
    return lax.ppermute(value, ("z", "yl"), pairs)


def summed(parts):
    return jnp.sum(parts.astype(F32), axis=0)


def added(first, *others):
    total = first.astype(F32)
    for other in others:
        total = total + other.astype(F32)
    return total.astype(BF)


def repeated(part, count):
    wide = jnp.broadcast_to(part[None], (count,) + part.shape)
    return wide.reshape(count * part.shape[0], part.shape[1])


def dot_head(dproj_t, head):
    out = lax.dot_general(dproj_t, head, (((0,), (1,)), ((), ())), preferred_element_type=F32)
    return out.astype(BF)


def local(audio_embed, text_embed, audio_head, text_head, audio_lse, text_lse):
    rows, width = audio_embed.shape
    blocks = lax.axis_size(("z", "x", "yl", "c"))
    x = lax.axis_index("x")
    yl = lax.axis_index("yl")
    core = lax.axis_index("c")
    line = ("z", "x")
    together = lax.optimization_barrier

    lse = jnp.stack([audio_lse, text_lse])
    a_own, t_own = together((packed(audio_embed, lse[:1]), packed(text_embed, lse[1:])))
    audio = [a_own] + [shift(a_own, line, s) for s in (1, 2, 3, 4)]
    here = [t_own, shift(t_own, "yl", 1)]
    ahead = [shift(t_own, "z", -1), diagonal_shift(t_own, -1)]
    here += [shift(v, "c", 1) for v in here]
    ahead += [shift(v, "c", 1) for v in ahead]

    behind_y, behind_c = (yl == 1).astype(jnp.int32), (core == 1).astype(jnp.int32)
    where = jnp.stack([jnp.zeros_like(core), behind_y, behind_c, behind_y, core])
    *da, dt_mine, dt_send, keep, give = tiles(
        where, audio, here + ahead, audio_head, text_head, rows * blocks
    )

    head = added(keep, shift(give, "c", 1))
    dt_in = shift(dt_send, "c", 1)
    head = exchange(head, XY)
    dt_sum = added(dt_mine, dt_in)
    back = [shift(da[s], "x", -s) for s in (1, 2, 3)]
    dt_pair = added(dt_sum[:2], shift(dt_sum[2:], "yl", 1))
    here_sum, behind_sum = da[0].astype(F32), da[4].astype(F32)
    for s, part in zip((1, 2, 3), back):
        past = x + s >= 4
        here_sum = here_sum + jnp.where(past, 0.0, part.astype(F32))
        behind_sum = behind_sum + jnp.where(past, part.astype(F32), 0.0)
    dt_ahead = shift(dt_pair[1], "z", 1)
    da_ahead = shift(behind_sum.astype(BF), "z", -1)
    head = summed(head.reshape(8, width // 8, width)).astype(BF)
    head = added(head, *[shift(head, "z", s) for s in (1, -1, -2)])
    far = shift(head, "z", 4)
    head = exchange(repeated(added(head, far), 8), XY)
    audio_input = dot_head(added(here_sum, da_ahead), audio_head)
    text_input = dot_head(added(dt_pair[0], dt_ahead), text_head)
    head, audio_input, text_input = together((head, audio_input, text_input))
    other = shift(head, "c", 1)
    audio_total = jnp.where(core == 0, head, other).astype(F32)
    text_total = jnp.where(core == 0, other, head).astype(F32)
    return audio_input, text_input, audio_total, text_total


def solution(mesh):
    sizes = (8, 4, 2, 2, mesh.shape["rep"])
    grid = Mesh(mesh.devices.reshape(sizes), ("z", "x", "yl", "c", "rep"))
    every = ("rep", "z", "x", "yl", "c")
    return jax.shard_map(
        local,
        mesh=grid,
        in_specs=(P(every, None), P(every, None), P(), P(), P(every), P(every)),
        out_specs=(P(every, None), P(every, None), P("rep", None), P("rep", None)),
        check_vma=False,
    )
```

time: 1670 us -> 116 us (0.07)
  waiting for transfers between devices: 1190 us -> 18.5 us
  starting transfers between devices: 394 us -> 46 us
  matrix products: 57 us -> 3.23 us
  blocking collectives: 0 us -> 20.7 us
  Pallas kernels: 0 us -> 17.2 us
    psum x1 -> x0, waiting for transfers between devices: 1090 us -> none  [local(): audio_total, text_total = lax.psum((audio_sum, text_sum), 'blk')]
    ppermute x94 -> x24, starting transfers between devices: 394 us -> 42.2 us  [the longest x23 34.7 us: shift(): lax.ppermute(value, axis, [(i, (i + steps) % count) for i in range(count)])]
    ppermute x94 -> x24, waiting for transfers between devices: 97.8 us -> 18.5 us  [the longest x23 17.7 us: shift(): lax.ppermute(value, axis, [(i, (i + steps) % count) for i in range(count)])]
    dot_general x102 -> x2, matrix products: 57 us -> 3.23 us  [dot_head(): lax.dot_general(dproj_t, head, (((0,), (1,)), ((), ())), preferred_elemen...]
    all_to_all x0 -> x1, blocking collectives: none -> 20.7 us  [exchange(): return lax.all_to_all(value, axis, split_axis=0, concat_axis=0, tiled=True)]
    pallas_call x0 -> x1, Pallas kernels: none -> 17.2 us  [tiles(): pl.pallas_call(functools.partial(tiles_kernel, 1.0 / batch_rows), out_sha...]
  transfers between devices with their start and end apart: 95 -> 25, of which waited for: 33 -> 11; matrix products, arithmetic and copies ran while one was open for 1% -> 6% of each run, Pallas kernels for 0% -> 0%
where the time goes in v3:
time: 116 us
  starting transfers between devices  46 us (40%)
  blocking collectives  20.7 us (18%)
  waiting for transfers between devices  18.5 us (16%)
  Pallas kernels  17.2 us (15%)
  other arithmetic  5.1 us (4%)
  local copies, waits for them, and re-layouts  3.99 us (3%)
  matrix products  3.23 us (3%)
    ppermute x23, starting transfers between devices, shift(): lax.ppermute(value, axis, [(i, (i + steps) % count) for i in range(count)])  34.7 us
    all_to_all x1, blocking collectives, exchange(): return lax.all_to_all(value, axis, split_axis=0, concat_axis=0, tiled=True)  20.7 us
    ppermute x23, waiting for transfers between devices, shift(): lax.ppermute(value, axis, [(i, (i + steps) % count) for i in range(count)])  17.7 us
    pallas_call x1, Pallas kernels, tiles(): pl.pallas_call(functools.partial(tiles_kernel, 1.0 / batch_rows), out_sha...  17.2 us
    ppermute x1, starting transfers between devices, diagonal_shift(): return lax.ppermute(value, ('z', 'yl'), pairs)  7.49 us
    all_to_all x1, starting transfers between devices, exchange(): return lax.all_to_all(value, axis, split_axis=0, concat_axis=0, tiled=True)  3.78 us
    dot_general x2, matrix products, dot_head(): lax.dot_general(dproj_t, head, (((0,), (1,)), ((), ())), preferred_elemen...  3.23 us
  transfers between devices with their start and end apart: 25, of which 11 were waited for; matrix products, arithmetic and copies ran while one was open for 6% of the time, Pallas kernels for 0%

profile of v3, /device:TPU:1, one launch (start us, length us, event | category | flops | bytes accessed | tf_op | source)
XLA Modules:
  0.0 115.7 jit_solution(5486021145407396365)
XLA Ops:
  1.9 1.1 fusion.12
  3.0 7.5 %collective-permute-start.8 = (bf16[272,512]{1,0:T(8,128)(2,1)S(1)}, bf16[272,512]{1,0:T(8,128)(2,1)S(1)}, u32[]{:S(2)}, u32[]{:S(2)}) collective-permute-start(bf16[272,512]{1,0:T(8,128)(2,1)S(1)} %get-tuple-element.19.refs_5_), channel_id=1, source_target_pairs={{0,228},{4,224},{32,4},{36,0},{64,36},{68,32},{96,68},{100,64},{12... | collective-permute-start | bytes 835592 | tf_op jit(solution)/shard_map/ppermute | solution.py:225
  11.4 1.2 %collective-permute-start = (bf16[272,512]{1,0:T(8,128)(2,1)S(1)}, bf16[272,512]{1,0:T(8,128)(2,1)S(1)}, u32[]{:S(2)}, u32[]{:S(2)}) collective-permute-start(bf16[272,512]{1,0:T(8,128)(2,1)S(1)} %get-tuple-element.18.refs_0_), channel_id=1, source_target_pairs={{0,8},{8,16},{16,24},{24,32},{32,40},{40,48},{48,56},{56,64},{64,7... | collective-permute-start | bytes 835592 | tf_op jit(solution)/shard_map/ppermute | solution.py:21
  12.7 2.5 %collective-permute-start.1 = (bf16[272,512]{1,0:T(8,128)(2,1)S(1)}, bf16[272,512]{1,0:T(8,128)(2,1)S(1)}, u32[]{:S(2)}, u32[]{:S(2)}) collective-permute-start(bf16[272,512]{1,0:T(8,128)(2,1)S(1)} %get-tuple-element.18.refs_0_), channel_id=1, source_target_pairs={{0,16},{8,24},{16,32},{24,40},{32,48},{40,56},{48,64},{56,72},{64,... | collective-permute-start | bytes 835592 | tf_op jit(solution)/shard_map/ppermute | solution.py:21
  15.9 2.5 %collective-permute-start.2 = (bf16[272,512]{1,0:T(8,128)(2,1)S(1)}, bf16[272,512]{1,0:T(8,128)(2,1)S(1)}, u32[]{:S(2)}, u32[]{:S(2)}) collective-permute-start(bf16[272,512]{1,0:T(8,128)(2,1)S(1)} %get-tuple-element.18.refs_0_), channel_id=1, source_target_pairs={{0,24},{8,32},{16,40},{24,48},{32,56},{40,64},{48,72},{56,80},{64,... | collective-permute-start | bytes 835592 | tf_op jit(solution)/shard_map/ppermute | solution.py:21
  18.9 1.7 %collective-permute-start.3 = (bf16[272,512]{1,0:T(8,128)(2,1)S(1)}, bf16[272,512]{1,0:T(8,128)(2,1)S(1)}, u32[]{:S(2)}, u32[]{:S(2)}) collective-permute-start(bf16[272,512]{1,0:T(8,128)(2,1)S(1)} %get-tuple-element.18.refs_0_), channel_id=1, source_target_pairs={{0,32},{8,40},{16,48},{24,56},{32,64},{40,72},{48,80},{56,88},{64,... | collective-permute-start | bytes 835592 | tf_op jit(solution)/shard_map/ppermute | solution.py:21
  20.6 1.3 %collective-permute-done.7.refs_9_ = bf16[272,512]{1,0:T(8,128)(2,1)S(1)} collective-permute-done((bf16[272,512]{1,0:T(8,128)(2,1)S(1)}, bf16[272,512]{1,0:T(8,128)(2,1)S(1)}, u32[]{:S(2)}, u32[]{:S(2)}) %collective-permute-start.7) | collective-permute-done | bytes 278560 | tf_op jit(solution)/shard_map/ppermute | solution.py:21
  21.9 1.5 %collective-permute-start.5 = (bf16[272,512]{1,0:T(8,128)(2,1)S(1)}, bf16[272,512]{1,0:T(8,128)(2,1)S(1)}, u32[]{:S(2)}, u32[]{:S(2)}) collective-permute-start(bf16[272,512]{1,0:T(8,128)(2,1)S(1)} %get-tuple-element.19.refs_5_), channel_id=1, source_target_pairs={{0,2},{2,0},{1,3},{3,1},{4,6},{6,4},{5,7},{7,5},{8,10},{10,8},{9,1... | collective-permute-start | bytes 835592 | tf_op jit(solution)/shard_map/ppermute | solution.py:21
  23.4 4.7 %collective-permute-start.10 = (bf16[272,512]{1,0:T(8,128)(2,1)S(1)}, bf16[272,512]{1,0:T(8,128)(2,1)S(1)}, u32[]{:S(2)}, u32[]{:S(2)}) collective-permute-start(bf16[272,512]{1,0:T(8,128)(2,1)S(1)} %collective-permute-done.8.refs_10_), channel_id=1, source_target_pairs={{0,2},{2,0},{1,3},{3,1},{4,6},{6,4},{5,7},{7,5},{8,10},{10,8},{9,1... | collective-permute-start | bytes 835592 | tf_op jit(solution)/shard_map/ppermute | solution.py:21
  28.2 1.7 %collective-permute-start.6 = (bf16[272,512]{1,0:T(8,128)(2,1)S(1)}, bf16[272,512]{1,0:T(8,128)(2,1)S(1)}, u32[]{:S(2)}, u32[]{:S(2)}) collective-permute-start(bf16[272,512]{1,0:T(8,128)(2,1)S(1)} %collective-permute-done.4.refs_6_), channel_id=1, source_target_pairs={{0,2},{2,0},{1,3},{3,1},{4,6},{6,4},{5,7},{7,5},{8,10},{10,8},{9,1... | collective-permute-start | bytes 835592 | tf_op jit(solution)/shard_map/ppermute | solution.py:21
  32.5 17.2 %shard_map.93 = (bf16[512,256]{1,0:T(8,128)(2,1)}, bf16[512,256]{1,0:T(8,128)(2,1)}, bf16[512,256]{1,0:T(8,128)(2,1)}, bf16[512,256]{1,0:T(8,128)(2,1)}, bf16[51...) custom-call(s32[5]{0:T(128)} %stack.30.where_ref, ...), custom_call_target="tpu_custom_call" | custom-call | flops 12000000000 | bytes 9000000 | tf_op jit(solution)/shard_map/pallas_call | solution.py:174
  49.7 1.8 %collective-permute-start.11 = (bf16[512,512]{1,0:T(8,128)(2,1)}, bf16[512,512]{1,0:T(8,128)(2,1)S(1)}, u32[]{:S(2)}, u32[]{:S(2)}) collective-permute-start(bf16[512,512]{1,0:T(8,128)(2,1)} %get-tuple-element.21), channel_id=1, source_target_pairs={{0,2},{2,0},{1,3},{3,1},{4,6},{6,4},{5,7},{7,5},{8,10},{10,8},{9,1... | collective-permute-start | bytes 1572872 | tf_op jit(solution)/shard_map/ppermute | solution.py:21
  51.6 1.6 %collective-permute-done.11 = bf16[512,512]{1,0:T(8,128)(2,1)S(1)} collective-permute-done((bf16[512,512]{1,0:T(8,128)(2,1)}, bf16[512,512]{1,0:T(8,128)(2,1)S(1)}, u32[]{:S(2)}, u32[]{:S(2)}) %collective-permute-start.11) | collective-permute-done | bytes 524320 | tf_op jit(solution)/shard_map/ppermute | solution.py:21
  53.3 1.2 %add_convert_fusion.2 = bf16[512,512]{1,0:T(8,128)(2,1)S(1)} fusion(bf16[512,512]{1,0:T(8,128)(2,1)S(1)} %collective-permute-done.11, bf16[512,512]{1,0:T(8,128)(2,1)} %get-tuple-element.20), kind=kLoop, calls=%fused_computation.4 | loop fusion | flops 1048576 | bytes 1572864 | tf_op jit(solution)/shard_map/convert_element_type | solution.py:236
  54.5 20.7 %all_to_all.18 = bf16[8,64,512]{2,1,0:T(8,128)(2,1)S(1)} all-to-all(bf16[8,64,512]{2,1,0:T(8,128)(2,1)S(1)} %bitcast.15), channel_id=1, replica_groups=mesh['z'=8,'x'=4,'yl'=2,'c'=2,'rep'=2] {'x','yl'}, dimensions={0} | all-to-all | bytes 1048576 | tf_op jit(solution)/shard_map/all_to_all | solution.py:25
  75.3 1.3 %collective-permute-start.12 = (bf16[64,512]{1,0:T(8,128)(2,1)S(1)}, bf16[64,512]{1,0:T(8,128)(2,1)S(1)}, u32[]{:S(2)}, u32[]{:S(2)}) collective-permute-start(bf16[64,512]{1,0:T(8,128)(2,1)S(1)} %reduce_sum.12), channel_id=1, source_target_pairs={{0,32},{32,64},{64,96},{96,128},{128,160},{160,192},{192,224},{224... | collective-permute-start | bytes 196616 | tf_op jit(solution)/shard_map/ppermute | solution.py:21
  76.6 1.0 collective-permute-start.16
  77.6 1.4 %collective-permute-start.17 = (bf16[512,256]{1,0:T(8,128)(2,1)}, bf16[512,256]{1,0:T(8,128)(2,1)S(1)}, u32[]{:S(2)}, u32[]{:S(2)}) collective-permute-start(bf16[512,256]{1,0:T(8,128)(2,1)} %get-tuple-element.24), channel_id=1, source_target_pairs={{0,16},{8,24},{16,0},{24,8},{1,17},{9,25},{17,1},{25,9},{2,18},{10... | collective-permute-start | bytes 786440 | tf_op jit(solution)/shard_map/ppermute | solution.py:21
  79.0 1.4 %collective-permute-start.13 = (bf16[64,512]{1,0:T(8,128)(2,1)S(1)}, bf16[64,512]{1,0:T(8,128)(2,1)S(1)}, u32[]{:S(2)}, u32[]{:S(2)}) collective-permute-start(bf16[64,512]{1,0:T(8,128)(2,1)S(1)} %reduce_sum.12), channel_id=1, source_target_pairs={{0,224},{32,0},{64,32},{96,64},{128,96},{160,128},{192,160},{224,1... | collective-permute-start | bytes 196616 | tf_op jit(solution)/shard_map/ppermute | solution.py:21
  81.2 1.2 %collective-permute-done.13 = bf16[64,512]{1,0:T(8,128)(2,1)S(1)} collective-permute-done((bf16[64,512]{1,0:T(8,128)(2,1)S(1)}, bf16[64,512]{1,0:T(8,128)(2,1)S(1)}, u32[]{:S(2)}, u32[]{:S(2)}) %collective-permute-start.13) | collective-permute-done | bytes 65568 | tf_op jit(solution)/shard_map/ppermute | solution.py:21
  82.4 1.2 %collective-permute-start.21 = (bf16[2,512,256]{2,1,0:T(8,128)(2,1)S(1)}, bf16[2,512,256]{2,1,0:T(8,128)(2,1)S(1)}, u32[]{:S(2)}, u32[]{:S(2)}) collective-permute-start(bf16[2,512,256]{2,1,0:T(8,128)(2,1)S(1)} %slice.17), channel_id=1, source_target_pairs={{0,4},{4,0},{1,5},{5,1},{2,6},{6,2},{3,7},{7,3},{8,12},{12,8},{9,1... | collective-permute-start | bytes 1572872 | tf_op jit(solution)/shard_map/ppermute | solution.py:21
  83.6 1.7 %collective-permute-done.14 = bf16[64,512]{1,0:T(8,128)(2,1)S(1)} collective-permute-done((bf16[64,512]{1,0:T(8,128)(2,1)S(1)}, bf16[64,512]{1,0:T(8,128)(2,1)S(1)}, u32[]{:S(2)}, u32[]{:S(2)}) %collective-permute-start.14) | collective-permute-done | bytes 65568 | tf_op jit(solution)/shard_map/ppermute | solution.py:21
  85.3 2.2 %collective-permute-start.15 = (bf16[64,512]{1,0:T(8,128)(2,1)S(1)}, bf16[64,512]{1,0:T(8,128)(2,1)S(1)}, u32[]{:S(2)}, u32[]{:S(2)}) collective-permute-start(bf16[64,512]{1,0:T(8,128)(2,1)S(1)} %add_convert_fusion.4), channel_id=1, source_target_pairs={{0,128},{32,160},{64,192},{96,224},{128,0},{160,32},{192,64},{224,... | collective-permute-start | bytes 196616 | tf_op jit(solution)/shard_map/ppermute | solution.py:21
  87.5 5.0 %collective-permute-done.18 = bf16[512,256]{1,0:T(8,128)(2,1)S(1)} collective-permute-done((bf16[512,256]{1,0:T(8,128)(2,1)}, bf16[512,256]{1,0:T(8,128)(2,1)S(1)}, u32[]{:S(2)}, u32[]{:S(2)}) %collective-permute-start.18) | collective-permute-done | bytes 262176 | tf_op jit(solution)/shard_map/ppermute | solution.py:21
  93.5 1.4 %collective-permute-start.19 = (bf16[512,256]{1,0:T(8,128)(2,1)}, bf16[512,256]{1,0:T(8,128)(2,1)}, u32[]{:S(2)}, u32[]{:S(2)}) collective-permute-start(bf16[512,256]{1,0:T(8,128)(2,1)} %fusion.10), channel_id=1, source_target_pairs={{0,224},{32,0},{64,32},{96,64},{128,96},{160,128},{192,160},{224,1... | collective-permute-start | bytes 786440 | tf_op jit(solution)/shard_map/ppermute | solution.py:21
  95.8 3.8 %all-to-all-start.1 = ((bf16[8,64,512]{2,1,0:T(8,128)(2,1)}), bf16[8,64,512]{2,1,0:T(8,128)(2,1)S(1)}, u32[]{:S(2)}, u32[]{:S(2)}) async-start(bf16[8,64,512]{2,1,0:T(8,128)(2,1)} %broadcast_in_dim.16), calls=%async_computation.1 | async-start | bytes 1048576 | tf_op jit(solution)/shard_map/all_to_all | solution.py:25
  100.8 2.2 %convolution_convert_fusion.1 = bf16[256,512]{1,0:T(8,128)(2,1)} fusion(bf16[512,512]{1,0:T(8,128)(2,1)S(1)} %copy-done.9, bf16[512,256]{1,0:T(8,128)(2,1)S(1)} %collective-permute-done.16, bf16[512,256]{1,0:T(8,128)(2,1)S(1)} %copy-done.6, bf16[512,256]{1,0:T(8,128)(2,1)S(1)} %copy-done.8, bf16[512,256]{1,0:T(8,128)(2,1)} %collective-permute-done.19, ...), kind=kOutput, calls=%fused_computation.2 | convolution fusion | flops 136052736 | bytes 2097155 | tf_op jit(solution)/shard_map/dot_general | solution.py:245
  103.0 3.3 %collective-permute-done.22 = bf16[512,256]{1,0:T(8,128)(2,1)S(1)} collective-permute-done((bf16[512,256]{1,0:T(8,128)(2,1)S(1)}, bf16[512,256]{1,0:T(8,128)(2,1)S(1)}, u32[]{:S(2)}, u32[]{:S(2)}) %collective-permute-start.22) | collective-permute-done | bytes 262176 | tf_op jit(solution)/shard_map/ppermute | solution.py:21
  106.3 1.1 convolution_convert_fusion
  107.3 5.3 %collective-permute-start.23 = (bf16[512,512]{1,0:T(8,128)(2,1)S(1)}, bf16[512,512]{1,0:T(8,128)(2,1)S(1)}, u32[]{:S(2)}, u32[]{:S(2)}) collective-permute-start(bf16[512,512]{1,0:T(8,128)(2,1)S(1)} %bitcast.16), channel_id=1, source_target_pairs={{0,2},{2,0},{1,3},{3,1},{4,6},{6,4},{5,7},{7,5},{8,10},{10,8},{9,1... | collective-permute-start | bytes 1572872 | tf_op jit(solution)/shard_map/ppermute | solution.py:21
  112.7 1.5 %collective-permute-done.23 = bf16[512,512]{1,0:T(8,128)(2,1)S(1)} collective-permute-done((bf16[512,512]{1,0:T(8,128)(2,1)S(1)}, bf16[512,512]{1,0:T(8,128)(2,1)S(1)}, u32[]{:S(2)}, u32[]{:S(2)}) %collective-permute-start.23) | collective-permute-done | bytes 524320 | tf_op jit(solution)/shard_map/ppermute | solution.py:21
  114.2 1.5 %select_convert_fusion = (f32[512,512]{1,0:T(8,128)}, f32[512,512]{1,0:T(8,128)}) fusion(bf16[512,512]{1,0:T(8,128)(2,1)S(1)} %collective-permute-done.23, bf16[512,512]{1,0:T(8,128)(2,1)S(1)} %bitcast.17, pred[]{:T(512)S(6)} %eq.12), kind=kLoop, calls=%fused_computation.25 | loop fusion | flops 1048576 | bytes 3145729 | tf_op jit(solution)/shard_map/convert_element_type | solution.py:294
  (79 shorter events, 10.1 us)
Async XLA Ops:
  3.0 28.5 %copy-start.2 = (bf16[272,512]{1,0:T(8,128)(2,1)}, bf16[272,512]{1,0:T(8,128)(2,1)S(1)}, u32[]{:S(2)}) copy-start(bf16[272,512]{1,0:T(8,128)(2,1)S(1)} %get-tuple-element.18.refs_0_) | copy-start | bytes 835588
  3.0 28.5 %copy-start.3 = (bf16[272,512]{1,0:T(8,128)(2,1)}, bf16[272,512]{1,0:T(8,128)(2,1)S(1)}, u32[]{:S(2)}) copy-start(bf16[272,512]{1,0:T(8,128)(2,1)S(1)} %get-tuple-element.19.refs_5_) | copy-start | bytes 835588
  3.0 12.9 %collective-permute-start.8 = (bf16[272,512]{1,0:T(8,128)(2,1)S(1)}, bf16[272,512]{1,0:T(8,128)(2,1)S(1)}, u32[]{:S(2)}, u32[]{:S(2)}) collective-permute-start(bf16[272,512]{1,0:T(8,128)(2,1)S(1)} %get-tuple-element.19.refs_5_), channel_id=1, source_target_pairs={{0,228},{4,224},{32,4},{36,0},{64,36},{68,32},{96,68},{100,64},{12... | collective-permute-start | bytes 835592 | tf_op jit(solution)/shard_map/ppermute | solution.py:225
  10.5 8.3 %collective-permute-start.4 = (bf16[272,512]{1,0:T(8,128)(2,1)S(1)}, bf16[272,512]{1,0:T(8,128)(2,1)S(1)}, u32[]{:S(2)}, u32[]{:S(2)}) collective-permute-start(bf16[272,512]{1,0:T(8,128)(2,1)S(1)} %get-tuple-element.19.refs_5_), channel_id=1, source_target_pairs={{0,4},{4,0},{1,5},{5,1},{2,6},{6,2},{3,7},{7,3},{8,12},{12,8},{9,1... | collective-permute-start | bytes 835592 | tf_op jit(solution)/shard_map/ppermute | solution.py:21
  10.7 11.2 %collective-permute-start.7 = (bf16[272,512]{1,0:T(8,128)(2,1)S(1)}, bf16[272,512]{1,0:T(8,128)(2,1)S(1)}, u32[]{:S(2)}, u32[]{:S(2)}) collective-permute-start(bf16[272,512]{1,0:T(8,128)(2,1)S(1)} %get-tuple-element.19.refs_5_), channel_id=1, source_target_pairs={{0,224},{32,0},{64,32},{96,64},{128,96},{160,128},{192,160},{224,1... | collective-permute-start | bytes 835592 | tf_op jit(solution)/shard_map/ppermute | solution.py:21
  11.4 12.0 %collective-permute-start = (bf16[272,512]{1,0:T(8,128)(2,1)S(1)}, bf16[272,512]{1,0:T(8,128)(2,1)S(1)}, u32[]{:S(2)}, u32[]{:S(2)}) collective-permute-start(bf16[272,512]{1,0:T(8,128)(2,1)S(1)} %get-tuple-element.18.refs_0_), channel_id=1, source_target_pairs={{0,8},{8,16},{16,24},{24,32},{32,40},{40,48},{48,56},{56,64},{64,7... | collective-permute-start | bytes 835592 | tf_op jit(solution)/shard_map/ppermute | solution.py:21
  12.7 15.5 %collective-permute-start.1 = (bf16[272,512]{1,0:T(8,128)(2,1)S(1)}, bf16[272,512]{1,0:T(8,128)(2,1)S(1)}, u32[]{:S(2)}, u32[]{:S(2)}) collective-permute-start(bf16[272,512]{1,0:T(8,128)(2,1)S(1)} %get-tuple-element.18.refs_0_), channel_id=1, source_target_pairs={{0,16},{8,24},{16,32},{24,40},{32,48},{40,56},{48,64},{56,72},{64,... | collective-permute-start | bytes 835592 | tf_op jit(solution)/shard_map/ppermute | solution.py:21
  15.9 15.7 %copy-start.10 = (bf16[272,512]{1,0:T(8,128)(2,1)}, bf16[272,512]{1,0:T(8,128)(2,1)S(1)}, u32[]{:S(2)}) copy-start(bf16[272,512]{1,0:T(8,128)(2,1)S(1)} %collective-permute-done.8.refs_10_) | copy-start | bytes 835588
  15.9 13.9 %collective-permute-start.2 = (bf16[272,512]{1,0:T(8,128)(2,1)S(1)}, bf16[272,512]{1,0:T(8,128)(2,1)S(1)}, u32[]{:S(2)}, u32[]{:S(2)}) collective-permute-start(bf16[272,512]{1,0:T(8,128)(2,1)S(1)} %get-tuple-element.18.refs_0_), channel_id=1, source_target_pairs={{0,24},{8,32},{16,40},{24,48},{32,56},{40,64},{48,72},{56,80},{64,... | collective-permute-start | bytes 835592 | tf_op jit(solution)/shard_map/ppermute | solution.py:21
  18.9 12.7 %copy-start.11 = (bf16[272,512]{1,0:T(8,128)(2,1)}, bf16[272,512]{1,0:T(8,128)(2,1)S(1)}, u32[]{:S(2)}) copy-start(bf16[272,512]{1,0:T(8,128)(2,1)S(1)} %collective-permute-done.4.refs_6_) | copy-start | bytes 835588
  18.9 12.6 %collective-permute-start.3 = (bf16[272,512]{1,0:T(8,128)(2,1)S(1)}, bf16[272,512]{1,0:T(8,128)(2,1)S(1)}, u32[]{:S(2)}, u32[]{:S(2)}) collective-permute-start(bf16[272,512]{1,0:T(8,128)(2,1)S(1)} %get-tuple-element.18.refs_0_), channel_id=1, source_target_pairs={{0,32},{8,40},{16,48},{24,56},{32,64},{40,72},{48,80},{56,88},{64,... | collective-permute-start | bytes 835592 | tf_op jit(solution)/shard_map/ppermute | solution.py:21
  21.9 9.7 %copy-start.12 = (bf16[272,512]{1,0:T(8,128)(2,1)}, bf16[272,512]{1,0:T(8,128)(2,1)S(1)}, u32[]{:S(2)}) copy-start(bf16[272,512]{1,0:T(8,128)(2,1)S(1)} %collective-permute-done.7.refs_9_) | copy-start | bytes 835588
  21.9 9.6 %collective-permute-start.5 = (bf16[272,512]{1,0:T(8,128)(2,1)S(1)}, bf16[272,512]{1,0:T(8,128)(2,1)S(1)}, u32[]{:S(2)}, u32[]{:S(2)}) collective-permute-start(bf16[272,512]{1,0:T(8,128)(2,1)S(1)} %get-tuple-element.19.refs_5_), channel_id=1, source_target_pairs={{0,2},{2,0},{1,3},{3,1},{4,6},{6,4},{5,7},{7,5},{8,10},{10,8},{9,1... | collective-permute-start | bytes 835592 | tf_op jit(solution)/shard_map/ppermute | solution.py:21
  23.4 8.1 %collective-permute-start.10 = (bf16[272,512]{1,0:T(8,128)(2,1)S(1)}, bf16[272,512]{1,0:T(8,128)(2,1)S(1)}, u32[]{:S(2)}, u32[]{:S(2)}) collective-permute-start(bf16[272,512]{1,0:T(8,128)(2,1)S(1)} %collective-permute-done.8.refs_10_), channel_id=1, source_target_pairs={{0,2},{2,0},{1,3},{3,1},{4,6},{6,4},{5,7},{7,5},{8,10},{10,8},{9,1... | collective-permute-start | bytes 835592 | tf_op jit(solution)/shard_map/ppermute | solution.py:21
  28.2 3.4 %collective-permute-start.6 = (bf16[272,512]{1,0:T(8,128)(2,1)S(1)}, bf16[272,512]{1,0:T(8,128)(2,1)S(1)}, u32[]{:S(2)}, u32[]{:S(2)}) collective-permute-start(bf16[272,512]{1,0:T(8,128)(2,1)S(1)} %collective-permute-done.4.refs_6_), channel_id=1, source_target_pairs={{0,2},{2,0},{1,3},{3,1},{4,6},{6,4},{5,7},{7,5},{8,10},{10,8},{9,1... | collective-permute-start | bytes 835592 | tf_op jit(solution)/shard_map/ppermute | solution.py:21
  29.8 1.7 %collective-permute-start.9 = (bf16[272,512]{1,0:T(8,128)(2,1)S(1)}, bf16[272,512]{1,0:T(8,128)(2,1)}, u32[]{:S(2)}, u32[]{:S(2)}) collective-permute-start(bf16[272,512]{1,0:T(8,128)(2,1)S(1)} %collective-permute-done.7.refs_9_), channel_id=1, source_target_pairs={{0,2},{2,0},{1,3},{3,1},{4,6},{6,4},{5,7},{7,5},{8,10},{10,8},{9,1... | collective-permute-start | bytes 835592 | tf_op jit(solution)/shard_map/ppermute | solution.py:21
  49.7 3.6 %collective-permute-start.11 = (bf16[512,512]{1,0:T(8,128)(2,1)}, bf16[512,512]{1,0:T(8,128)(2,1)S(1)}, u32[]{:S(2)}, u32[]{:S(2)}) collective-permute-start(bf16[512,512]{1,0:T(8,128)(2,1)} %get-tuple-element.21), channel_id=1, source_target_pairs={{0,2},{2,0},{1,3},{3,1},{4,6},{6,4},{5,7},{7,5},{8,10},{10,8},{9,1... | collective-permute-start | bytes 1572872 | tf_op jit(solution)/shard_map/ppermute | solution.py:21
  51.5 27.4 %collective-permute-start.20 = (bf16[4,512,256]{2,1,0:T(8,128)(2,1)}, bf16[4,512,256]{2,1,0:T(8,128)(2,1)S(1)}, u32[]{:S(2)}, u32[]{:S(2)}) collective-permute-start(bf16[4,512,256]{2,1,0:T(8,128)(2,1)} %get-tuple-element.28), channel_id=1, source_target_pairs={{0,2},{2,0},{1,3},{3,1},{4,6},{6,4},{5,7},{7,5},{8,10},{10,8},{9,1... | collective-permute-start | bytes 3145736 | tf_op jit(solution)/shard_map/ppermute | solution.py:21
  54.5 26.4 %copy-start = (bf16[4,512,256]{2,1,0:T(8,128)(2,1)S(1)}, bf16[4,512,256]{2,1,0:T(8,128)(2,1)}, u32[]{:S(2)}) copy-start(bf16[4,512,256]{2,1,0:T(8,128)(2,1)} %get-tuple-element.27) | copy-start | bytes 3145732
  75.3 5.1 %collective-permute-start.12 = (bf16[64,512]{1,0:T(8,128)(2,1)S(1)}, bf16[64,512]{1,0:T(8,128)(2,1)S(1)}, u32[]{:S(2)}, u32[]{:S(2)}) collective-permute-start(bf16[64,512]{1,0:T(8,128)(2,1)S(1)} %reduce_sum.12), channel_id=1, source_target_pairs={{0,32},{32,64},{64,96},{96,128},{128,160},{160,192},{192,224},{224... | collective-permute-start | bytes 196616 | tf_op jit(solution)/shard_map/ppermute | solution.py:21
  76.6 10.9 %collective-permute-start.16 = (bf16[512,256]{1,0:T(8,128)(2,1)}, bf16[512,256]{1,0:T(8,128)(2,1)S(1)}, u32[]{:S(2)}, u32[]{:S(2)}) collective-permute-start(bf16[512,256]{1,0:T(8,128)(2,1)} %get-tuple-element.23), channel_id=1, source_target_pairs={{0,24},{8,0},{16,8},{24,16},{1,25},{9,1},{17,9},{25,17},{2,26},{10... | collective-permute-start | bytes 786440 | tf_op jit(solution)/shard_map/ppermute | solution.py:21
  77.6 9.9 %collective-permute-start.17 = (bf16[512,256]{1,0:T(8,128)(2,1)}, bf16[512,256]{1,0:T(8,128)(2,1)S(1)}, u32[]{:S(2)}, u32[]{:S(2)}) collective-permute-start(bf16[512,256]{1,0:T(8,128)(2,1)} %get-tuple-element.24), channel_id=1, source_target_pairs={{0,16},{8,24},{16,0},{24,8},{1,17},{9,25},{17,1},{25,9},{2,18},{10... | collective-permute-start | bytes 786440 | tf_op jit(solution)/shard_map/ppermute | solution.py:21
  79.0 13.6 %collective-permute-start.18 = (bf16[512,256]{1,0:T(8,128)(2,1)}, bf16[512,256]{1,0:T(8,128)(2,1)S(1)}, u32[]{:S(2)}, u32[]{:S(2)}) collective-permute-start(bf16[512,256]{1,0:T(8,128)(2,1)} %get-tuple-element.25), channel_id=1, source_target_pairs={{0,8},{8,16},{16,24},{24,0},{1,9},{9,17},{17,25},{25,1},{2,10},{10... | collective-permute-start | bytes 786440 | tf_op jit(solution)/shard_map/ppermute | solution.py:21
  79.0 3.4 %collective-permute-start.13 = (bf16[64,512]{1,0:T(8,128)(2,1)S(1)}, bf16[64,512]{1,0:T(8,128)(2,1)S(1)}, u32[]{:S(2)}, u32[]{:S(2)}) collective-permute-start(bf16[64,512]{1,0:T(8,128)(2,1)S(1)} %reduce_sum.12), channel_id=1, source_target_pairs={{0,224},{32,0},{64,32},{96,64},{128,96},{160,128},{192,160},{224,1... | collective-permute-start | bytes 196616 | tf_op jit(solution)/shard_map/ppermute | solution.py:21
  80.4 4.9 %collective-permute-start.14 = (bf16[64,512]{1,0:T(8,128)(2,1)S(1)}, bf16[64,512]{1,0:T(8,128)(2,1)S(1)}, u32[]{:S(2)}, u32[]{:S(2)}) collective-permute-start(bf16[64,512]{1,0:T(8,128)(2,1)S(1)} %reduce_sum.12), channel_id=1, source_target_pairs={{0,192},{32,224},{64,0},{96,32},{128,64},{160,96},{192,128},{224,1... | collective-permute-start | bytes 196616 | tf_op jit(solution)/shard_map/ppermute | solution.py:21
  81.1 11.4 %copy-start.4 = (bf16[512,256]{1,0:T(8,128)(2,1)S(1)}, bf16[512,256]{1,0:T(8,128)(2,1)}, u32[]{:S(2)}) copy-start(bf16[512,256]{1,0:T(8,128)(2,1)} %get-tuple-element.26) | copy-start | bytes 786436
  82.4 17.2 %collective-permute-start.21 = (bf16[2,512,256]{2,1,0:T(8,128)(2,1)S(1)}, bf16[2,512,256]{2,1,0:T(8,128)(2,1)S(1)}, u32[]{:S(2)}, u32[]{:S(2)}) collective-permute-start(bf16[2,512,256]{2,1,0:T(8,128)(2,1)S(1)} %slice.17), channel_id=1, source_target_pairs={{0,4},{4,0},{1,5},{5,1},{2,6},{6,2},{3,7},{7,3},{8,12},{12,8},{9,1... | collective-permute-start | bytes 1572872 | tf_op jit(solution)/shard_map/ppermute | solution.py:21
  85.3 9.6 %collective-permute-start.15 = (bf16[64,512]{1,0:T(8,128)(2,1)S(1)}, bf16[64,512]{1,0:T(8,128)(2,1)S(1)}, u32[]{:S(2)}, u32[]{:S(2)}) collective-permute-start(bf16[64,512]{1,0:T(8,128)(2,1)S(1)} %add_convert_fusion.4), channel_id=1, source_target_pairs={{0,128},{32,160},{64,192},{96,224},{128,0},{160,32},{192,64},{224,... | collective-permute-start | bytes 196616 | tf_op jit(solution)/shard_map/ppermute | solution.py:21
  93.5 7.1 %collective-permute-start.19 = (bf16[512,256]{1,0:T(8,128)(2,1)}, bf16[512,256]{1,0:T(8,128)(2,1)}, u32[]{:S(2)}, u32[]{:S(2)}) collective-permute-start(bf16[512,256]{1,0:T(8,128)(2,1)} %fusion.10), channel_id=1, source_target_pairs={{0,224},{32,0},{64,32},{96,64},{128,96},{160,128},{192,160},{224,1... | collective-permute-start | bytes 786440 | tf_op jit(solution)/shard_map/ppermute | solution.py:21
  95.8 11.6 %all-to-all-start.1 = ((bf16[8,64,512]{2,1,0:T(8,128)(2,1)}), bf16[8,64,512]{2,1,0:T(8,128)(2,1)S(1)}, u32[]{:S(2)}, u32[]{:S(2)}) async-start(bf16[8,64,512]{2,1,0:T(8,128)(2,1)} %broadcast_in_dim.16), calls=%async_computation.1 | async-start | bytes 1048576 | tf_op jit(solution)/shard_map/all_to_all | solution.py:25
  99.8 6.5 %collective-permute-start.22 = (bf16[512,256]{1,0:T(8,128)(2,1)S(1)}, bf16[512,256]{1,0:T(8,128)(2,1)S(1)}, u32[]{:S(2)}, u32[]{:S(2)}) collective-permute-start(bf16[512,256]{1,0:T(8,128)(2,1)S(1)} %slice_bitcast_fusion), channel_id=1, source_target_pairs={{0,32},{32,64},{64,96},{96,128},{128,160},{160,192},{192,224},{224... | collective-permute-start | bytes 786440 | tf_op jit(solution)/shard_map/ppermute | solution.py:21
  107.3 6.9 %collective-permute-start.23 = (bf16[512,512]{1,0:T(8,128)(2,1)S(1)}, bf16[512,512]{1,0:T(8,128)(2,1)S(1)}, u32[]{:S(2)}, u32[]{:S(2)}) collective-permute-start(bf16[512,512]{1,0:T(8,128)(2,1)S(1)} %bitcast.16), channel_id=1, source_target_pairs={{0,2},{2,0},{1,3},{3,1},{4,6},{6,4},{5,7},{7,5},{8,10},{10,8},{9,1... | collective-permute-start | bytes 1572872 | tf_op jit(solution)/shard_map/ppermute | solution.py:21
  (14 other events, 36.5 us)

commit v4 on v3

--- a/solution.py
+++ b/solution.py
@@ -33,7 +33,7 @@
     return lax.dot_general(a, b, (((1,), (1,)), ((), ())), preferred_element_type=F32)
 
 
-def tiles_kernel(inv_rows, where_ref, *refs):
+def tiles_kernel(inv_rows, *refs):
     audio_hbm = refs[:5]
     text_hbm = refs[5:13]
     ha_hbm, ht_hbm = refs[13:15]
@@ -43,7 +43,9 @@
     (da, dt, keep, give, in_sem, out_sem) = refs[41:]
     width = ha.shape[0]
     rows = ae.shape[0] // 5
-    core = where_ref[4]
+    core = lax.axis_index("c")
+    high = lax.axis_index("yl")
+    first_met = (0, high, core, high)
 
     def span(first, count=1):
         return slice(first * rows, (first + count) * rows)
@@ -55,12 +57,11 @@
         ]
 
     copies = [(ha_hbm, ha), (ht_hbm, ht)]
-    copies += fetch(audio_hbm[0], ae, al, 0)
+    for i in range(5):
+        copies += fetch(audio_hbm[i], ae, al, i)
     for j in range(4):
         for plane in range(2):
             copies += fetch(text_hbm[4 * plane + j], te, tl, 2 * j + plane)
-    for i in range(1, 5):
-        copies += fetch(audio_hbm[i], ae, al, i)
     copies = [pltpu.make_async_copy(s, d, in_sem.at[i]) for i, (s, d) in enumerate(copies)]
     for c in copies:
         c.start()
@@ -98,7 +99,7 @@
 
     def tile(j):
         cols = span(2 * j, 2)
-        at = pl.ds(pl.multiple_of(where_ref[j] * rows, rows), 4 * rows) if j else span(0, 4)
+        at = pl.ds(pl.multiple_of(first_met[j] * rows, rows), 4 * rows) if j else span(0, 4)
         z = zt[:, cols]
         e = jnp.exp2(dot_nn(za[at, :], z) * (logit_scale * log2_e))
         row_scale = ea[at, :]
@@ -115,35 +116,36 @@
             ga[:, at] += dot_nt(z, w)
         gt[:, cols] = dot_nn(zat[:, at], w)
 
-    for c in copies[2:4]:
-        c.wait()
-    audio_block(0)
-    for c in copies[4:20]:
-        c.wait()
-    for j in range(4):
-        text_chunk(j)
-    for c in copies[20:]:
-        c.wait()
-    for i in range(1, 5):
-        audio_block(i)
-    for j in range(4):
-        tile(j)
-
     def finish(g_ref, u_ref, n_ref, d_ref, cols):
         g = g_ref[:, cols]
         u = u_ref[:, cols]
         along = jnp.sum(u * g, axis=0, keepdims=True)
         d_ref[:, cols] = ((g - u * along) * (n_ref[0:1, cols] * logit_scale)).astype(BF)
 
+    def send(pairs, first):
+        sent = [pltpu.make_async_copy(s, d, out_sem.at[first + i]) for i, (s, d) in enumerate(pairs)]
+        for c in sent:
+            c.start()
+        return sent
+
+    for c in copies[2:12]:
+        c.wait()
+    for i in range(5):
+        audio_block(i)
+    for c in copies[12:]:
+        c.wait()
+    outs = []
     for j in range(4):
+        text_chunk(j)
+    for j in range(4):
+        tile(j)
         finish(gt, ut, nt, dt, span(2 * j, 2))
+        blocks = (2 * j, 2 * j + 1)
+        to = mine_hbm if j < 2 else send_hbm
+        outs += send([(dt.at[:, span(b)], to.at[b % 4]) for b in blocks], 2 * j)
     for i in range(5):
         finish(ga, ua, na, da, span(i))
-    outs = [(dt.at[:, span(b)], (mine_hbm if b < 4 else send_hbm).at[b % 4]) for b in range(8)]
-    outs += [(da.at[:, span(i)], da_hbm[i]) for i in range(5)]
-    outs = [pltpu.make_async_copy(s, d, out_sem.at[i]) for i, (s, d) in enumerate(outs)]
-    for c in outs:
-        c.start()
+    outs += send([(da.at[:, span(i)], da_hbm[i]) for i in range(5)], 8)
     head_t = (dot_nn(dt[...], te[...]) * inv_rows).astype(BF).T
     head_a = (dot_nn(da[...], ae[...]) * inv_rows).astype(BF).T
 
@@ -157,15 +159,12 @@
         keep[...] = head_t
         give[...] = head_a
 
-    last = [(give, give_hbm), (keep, keep_hbm)]
-    last = [pltpu.make_async_copy(s, d, out_sem.at[13 + i]) for i, (s, d) in enumerate(last)]
-    for c in last:
-        c.start()
-    for c in outs + last:
+    outs += send([(give, give_hbm), (keep, keep_hbm)], 13)
+    for c in outs:
         c.wait()
 
 
-def tiles(where, audio, text, audio_head, text_head, batch_rows):
+def tiles(audio, text, audio_head, text_head, batch_rows):
     rows, width = audio[0].shape[0] - PAD, audio[0].shape[1]
     lanes = min(128, rows)
     anywhere = pl.BlockSpec(memory_space=pl.ANY)
@@ -180,7 +179,7 @@
             shape((width, width), BF),
             shape((width, width), BF),
         ),
-        in_specs=[pl.BlockSpec(memory_space=pltpu.SMEM)] + [anywhere] * 15,
+        in_specs=[anywhere] * 15,
         out_specs=(anywhere,) * 9,
         scratch_shapes=[
             vmem((5 * rows, width), BF),
@@ -211,7 +210,7 @@
         cost_estimate=pl.CostEstimate(
             flops=12_000_000_000, bytes_accessed=9_000_000, transcendentals=2_100_000
         ),
-    )(where, *audio, *text, audio_head, text_head)
+    )(*audio, *text, audio_head, text_head)
 
 
 def packed(embed, lse):
@@ -257,16 +256,21 @@
 
     lse = jnp.stack([audio_lse, text_lse])
     a_own, t_own = together((packed(audio_embed, lse[:1]), packed(text_embed, lse[1:])))
-    audio = [a_own] + [shift(a_own, line, s) for s in (1, 2, 3, 4)]
-    here = [t_own, shift(t_own, "yl", 1)]
-    ahead = [shift(t_own, "z", -1), diagonal_shift(t_own, -1)]
-    here += [shift(v, "c", 1) for v in here]
-    ahead += [shift(v, "c", 1) for v in ahead]
-
-    behind_y, behind_c = (yl == 1).astype(jnp.int32), (core == 1).astype(jnp.int32)
-    where = jnp.stack([jnp.zeros_like(core), behind_y, behind_c, behind_y, core])
+    a_4 = shift(a_own, line, 4)
+    a_1 = shift(a_own, line, 1)
+    t_y = shift(t_own, "yl", 1)
+    t_next = shift(t_own, "z", -1)
+    t_next_y = diagonal_shift(t_own, -1)
+    t_c = shift(t_own, "c", 1)
+    a_2 = shift(jnp.where(x + 2 < 4, a_own, a_4), "x", 2)
+    a_3 = shift(jnp.where(x + 3 < 4, a_own, a_4), "x", 3)
+    t_y, t_next, t_next_y, a_2, a_3 = together((t_y, t_next, t_next_y, a_2, a_3))
+    audio = [a_own, a_1, a_2, a_3, a_4]
+    here = [t_own, t_y, t_c, shift(t_y, "c", 1)]
+    ahead = [t_next, t_next_y, shift(t_next, "c", 1), shift(t_next_y, "c", 1)]
+
     *da, dt_mine, dt_send, keep, give = tiles(
-        where, audio, here + ahead, audio_head, text_head, rows * blocks
+        audio, here + ahead, audio_head, text_head, rows * blocks
     )
 
     head = added(keep, shift(give, "c", 1))
@@ -280,8 +284,9 @@
         past = x + s >= 4
         here_sum = here_sum + jnp.where(past, 0.0, part.astype(F32))
         behind_sum = behind_sum + jnp.where(past, part.astype(F32), 0.0)
+    behind_sum = behind_sum.astype(BF)
     dt_ahead = shift(dt_pair[1], "z", 1)
-    da_ahead = shift(behind_sum.astype(BF), "z", -1)
+    da_ahead = shift(behind_sum, "z", -1)
     head = summed(head.reshape(8, width // 8, width)).astype(BF)
     head = added(head, *[shift(head, "z", s) for s in (1, -1, -2)])
     far = shift(head, "z", 4)

time: 116 us -> 109 us (0.940)
  blocking collectives: 20.7 us -> 11.9 us
  waiting for transfers between devices: 18.5 us -> 26.7 us
  starting transfers between devices: 46 us -> 41.6 us
    ppermute x23, waiting for transfers between devices: 17.7 us -> 26.7 us  [shift(): lax.ppermute(value, axis, [(i, (i + steps) % count) for i in range(count)])]
    all_to_all x1, blocking collectives: 20.7 us -> 11.9 us  [exchange(): return lax.all_to_all(value, axis, split_axis=0, concat_axis=0, tiled=True)]
    ppermute x1, starting transfers between devices: 7.49 us -> 5.04 us  [diagonal_shift(): return lax.ppermute(value, ('z', 'yl'), pairs)]
    ppermute x23, starting transfers between devices: 34.7 us -> 32.8 us  [shift(): lax.ppermute(value, axis, [(i, (i + steps) % count) for i in range(count)])]
  transfers between devices with their start and end apart: 25 -> 25, of which waited for: 11 -> 14; matrix products, arithmetic and copies ran while one was open for 6% -> 6% of each run, Pallas kernels for 0% -> 0%
where the time goes in v4:
time: 109 us
  starting transfers between devices  41.6 us (38%)
  waiting for transfers between devices  26.7 us (24%)
  Pallas kernels  16.1 us (15%)
  blocking collectives  11.9 us (11%)
  other arithmetic  5.13 us (5%)
  local copies, waits for them, and re-layouts  3.25 us (3%)
  matrix products  3.22 us (3%)
    ppermute x23, starting transfers between devices, shift(): lax.ppermute(value, axis, [(i, (i + steps) % count) for i in range(count)])  32.8 us
    ppermute x23, waiting for transfers between devices, shift(): lax.ppermute(value, axis, [(i, (i + steps) % count) for i in range(count)])  26.7 us
    pallas_call x1, Pallas kernels, tiles(): pl.pallas_call(functools.partial(tiles_kernel, 1.0 / batch_rows), out_sha...  16.1 us
    all_to_all x1, blocking collectives, exchange(): return lax.all_to_all(value, axis, split_axis=0, concat_axis=0, tiled=True)  11.9 us
    ppermute x1, starting transfers between devices, diagonal_shift(): return lax.ppermute(value, ('z', 'yl'), pairs)  5.04 us
    all_to_all x1, starting transfers between devices, exchange(): return lax.all_to_all(value, axis, split_axis=0, concat_axis=0, tiled=True)  3.78 us
    dot_general x2, matrix products, dot_head(): lax.dot_general(dproj_t, head, (((0,), (1,)), ((), ())), preferred_elemen...  3.22 us
  transfers between devices with their start and end apart: 25, of which 14 were waited for; matrix products, arithmetic and copies ran while one was open for 6% of the time, Pallas kernels for 0%

profile of v4, /device:TPU:1, one launch (start us, length us, event | category | flops | bytes accessed | tf_op | source)
XLA Modules:
  0.0 108.8 jit_solution(3351963390934077118)
XLA Ops:
  1.9 1.1 fusion.12
  3.0 2.5 %collective-permute-start.4 = (bf16[272,512]{1,0:T(8,128)(2,1)S(1)}, bf16[272,512]{1,0:T(8,128)(2,1)S(1)}, u32[]{:S(2)}, u32[]{:S(2)}) collective-permute-start(bf16[272,512]{1,0:T(8,128)(2,1)S(1)} %get-tuple-element.23.refs_0_), channel_id=1, source_target_pairs={{0,32},{8,40},{16,48},{24,56},{32,64},{40,72},{48,80},{56,88},{64,... | collective-permute-start | bytes 835592 | tf_op jit(solution)/shard_map/ppermute | solution.py:21
  5.6 5.0 %collective-permute-start.3 = (bf16[272,512]{1,0:T(8,128)(2,1)S(1)}, bf16[272,512]{1,0:T(8,128)(2,1)S(1)}, u32[]{:S(2)}, u32[]{:S(2)}) collective-permute-start(bf16[272,512]{1,0:T(8,128)(2,1)S(1)} %get-tuple-element.24.refs_5_), channel_id=1, source_target_pairs={{0,228},{4,224},{32,4},{36,0},{64,36},{68,32},{96,68},{100,64},{12... | collective-permute-start | bytes 835592 | tf_op jit(solution)/shard_map/ppermute | solution.py:224
  10.6 1.4 %collective-permute-start.2 = (bf16[272,512]{1,0:T(8,128)(2,1)S(1)}, bf16[272,512]{1,0:T(8,128)(2,1)S(1)}, u32[]{:S(2)}, u32[]{:S(2)}) collective-permute-start(bf16[272,512]{1,0:T(8,128)(2,1)S(1)} %get-tuple-element.24.refs_5_), channel_id=1, source_target_pairs={{0,224},{32,0},{64,32},{96,64},{128,96},{160,128},{192,160},{224,1... | collective-permute-start | bytes 835592 | tf_op jit(solution)/shard_map/ppermute | solution.py:21
  12.2 3.7 %collective-permute-done.4.refs_4_ = bf16[272,512]{1,0:T(8,128)(2,1)S(1)} collective-permute-done((bf16[272,512]{1,0:T(8,128)(2,1)S(1)}, bf16[272,512]{1,0:T(8,128)(2,1)S(1)}, u32[]{:S(2)}, u32[]{:S(2)}) %collective-permute-start.4) | collective-permute-done | bytes 278560 | tf_op jit(solution)/shard_map/ppermute | solution.py:21
  16.0 2.6 %collective-permute-start.6 = (bf16[272,512]{1,0:T(8,128)(2,1)S(1)}, bf16[272,512]{1,0:T(8,128)(2,1)S(1)}, u32[]{:S(2)}, u32[]{:S(2)}) collective-permute-start(bf16[272,512]{1,0:T(8,128)(2,1)S(1)} %get-tuple-element.44), channel_id=1, source_target_pairs={{0,24},{8,0},{16,8},{24,16},{1,25},{9,1},{17,9},{25,17},{2,26},{10... | collective-permute-start | bytes 835592 | tf_op jit(solution)/shard_map/ppermute | solution.py:21
  19.6 2.3 %collective-permute-done.2.refs_9_ = bf16[272,512]{1,0:T(8,128)(2,1)S(1)} collective-permute-done((bf16[272,512]{1,0:T(8,128)(2,1)S(1)}, bf16[272,512]{1,0:T(8,128)(2,1)S(1)}, u32[]{:S(2)}, u32[]{:S(2)}) %collective-permute-start.2) | collective-permute-done | bytes 278560 | tf_op jit(solution)/shard_map/ppermute | solution.py:21
  22.0 1.5 %collective-permute-start.7 = (bf16[272,512]{1,0:T(8,128)(2,1)S(1)}, bf16[272,512]{1,0:T(8,128)(2,1)S(1)}, u32[]{:S(2)}, u32[]{:S(2)}) collective-permute-start(bf16[272,512]{1,0:T(8,128)(2,1)S(1)} %get-tuple-element.24.refs_5_), channel_id=1, source_target_pairs={{0,2},{2,0},{1,3},{3,1},{4,6},{6,4},{5,7},{7,5},{8,10},{10,8},{9,1... | collective-permute-start | bytes 835592 | tf_op jit(solution)/shard_map/ppermute | solution.py:21
  24.0 4.5 %collective-permute-done.5.refs_2_ = bf16[272,512]{1,0:T(8,128)(2,1)S(1)} collective-permute-done((bf16[272,512]{1,0:T(8,128)(2,1)S(1)}, bf16[272,512]{1,0:T(8,128)(2,1)S(1)}, u32[]{:S(2)}, u32[]{:S(2)}) %collective-permute-start.5) | collective-permute-done | bytes 278560 | tf_op jit(solution)/shard_map/ppermute | solution.py:21
  28.5 5.7 %collective-permute-start.8 = (bf16[272,512]{1,0:T(8,128)(2,1)S(1)}, bf16[272,512]{1,0:T(8,128)(2,1)S(1)}, u32[]{:S(2)}, u32[]{:S(2)}) collective-permute-start(bf16[272,512]{1,0:T(8,128)(2,1)S(1)} %collective-permute-done.1.refs_6_), channel_id=1, source_target_pairs={{0,2},{2,0},{1,3},{3,1},{4,6},{6,4},{5,7},{7,5},{8,10},{10,8},{9,1... | collective-permute-start | bytes 835592 | tf_op jit(solution)/shard_map/ppermute | solution.py:21
  37.2 16.1 %shard_map.93 = (bf16[512,256]{1,0:T(8,128)(2,1)}, bf16[512,256]{1,0:T(8,128)(2,1)}, bf16[512,256]{1,0:T(8,128)(2,1)}, bf16[512,256]{1,0:T(8,128)(2,1)}, bf16[51...) custom-call(bf16[272,512]{1,0:T(8,128)(2,1)} %copy-done, ...), custom_call_target="tpu_custom_call" | custom-call | flops 12000000000 | bytes 9000000 | tf_op jit(solution)/shard_map/pallas_call | solution.py:173
  54.2 1.4 %collective-permute-done.11 = bf16[512,512]{1,0:T(8,128)(2,1)S(1)} collective-permute-done((bf16[512,512]{1,0:T(8,128)(2,1)}, bf16[512,512]{1,0:T(8,128)(2,1)S(1)}, u32[]{:S(2)}, u32[]{:S(2)}) %collective-permute-start.11) | collective-permute-done | bytes 524320 | tf_op jit(solution)/shard_map/ppermute | solution.py:21
  55.6 1.2 %add_convert_fusion.2 = bf16[512,512]{1,0:T(8,128)(2,1)S(1)} fusion(bf16[512,512]{1,0:T(8,128)(2,1)S(1)} %collective-permute-done.11, bf16[512,512]{1,0:T(8,128)(2,1)} %get-tuple-element.30), kind=kLoop, calls=%fused_computation.4 | loop fusion | flops 1048576 | bytes 1572864 | tf_op jit(solution)/shard_map/convert_element_type | solution.py:235
  56.8 11.9 %all_to_all.18 = bf16[8,64,512]{2,1,0:T(8,128)(2,1)S(1)} all-to-all(bf16[8,64,512]{2,1,0:T(8,128)(2,1)S(1)} %bitcast.12), channel_id=1, replica_groups=mesh['z'=8,'x'=4,'yl'=2,'c'=2,'rep'=2] {'x','yl'}, dimensions={0} | all-to-all | bytes 1048576 | tf_op jit(solution)/shard_map/all_to_all | solution.py:25
  68.8 1.6 %collective-permute-start.14 = (bf16[64,512]{1,0:T(8,128)(2,1)S(1)}, bf16[64,512]{1,0:T(8,128)(2,1)S(1)}, u32[]{:S(2)}, u32[]{:S(2)}) collective-permute-start(bf16[64,512]{1,0:T(8,128)(2,1)S(1)} %reduce_sum.12), channel_id=1, source_target_pairs={{0,192},{32,224},{64,0},{96,32},{128,64},{160,96},{192,128},{224,1... | collective-permute-start | bytes 196616 | tf_op jit(solution)/shard_map/ppermute | solution.py:21
  70.3 1.0 collective-permute-start.16
  71.3 1.4 %collective-permute-start.17 = (bf16[512,256]{1,0:T(8,128)(2,1)}, bf16[512,256]{1,0:T(8,128)(2,1)S(1)}, u32[]{:S(2)}, u32[]{:S(2)}) collective-permute-start(bf16[512,256]{1,0:T(8,128)(2,1)} %get-tuple-element.34), channel_id=1, source_target_pairs={{0,16},{8,24},{16,0},{24,8},{1,17},{9,25},{17,1},{25,9},{2,18},{10... | collective-permute-start | bytes 786440 | tf_op jit(solution)/shard_map/ppermute | solution.py:21
  72.7 0.7 collective-permute-start.13
  74.5 2.5 %collective-permute-done.13 = bf16[64,512]{1,0:T(8,128)(2,1)S(1)} collective-permute-done((bf16[64,512]{1,0:T(8,128)(2,1)S(1)}, bf16[64,512]{1,0:T(8,128)(2,1)S(1)}, u32[]{:S(2)}, u32[]{:S(2)}) %collective-permute-start.13) | collective-permute-done | bytes 65568 | tf_op jit(solution)/shard_map/ppermute | solution.py:21
  77.0 0.9 collective-permute-start.21
  77.9 3.3 %collective-permute-start.15 = (bf16[64,512]{1,0:T(8,128)(2,1)S(1)}, bf16[64,512]{1,0:T(8,128)(2,1)S(1)}, u32[]{:S(2)}, u32[]{:S(2)}) collective-permute-start(bf16[64,512]{1,0:T(8,128)(2,1)S(1)} %add_convert_fusion.4), channel_id=1, source_target_pairs={{0,128},{32,160},{64,192},{96,224},{128,0},{160,32},{192,64},{224,... | collective-permute-start | bytes 196616 | tf_op jit(solution)/shard_map/ppermute | solution.py:21
  81.2 5.1 %collective-permute-done.18 = bf16[512,256]{1,0:T(8,128)(2,1)S(1)} collective-permute-done((bf16[512,256]{1,0:T(8,128)(2,1)}, bf16[512,256]{1,0:T(8,128)(2,1)S(1)}, u32[]{:S(2)}, u32[]{:S(2)}) %collective-permute-start.18) | collective-permute-done | bytes 262176 | tf_op jit(solution)/shard_map/ppermute | solution.py:21
  86.3 0.9 fusion.10
  88.0 0.8 broadcast_in_dim.16
  88.8 3.8 %all-to-all-start.1 = ((bf16[8,64,512]{2,1,0:T(8,128)(2,1)}), bf16[8,64,512]{2,1,0:T(8,128)(2,1)S(1)}, u32[]{:S(2)}, u32[]{:S(2)}) async-start(bf16[8,64,512]{2,1,0:T(8,128)(2,1)} %broadcast_in_dim.16), calls=%async_computation.1 | async-start | bytes 1048576 | tf_op jit(solution)/shard_map/all_to_all | solution.py:25
  92.8 0.8 collective-permute-start.22
  94.3 2.2 %convolution_convert_fusion.1 = bf16[256,512]{1,0:T(8,128)(2,1)} fusion(bf16[512,512]{1,0:T(8,128)(2,1)S(1)} %copy-done.10, bf16[512,256]{1,0:T(8,128)(2,1)S(1)} %collective-permute-done.16, bf16[512,256]{1,0:T(8,128)(2,1)S(1)} %copy-done.7, bf16[512,256]{1,0:T(8,128)(2,1)S(1)} %copy-done.9, bf16[512,256]{1,0:T(8,128)(2,1)} %collective-permute-done.19, ...), kind=kOutput, calls=%fused_computation.2 | convolution fusion | flops 136052736 | bytes 2097155 | tf_op jit(solution)/shard_map/dot_general | solution.py:244
  96.4 2.9 %collective-permute-done.22 = bf16[512,256]{1,0:T(8,128)(2,1)S(1)} collective-permute-done((bf16[512,256]{1,0:T(8,128)(2,1)S(1)}, bf16[512,256]{1,0:T(8,128)(2,1)S(1)}, u32[]{:S(2)}, u32[]{:S(2)}) %collective-permute-start.22) | collective-permute-done | bytes 262176 | tf_op jit(solution)/shard_map/ppermute | solution.py:21
  99.3 1.1 convolution_convert_fusion
  100.4 5.4 %collective-permute-start.23 = (bf16[512,512]{1,0:T(8,128)(2,1)S(1)}, bf16[512,512]{1,0:T(8,128)(2,1)S(1)}, u32[]{:S(2)}, u32[]{:S(2)}) collective-permute-start(bf16[512,512]{1,0:T(8,128)(2,1)S(1)} %bitcast.13), channel_id=1, source_target_pairs={{0,2},{2,0},{1,3},{3,1},{4,6},{6,4},{5,7},{7,5},{8,10},{10,8},{9,1... | collective-permute-start | bytes 1572872 | tf_op jit(solution)/shard_map/ppermute | solution.py:21
  105.8 1.5 %collective-permute-done.23 = bf16[512,512]{1,0:T(8,128)(2,1)S(1)} collective-permute-done((bf16[512,512]{1,0:T(8,128)(2,1)S(1)}, bf16[512,512]{1,0:T(8,128)(2,1)S(1)}, u32[]{:S(2)}, u32[]{:S(2)}) %collective-permute-start.23) | collective-permute-done | bytes 524320 | tf_op jit(solution)/shard_map/ppermute | solution.py:21
  107.3 1.5 %select_convert_fusion = (f32[512,512]{1,0:T(8,128)}, f32[512,512]{1,0:T(8,128)}) fusion(bf16[512,512]{1,0:T(8,128)(2,1)S(1)} %collective-permute-done.23, bf16[512,512]{1,0:T(8,128)(2,1)S(1)} %bitcast.14, pred[]{:T(512)S(6)} %eq.4), kind=kLoop, calls=%fused_computation.25 | loop fusion | flops 1048576 | bytes 3145729 | tf_op jit(solution)/shard_map/convert_element_type | solution.py:299
  (81 shorter events, 9.7 us)
Async XLA Ops:
  3.0 33.2 %copy-start = (bf16[272,512]{1,0:T(8,128)(2,1)}, bf16[272,512]{1,0:T(8,128)(2,1)S(1)}, u32[]{:S(2)}) copy-start(bf16[272,512]{1,0:T(8,128)(2,1)S(1)} %get-tuple-element.23.refs_0_) | copy-start | bytes 835588
  3.0 33.2 %copy-start.3 = (bf16[272,512]{1,0:T(8,128)(2,1)}, bf16[272,512]{1,0:T(8,128)(2,1)S(1)}, u32[]{:S(2)}) copy-start(bf16[272,512]{1,0:T(8,128)(2,1)S(1)} %get-tuple-element.24.refs_5_) | copy-start | bytes 835588
  3.0 12.9 %collective-permute-start.4 = (bf16[272,512]{1,0:T(8,128)(2,1)S(1)}, bf16[272,512]{1,0:T(8,128)(2,1)S(1)}, u32[]{:S(2)}, u32[]{:S(2)}) collective-permute-start(bf16[272,512]{1,0:T(8,128)(2,1)S(1)} %get-tuple-element.23.refs_0_), channel_id=1, source_target_pairs={{0,32},{8,40},{16,48},{24,56},{32,64},{40,72},{48,80},{56,88},{64,... | collective-permute-start | bytes 835592 | tf_op jit(solution)/shard_map/ppermute | solution.py:21
  5.6 13.4 %collective-permute-start.3 = (bf16[272,512]{1,0:T(8,128)(2,1)S(1)}, bf16[272,512]{1,0:T(8,128)(2,1)S(1)}, u32[]{:S(2)}, u32[]{:S(2)}) collective-permute-start(bf16[272,512]{1,0:T(8,128)(2,1)S(1)} %get-tuple-element.24.refs_5_), channel_id=1, source_target_pairs={{0,228},{4,224},{32,4},{36,0},{64,36},{68,32},{96,68},{100,64},{12... | collective-permute-start | bytes 835592 | tf_op jit(solution)/shard_map/ppermute | solution.py:224
  10.6 11.3 %collective-permute-start.2 = (bf16[272,512]{1,0:T(8,128)(2,1)S(1)}, bf16[272,512]{1,0:T(8,128)(2,1)S(1)}, u32[]{:S(2)}, u32[]{:S(2)}) collective-permute-start(bf16[272,512]{1,0:T(8,128)(2,1)S(1)} %get-tuple-element.24.refs_5_), channel_id=1, source_target_pairs={{0,224},{32,0},{64,32},{96,64},{128,96},{160,128},{192,160},{224,1... | collective-permute-start | bytes 835592 | tf_op jit(solution)/shard_map/ppermute | solution.py:21
  12.0 11.5 %collective-permute-start.1 = (bf16[272,512]{1,0:T(8,128)(2,1)S(1)}, bf16[272,512]{1,0:T(8,128)(2,1)S(1)}, u32[]{:S(2)}, u32[]{:S(2)}) collective-permute-start(bf16[272,512]{1,0:T(8,128)(2,1)S(1)} %get-tuple-element.24.refs_5_), channel_id=1, source_target_pairs={{0,4},{4,0},{1,5},{5,1},{2,6},{6,2},{3,7},{7,3},{8,12},{12,8},{9,1... | collective-permute-start | bytes 835592 | tf_op jit(solution)/shard_map/ppermute | solution.py:21
  15.9 20.3 %copy-start.4 = (bf16[272,512]{1,0:T(8,128)(2,1)}, bf16[272,512]{1,0:T(8,128)(2,1)S(1)}, u32[]{:S(2)}) copy-start(bf16[272,512]{1,0:T(8,128)(2,1)S(1)} %collective-permute-done.4.refs_4_) | copy-start | bytes 835588
  16.0 8.1 %collective-permute-start.6 = (bf16[272,512]{1,0:T(8,128)(2,1)S(1)}, bf16[272,512]{1,0:T(8,128)(2,1)S(1)}, u32[]{:S(2)}, u32[]{:S(2)}) collective-permute-start(bf16[272,512]{1,0:T(8,128)(2,1)S(1)} %get-tuple-element.44), channel_id=1, source_target_pairs={{0,24},{8,0},{16,8},{24,16},{1,25},{9,1},{17,9},{25,17},{2,26},{10... | collective-permute-start | bytes 835592 | tf_op jit(solution)/shard_map/ppermute | solution.py:21
  18.5 10.0 %collective-permute-start.5 = (bf16[272,512]{1,0:T(8,128)(2,1)S(1)}, bf16[272,512]{1,0:T(8,128)(2,1)S(1)}, u32[]{:S(2)}, u32[]{:S(2)}) collective-permute-start(bf16[272,512]{1,0:T(8,128)(2,1)S(1)} %get-tuple-element.45), channel_id=1, source_target_pairs={{0,16},{8,24},{16,0},{24,8},{1,17},{9,25},{17,1},{25,9},{2,18},{10... | collective-permute-start | bytes 835592 | tf_op jit(solution)/shard_map/ppermute | solution.py:21
  19.0 17.2 %copy-start.11 = (bf16[272,512]{1,0:T(8,128)(2,1)}, bf16[272,512]{1,0:T(8,128)(2,1)S(1)}, u32[]{:S(2)}) copy-start(bf16[272,512]{1,0:T(8,128)(2,1)S(1)} %collective-permute-done.3.refs_10_) | copy-start | bytes 835588
  19.0 15.7 %collective-permute-start = (bf16[272,512]{1,0:T(8,128)(2,1)S(1)}, bf16[272,512]{1,0:T(8,128)(2,1)S(1)}, u32[]{:S(2)}, u32[]{:S(2)}) collective-permute-start(bf16[272,512]{1,0:T(8,128)(2,1)S(1)} %get-tuple-element.23.refs_0_), channel_id=1, source_target_pairs={{0,8},{8,16},{16,24},{24,32},{32,40},{40,48},{48,56},{56,64},{64,7... | collective-permute-start | bytes 835592 | tf_op jit(solution)/shard_map/ppermute | solution.py:21
  22.0 14.2 %copy-start.12 = (bf16[272,512]{1,0:T(8,128)(2,1)}, bf16[272,512]{1,0:T(8,128)(2,1)S(1)}, u32[]{:S(2)}) copy-start(bf16[272,512]{1,0:T(8,128)(2,1)S(1)} %collective-permute-done.2.refs_9_) | copy-start | bytes 835588
  22.0 12.8 %collective-permute-start.7 = (bf16[272,512]{1,0:T(8,128)(2,1)S(1)}, bf16[272,512]{1,0:T(8,128)(2,1)S(1)}, u32[]{:S(2)}, u32[]{:S(2)}) collective-permute-start(bf16[272,512]{1,0:T(8,128)(2,1)S(1)} %get-tuple-element.24.refs_5_), channel_id=1, source_target_pairs={{0,2},{2,0},{1,3},{3,1},{4,6},{6,4},{5,7},{7,5},{8,10},{10,8},{9,1... | collective-permute-start | bytes 835592 | tf_op jit(solution)/shard_map/ppermute | solution.py:21
  23.5 12.7 %copy-start.13 = (bf16[272,512]{1,0:T(8,128)(2,1)}, bf16[272,512]{1,0:T(8,128)(2,1)S(1)}, u32[]{:S(2)}) copy-start(bf16[272,512]{1,0:T(8,128)(2,1)S(1)} %collective-permute-done.1.refs_6_) | copy-start | bytes 835588
  28.5 6.9 %collective-permute-start.8 = (bf16[272,512]{1,0:T(8,128)(2,1)S(1)}, bf16[272,512]{1,0:T(8,128)(2,1)S(1)}, u32[]{:S(2)}, u32[]{:S(2)}) collective-permute-start(bf16[272,512]{1,0:T(8,128)(2,1)S(1)} %collective-permute-done.1.refs_6_), channel_id=1, source_target_pairs={{0,2},{2,0},{1,3},{3,1},{4,6},{6,4},{5,7},{7,5},{8,10},{10,8},{9,1... | collective-permute-start | bytes 835592 | tf_op jit(solution)/shard_map/ppermute | solution.py:21
  34.2 1.6 %collective-permute-start.9 = (bf16[272,512]{1,0:T(8,128)(2,1)S(1)}, bf16[272,512]{1,0:T(8,128)(2,1)S(1)}, u32[]{:S(2)}, u32[]{:S(2)}) collective-permute-start(bf16[272,512]{1,0:T(8,128)(2,1)S(1)} %collective-permute-done.2.refs_9_), channel_id=1, source_target_pairs={{0,2},{2,0},{1,3},{3,1},{4,6},{6,4},{5,7},{7,5},{8,10},{10,8},{9,1... | collective-permute-start | bytes 835592 | tf_op jit(solution)/shard_map/ppermute | solution.py:21
  34.2 2.0 %collective-permute-start.10 = (bf16[272,512]{1,0:T(8,128)(2,1)S(1)}, bf16[272,512]{1,0:T(8,128)(2,1)S(1)}, u32[]{:S(2)}, u32[]{:S(2)}) collective-permute-start(bf16[272,512]{1,0:T(8,128)(2,1)S(1)} %collective-permute-done.3.refs_10_), channel_id=1, source_target_pairs={{0,2},{2,0},{1,3},{3,1},{4,6},{6,4},{5,7},{7,5},{8,10},{10,8},{9,1... | collective-permute-start | bytes 835592 | tf_op jit(solution)/shard_map/ppermute | solution.py:21
  53.3 2.2 %collective-permute-start.11 = (bf16[512,512]{1,0:T(8,128)(2,1)}, bf16[512,512]{1,0:T(8,128)(2,1)S(1)}, u32[]{:S(2)}, u32[]{:S(2)}) collective-permute-start(bf16[512,512]{1,0:T(8,128)(2,1)} %get-tuple-element.31), channel_id=1, source_target_pairs={{0,2},{2,0},{1,3},{3,1},{4,6},{6,4},{5,7},{7,5},{8,10},{10,8},{9,1... | collective-permute-start | bytes 1572872 | tf_op jit(solution)/shard_map/ppermute | solution.py:21
  53.8 18.9 %collective-permute-start.20 = (bf16[4,512,256]{2,1,0:T(8,128)(2,1)}, bf16[4,512,256]{2,1,0:T(8,128)(2,1)S(1)}, u32[]{:S(2)}, u32[]{:S(2)}) collective-permute-start(bf16[4,512,256]{2,1,0:T(8,128)(2,1)} %get-tuple-element.38), channel_id=1, source_target_pairs={{0,2},{2,0},{1,3},{3,1},{4,6},{6,4},{5,7},{7,5},{8,10},{10,8},{9,1... | collective-permute-start | bytes 3145736 | tf_op jit(solution)/shard_map/ppermute | solution.py:21
  56.8 17.4 %copy-start.1 = (bf16[4,512,256]{2,1,0:T(8,128)(2,1)S(1)}, bf16[4,512,256]{2,1,0:T(8,128)(2,1)}, u32[]{:S(2)}) copy-start(bf16[4,512,256]{2,1,0:T(8,128)(2,1)} %get-tuple-element.37) | copy-start | bytes 3145732
  68.8 4.8 %collective-permute-start.14 = (bf16[64,512]{1,0:T(8,128)(2,1)S(1)}, bf16[64,512]{1,0:T(8,128)(2,1)S(1)}, u32[]{:S(2)}, u32[]{:S(2)}) collective-permute-start(bf16[64,512]{1,0:T(8,128)(2,1)S(1)} %reduce_sum.12), channel_id=1, source_target_pairs={{0,192},{32,224},{64,0},{96,32},{128,64},{160,96},{192,128},{224,1... | collective-permute-start | bytes 196616 | tf_op jit(solution)/shard_map/ppermute | solution.py:21
  70.3 10.9 %collective-permute-start.16 = (bf16[512,256]{1,0:T(8,128)(2,1)}, bf16[512,256]{1,0:T(8,128)(2,1)S(1)}, u32[]{:S(2)}, u32[]{:S(2)}) collective-permute-start(bf16[512,256]{1,0:T(8,128)(2,1)} %get-tuple-element.33), channel_id=1, source_target_pairs={{0,24},{8,0},{16,8},{24,16},{1,25},{9,1},{17,9},{25,17},{2,26},{10... | collective-permute-start | bytes 786440 | tf_op jit(solution)/shard_map/ppermute | solution.py:21
  71.3 9.9 %collective-permute-start.17 = (bf16[512,256]{1,0:T(8,128)(2,1)}, bf16[512,256]{1,0:T(8,128)(2,1)S(1)}, u32[]{:S(2)}, u32[]{:S(2)}) collective-permute-start(bf16[512,256]{1,0:T(8,128)(2,1)} %get-tuple-element.34), channel_id=1, source_target_pairs={{0,16},{8,24},{16,0},{24,8},{1,17},{9,25},{17,1},{25,9},{2,18},{10... | collective-permute-start | bytes 786440 | tf_op jit(solution)/shard_map/ppermute | solution.py:21
  72.7 13.6 %collective-permute-start.18 = (bf16[512,256]{1,0:T(8,128)(2,1)}, bf16[512,256]{1,0:T(8,128)(2,1)S(1)}, u32[]{:S(2)}, u32[]{:S(2)}) collective-permute-start(bf16[512,256]{1,0:T(8,128)(2,1)} %get-tuple-element.35), channel_id=1, source_target_pairs={{0,8},{8,16},{16,24},{24,0},{1,9},{9,17},{17,25},{25,1},{2,10},{10... | collective-permute-start | bytes 786440 | tf_op jit(solution)/shard_map/ppermute | solution.py:21
  72.7 4.3 %collective-permute-start.13 = (bf16[64,512]{1,0:T(8,128)(2,1)S(1)}, bf16[64,512]{1,0:T(8,128)(2,1)S(1)}, u32[]{:S(2)}, u32[]{:S(2)}) collective-permute-start(bf16[64,512]{1,0:T(8,128)(2,1)S(1)} %reduce_sum.12), channel_id=1, source_target_pairs={{0,224},{32,0},{64,32},{96,64},{128,96},{160,128},{192,160},{224,1... | collective-permute-start | bytes 196616 | tf_op jit(solution)/shard_map/ppermute | solution.py:21
  73.5 4.3 %collective-permute-start.12 = (bf16[64,512]{1,0:T(8,128)(2,1)S(1)}, bf16[64,512]{1,0:T(8,128)(2,1)S(1)}, u32[]{:S(2)}, u32[]{:S(2)}) collective-permute-start(bf16[64,512]{1,0:T(8,128)(2,1)S(1)} %reduce_sum.12), channel_id=1, source_target_pairs={{0,32},{32,64},{64,96},{96,128},{128,160},{160,192},{192,224},{224... | collective-permute-start | bytes 196616 | tf_op jit(solution)/shard_map/ppermute | solution.py:21
  77.0 15.7 %collective-permute-start.21 = (bf16[2,512,256]{2,1,0:T(8,128)(2,1)S(1)}, bf16[2,512,256]{2,1,0:T(8,128)(2,1)S(1)}, u32[]{:S(2)}, u32[]{:S(2)}) collective-permute-start(bf16[2,512,256]{2,1,0:T(8,128)(2,1)S(1)} %slice.17), channel_id=1, source_target_pairs={{0,4},{4,0},{1,5},{5,1},{2,6},{6,2},{3,7},{7,3},{8,12},{12,8},{9,1... | collective-permute-start | bytes 1572872 | tf_op jit(solution)/shard_map/ppermute | solution.py:21
  77.9 10.0 %collective-permute-start.15 = (bf16[64,512]{1,0:T(8,128)(2,1)S(1)}, bf16[64,512]{1,0:T(8,128)(2,1)S(1)}, u32[]{:S(2)}, u32[]{:S(2)}) collective-permute-start(bf16[64,512]{1,0:T(8,128)(2,1)S(1)} %add_convert_fusion.4), channel_id=1, source_target_pairs={{0,128},{32,160},{64,192},{96,224},{128,0},{160,32},{192,64},{224,... | collective-permute-start | bytes 196616 | tf_op jit(solution)/shard_map/ppermute | solution.py:21
  87.2 7.0 %collective-permute-start.19 = (bf16[512,256]{1,0:T(8,128)(2,1)}, bf16[512,256]{1,0:T(8,128)(2,1)}, u32[]{:S(2)}, u32[]{:S(2)}) collective-permute-start(bf16[512,256]{1,0:T(8,128)(2,1)} %fusion.10), channel_id=1, source_target_pairs={{0,224},{32,0},{64,32},{96,64},{128,96},{160,128},{192,160},{224,1... | collective-permute-start | bytes 786440 | tf_op jit(solution)/shard_map/ppermute | solution.py:21
  88.8 11.6 %all-to-all-start.1 = ((bf16[8,64,512]{2,1,0:T(8,128)(2,1)}), bf16[8,64,512]{2,1,0:T(8,128)(2,1)S(1)}, u32[]{:S(2)}, u32[]{:S(2)}) async-start(bf16[8,64,512]{2,1,0:T(8,128)(2,1)} %broadcast_in_dim.16), calls=%async_computation.1 | async-start | bytes 1048576 | tf_op jit(solution)/shard_map/all_to_all | solution.py:25
  92.8 6.5 %collective-permute-start.22 = (bf16[512,256]{1,0:T(8,128)(2,1)S(1)}, bf16[512,256]{1,0:T(8,128)(2,1)S(1)}, u32[]{:S(2)}, u32[]{:S(2)}) collective-permute-start(bf16[512,256]{1,0:T(8,128)(2,1)S(1)} %slice_bitcast_fusion), channel_id=1, source_target_pairs={{0,32},{32,64},{64,96},{96,128},{128,160},{160,192},{192,224},{224... | collective-permute-start | bytes 786440 | tf_op jit(solution)/shard_map/ppermute | solution.py:21
  100.4 6.9 %collective-permute-start.23 = (bf16[512,512]{1,0:T(8,128)(2,1)S(1)}, bf16[512,512]{1,0:T(8,128)(2,1)S(1)}, u32[]{:S(2)}, u32[]{:S(2)}) collective-permute-start(bf16[512,512]{1,0:T(8,128)(2,1)S(1)} %bitcast.13), channel_id=1, source_target_pairs={{0,2},{2,0},{1,3},{3,1},{4,6},{6,4},{5,7},{7,5},{8,10},{10,8},{9,1... | collective-permute-start | bytes 1572872 | tf_op jit(solution)/shard_map/ppermute | solution.py:21
  (15 other events, 57.2 us)

commit v5 on v4

--- a/solution.py
+++ b/solution.py
@@ -38,9 +38,9 @@
     text_hbm = refs[5:13]
     ha_hbm, ht_hbm = refs[13:15]
     da_hbm = refs[15:20]
-    mine_hbm, send_hbm, keep_hbm, give_hbm = refs[20:24]
+    mine_hbm, send_hbm, keep, give = refs[20:24]
     (ae, al, te, tl, ha, ht, za, zat, zt, ua, ut, na, nt, ea, eb, ga, gt) = refs[24:41]
-    (da, dt, keep, give, in_sem, out_sem) = refs[41:]
+    (da, dt, in_sem, out_sem) = refs[41:]
     width = ha.shape[0]
     rows = ae.shape[0] // 5
     core = lax.axis_index("c")
@@ -159,7 +159,6 @@
         keep[...] = head_t
         give[...] = head_a
 
-    outs += send([(give, give_hbm), (keep, keep_hbm)], 13)
     for c in outs:
         c.wait()
 
@@ -180,7 +179,7 @@
             shape((width, width), BF),
         ),
         in_specs=[anywhere] * 15,
-        out_specs=(anywhere,) * 9,
+        out_specs=(anywhere,) * 7 + (pl.BlockSpec(memory_space=pltpu.VMEM),) * 2,
         scratch_shapes=[
             vmem((5 * rows, width), BF),
             vmem((5, PAD, width), BF),
@@ -201,12 +200,10 @@
             vmem((width, 8 * rows), F32),
             vmem((width, 5 * rows), BF),
             vmem((width, 8 * rows), BF),
-            vmem((width, width), BF),
-            vmem((width, width), BF),
             pltpu.SemaphoreType.DMA((28,)),
-            pltpu.SemaphoreType.DMA((15,)),
+            pltpu.SemaphoreType.DMA((13,)),
         ],
-        compiler_params=pltpu.CompilerParams(vmem_limit_bytes=60 * 1024 * 1024),
+        compiler_params=pltpu.CompilerParams(vmem_limit_bytes=48 * 1024 * 1024),
         cost_estimate=pl.CostEstimate(
             flops=12_000_000_000, bytes_accessed=9_000_000, transcendentals=2_100_000
         ),
@@ -264,7 +261,7 @@
     t_c = shift(t_own, "c", 1)
     a_2 = shift(jnp.where(x + 2 < 4, a_own, a_4), "x", 2)
     a_3 = shift(jnp.where(x + 3 < 4, a_own, a_4), "x", 3)
-    t_y, t_next, t_next_y, a_2, a_3 = together((t_y, t_next, t_next_y, a_2, a_3))
+    t_next_y, a_2, a_3 = together((t_next_y, a_2, a_3))
     audio = [a_own, a_1, a_2, a_3, a_4]
     here = [t_own, t_y, t_c, shift(t_y, "c", 1)]
     ahead = [t_next, t_next_y, shift(t_next, "c", 1), shift(t_next_y, "c", 1)]

time: 109 us -> 106 us (0.972)
  waiting for transfers between devices: 26.7 us -> 20.5 us
  starting transfers between devices: 41.6 us -> 45.4 us
    ppermute x23, starting transfers between devices: 32.8 us -> 40.4 us  [shift(): lax.ppermute(value, axis, [(i, (i + steps) % count) for i in range(count)])]
    ppermute x23, waiting for transfers between devices: 26.7 us -> 20.5 us  [shift(): lax.ppermute(value, axis, [(i, (i + steps) % count) for i in range(count)])]
    ppermute x1, starting transfers between devices: 5.04 us -> 1.26 us  [diagonal_shift(): return lax.ppermute(value, ('z', 'yl'), pairs)]
  transfers between devices with their start and end apart: 25 -> 25, of which waited for: 14 -> 10; matrix products, arithmetic and copies ran while one was open for 6% -> 7% of each run, Pallas kernels for 0% -> 0%
where the time goes in v5:
time: 106 us
  starting transfers between devices  45.4 us (43%)
  waiting for transfers between devices  20.5 us (19%)
  Pallas kernels  16.1 us (15%)
  blocking collectives  11.8 us (11%)
  other arithmetic  5.61 us (5%)
  matrix products  3.23 us (3%)
  local copies, waits for them, and re-layouts  2.25 us (2%)
    ppermute x23, starting transfers between devices, shift(): lax.ppermute(value, axis, [(i, (i + steps) % count) for i in range(count)])  40.4 us
    ppermute x23, waiting for transfers between devices, shift(): lax.ppermute(value, axis, [(i, (i + steps) % count) for i in range(count)])  20.5 us
    pallas_call x1, Pallas kernels, tiles(): pl.pallas_call(functools.partial(tiles_kernel, 1.0 / batch_rows), out_sha...  16.1 us
    all_to_all x1, blocking collectives, exchange(): return lax.all_to_all(value, axis, split_axis=0, concat_axis=0, tiled=True)  11.8 us
    all_to_all x1, starting transfers between devices, exchange(): return lax.all_to_all(value, axis, split_axis=0, concat_axis=0, tiled=True)  3.78 us
    dot_general x2, matrix products, dot_head(): lax.dot_general(dproj_t, head, (((0,), (1,)), ((), ())), preferred_elemen...  3.23 us
  transfers between devices with their start and end apart: 25, of which 10 were waited for; matrix products, arithmetic and copies ran while one was open for 7% of the time, Pallas kernels for 0%

profile of v5, /device:TPU:1, one launch (start us, length us, event | category | flops | bytes accessed | tf_op | source)
XLA Modules:
  0.0 105.8 jit_solution(7343223428117301787)
XLA Ops:
  1.9 1.1 %fusion.12 = (bf16[272,512]{1,0:T(8,128)(2,1)S(1)}, bf16[272,512]{1,0:T(8,128)(2,1)S(1)}) fusion(bf16[1,256]{1,0:T(2,128)(2,1)S(1)} %stack.6, bf16[256,512]{1,0:T(8,128)(2,1)} %param.6, bf16[1,256]{1,0:T(2,128)(2,1)S(1)} %stack.7, bf16[256,512]{1,0:T(8,128)(2,1)} %param.7), kind=kLoop, calls=%fused_computation.27 | loop fusion | flops 1531904 | bytes 1082368 | tf_op jit(solution)/shard_map/concatenate | solution.py:215
  3.0 2.5 %collective-permute-start.2 = (bf16[272,512]{1,0:T(8,128)(2,1)S(1)}, bf16[272,512]{1,0:T(8,128)(2,1)S(1)}, u32[]{:S(2)}, u32[]{:S(2)}) collective-permute-start(bf16[272,512]{1,0:T(8,128)(2,1)S(1)} %get-tuple-element.21.refs_0_), channel_id=1, source_target_pairs={{0,32},{8,40},{16,48},{24,56},{32,64},{40,72},{48,80},{56,88},{64,... | collective-permute-start | bytes 835592 | tf_op jit(solution)/shard_map/ppermute | solution.py:21
  5.6 4.0 %collective-permute-start.8 = (bf16[272,512]{1,0:T(8,128)(2,1)S(1)}, bf16[272,512]{1,0:T(8,128)(2,1)S(1)}, u32[]{:S(2)}, u32[]{:S(2)}) collective-permute-start(bf16[272,512]{1,0:T(8,128)(2,1)S(1)} %get-tuple-element.22.refs_5_), channel_id=1, source_target_pairs={{0,224},{32,0},{64,32},{96,64},{128,96},{160,128},{192,160},{224,1... | collective-permute-start | bytes 835592 | tf_op jit(solution)/shard_map/ppermute | solution.py:21
  9.6 1.3 %collective-permute-start.5 = (bf16[272,512]{1,0:T(8,128)(2,1)S(1)}, bf16[272,512]{1,0:T(8,128)(2,1)S(1)}, u32[]{:S(2)}, u32[]{:S(2)}) collective-permute-start(bf16[272,512]{1,0:T(8,128)(2,1)S(1)} %get-tuple-element.22.refs_5_), channel_id=1, source_target_pairs={{0,4},{4,0},{1,5},{5,1},{2,6},{6,2},{3,7},{7,3},{8,12},{12,8},{9,1... | collective-permute-start | bytes 835592 | tf_op jit(solution)/shard_map/ppermute | solution.py:21
  10.9 1.3 %collective-permute-start.1 = (bf16[272,512]{1,0:T(8,128)(2,1)S(1)}, bf16[272,512]{1,0:T(8,128)(2,1)S(1)}, u32[]{:S(2)}, u32[]{:S(2)}) collective-permute-start(bf16[272,512]{1,0:T(8,128)(2,1)S(1)} %get-tuple-element.22.refs_5_), channel_id=1, source_target_pairs={{0,228},{4,224},{32,4},{36,0},{64,36},{68,32},{96,68},{100,64},{12... | collective-permute-start | bytes 835592 | tf_op jit(solution)/shard_map/ppermute | solution.py:221
  12.2 3.7 %collective-permute-done.2.refs_4_ = bf16[272,512]{1,0:T(8,128)(2,1)S(1)} collective-permute-done((bf16[272,512]{1,0:T(8,128)(2,1)S(1)}, bf16[272,512]{1,0:T(8,128)(2,1)S(1)}, u32[]{:S(2)}, u32[]{:S(2)}) %collective-permute-start.2) | collective-permute-done | bytes 278560 | tf_op jit(solution)/shard_map/ppermute | solution.py:21
  15.9 2.6 %collective-permute-start.4 = (bf16[272,512]{1,0:T(8,128)(2,1)S(1)}, bf16[272,512]{1,0:T(8,128)(2,1)S(1)}, u32[]{:S(2)}, u32[]{:S(2)}) collective-permute-start(bf16[272,512]{1,0:T(8,128)(2,1)S(1)} %get-tuple-element.40), channel_id=1, source_target_pairs={{0,24},{8,0},{16,8},{24,16},{1,25},{9,1},{17,9},{25,17},{2,26},{10... | collective-permute-start | bytes 835592 | tf_op jit(solution)/shard_map/ppermute | solution.py:21
  19.6 3.2 %collective-permute-done.5.refs_6_ = bf16[272,512]{1,0:T(8,128)(2,1)S(1)} collective-permute-done((bf16[272,512]{1,0:T(8,128)(2,1)S(1)}, bf16[272,512]{1,0:T(8,128)(2,1)S(1)}, u32[]{:S(2)}, u32[]{:S(2)}) %collective-permute-start.5) | collective-permute-done | bytes 278560 | tf_op jit(solution)/shard_map/ppermute | solution.py:21
  22.8 1.9 %collective-permute-start.6 = (bf16[272,512]{1,0:T(8,128)(2,1)S(1)}, bf16[272,512]{1,0:T(8,128)(2,1)S(1)}, u32[]{:S(2)}, u32[]{:S(2)}) collective-permute-start(bf16[272,512]{1,0:T(8,128)(2,1)S(1)} %get-tuple-element.22.refs_5_), channel_id=1, source_target_pairs={{0,2},{2,0},{1,3},{3,1},{4,6},{6,4},{5,7},{7,5},{8,10},{10,8},{9,1... | collective-permute-start | bytes 835592 | tf_op jit(solution)/shard_map/ppermute | solution.py:21
  24.7 6.7 %collective-permute-start.7 = (bf16[272,512]{1,0:T(8,128)(2,1)S(1)}, bf16[272,512]{1,0:T(8,128)(2,1)S(1)}, u32[]{:S(2)}, u32[]{:S(2)}) collective-permute-start(bf16[272,512]{1,0:T(8,128)(2,1)S(1)} %collective-permute-done.5.refs_6_), channel_id=1, source_target_pairs={{0,2},{2,0},{1,3},{3,1},{4,6},{6,4},{5,7},{7,5},{8,10},{10,8},{9,1... | collective-permute-start | bytes 835592 | tf_op jit(solution)/shard_map/ppermute | solution.py:21
  31.4 2.8 %collective-permute-start.10 = (bf16[272,512]{1,0:T(8,128)(2,1)S(1)}, bf16[272,512]{1,0:T(8,128)(2,1)S(1)}, u32[]{:S(2)}, u32[]{:S(2)}) collective-permute-start(bf16[272,512]{1,0:T(8,128)(2,1)S(1)} %collective-permute-done.1.refs_10_), channel_id=1, source_target_pairs={{0,2},{2,0},{1,3},{3,1},{4,6},{6,4},{5,7},{7,5},{8,10},{10,8},{9,1... | collective-permute-start | bytes 835592 | tf_op jit(solution)/shard_map/ppermute | solution.py:21
  34.2 1.2 %collective-permute-done.10.refs_12_ = bf16[272,512]{1,0:T(8,128)(2,1)S(1)} collective-permute-done((bf16[272,512]{1,0:T(8,128)(2,1)S(1)}, bf16[272,512]{1,0:T(8,128)(2,1)S(1)}, u32[]{:S(2)}, u32[]{:S(2)}) %collective-permute-start.10) | collective-permute-done | bytes 278560 | tf_op jit(solution)/shard_map/ppermute | solution.py:21
  35.4 16.1 %shard_map.93 = (bf16[512,256]{1,0:T(8,128)(2,1)S(1)}, bf16[512,256]{1,0:T(8,128)(2,1)S(1)}, bf16[512,256]{1,0:T(8,128)(2,1)S(1)}, bf16[512,256]{1,0:T(8,128)(2,...) custom-call(bf16[272,512]{1,0:T(8,128)(2,1)S(1)} %get-tuple-element., ...), custom_call_target="tpu_custom_call" | custom-call | flops 12000000000 | bytes 9000000 | tf_op jit(solution)/shard_map/pallas_call | solution.py:172
  52.3 1.4 %collective-permute-done.11 = bf16[512,512]{1,0:T(8,128)(2,1)S(1)} collective-permute-done((bf16[512,512]{1,0:T(8,128)(2,1)S(1)}, bf16[512,512]{1,0:T(8,128)(2,1)S(1)}, u32[]{:S(2)}, u32[]{:S(2)}) %collective-permute-start.11) | collective-permute-done | bytes 524320 | tf_op jit(solution)/shard_map/ppermute | solution.py:21
  53.9 11.8 %all_to_all.18 = bf16[8,64,512]{2,1,0:T(8,128)(2,1)S(1)} all-to-all(bf16[8,64,512]{2,1,0:T(8,128)(2,1)S(1)} %bitcast.12), channel_id=1, replica_groups=mesh['z'=8,'x'=4,'yl'=2,'c'=2,'rep'=2] {'x','yl'}, dimensions={0} | all-to-all | bytes 1048576 | tf_op jit(solution)/shard_map/all_to_all | solution.py:25
  65.8 1.6 %collective-permute-start.14 = (bf16[64,512]{1,0:T(8,128)(2,1)S(1)}, bf16[64,512]{1,0:T(8,128)(2,1)S(1)}, u32[]{:S(2)}, u32[]{:S(2)}) collective-permute-start(bf16[64,512]{1,0:T(8,128)(2,1)S(1)} %reduce_sum.12), channel_id=1, source_target_pairs={{0,192},{32,224},{64,0},{96,32},{128,64},{160,96},{192,128},{224,1... | collective-permute-start | bytes 196616 | tf_op jit(solution)/shard_map/ppermute | solution.py:21
  67.4 1.0 collective-permute-start.16
  68.4 1.4 %collective-permute-start.17 = (bf16[512,256]{1,0:T(8,128)(2,1)S(1)}, bf16[512,256]{1,0:T(8,128)(2,1)S(1)}, u32[]{:S(2)}, u32[]{:S(2)}) collective-permute-start(bf16[512,256]{1,0:T(8,128)(2,1)S(1)} %get-tuple-element.30), channel_id=1, source_target_pairs={{0,16},{8,24},{16,0},{24,8},{1,17},{9,25},{17,1},{25,9},{2,18},{10... | collective-permute-start | bytes 786440 | tf_op jit(solution)/shard_map/ppermute | solution.py:21
  71.2 1.8 %add_convert_fusion = bf16[4,512,256]{2,1,0:T(8,128)(2,1)S(1)} fusion(bf16[4,512,256]{2,1,0:T(8,128)(2,1)} %collective-permute-done.20, bf16[4,512,256]{2,1,0:T(8,128)(2,1)} %get-tuple-element.33), kind=kLoop, calls=%fused_computation | loop fusion | flops 2097152 | bytes 3145728 | tf_op jit(solution)/shard_map/convert_element_type | solution.py:232
  73.1 0.9 collective-permute-done.13
  74.0 0.9 collective-permute-start.21
  75.0 3.2 %collective-permute-start.15 = (bf16[64,512]{1,0:T(8,128)(2,1)S(1)}, bf16[64,512]{1,0:T(8,128)(2,1)S(1)}, u32[]{:S(2)}, u32[]{:S(2)}) collective-permute-start(bf16[64,512]{1,0:T(8,128)(2,1)S(1)} %add_convert_fusion.4), channel_id=1, source_target_pairs={{0,128},{32,160},{64,192},{96,224},{128,0},{160,32},{192,64},{224,... | collective-permute-start | bytes 196616 | tf_op jit(solution)/shard_map/ppermute | solution.py:21
  78.2 4.9 %collective-permute-done.18 = bf16[512,256]{1,0:T(8,128)(2,1)S(1)} collective-permute-done((bf16[512,256]{1,0:T(8,128)(2,1)S(1)}, bf16[512,256]{1,0:T(8,128)(2,1)S(1)}, u32[]{:S(2)}, u32[]{:S(2)}) %collective-permute-start.18) | collective-permute-done | bytes 262176 | tf_op jit(solution)/shard_map/ppermute | solution.py:21
  83.2 0.9 fusion.10
  84.9 0.8 broadcast_in_dim.16
  85.7 3.8 %all-to-all-start.1 = ((bf16[8,64,512]{2,1,0:T(8,128)(2,1)}), bf16[8,64,512]{2,1,0:T(8,128)(2,1)S(1)}, u32[]{:S(2)}, u32[]{:S(2)}) async-start(bf16[8,64,512]{2,1,0:T(8,128)(2,1)} %broadcast_in_dim.16), calls=%async_computation.1 | async-start | bytes 1048576 | tf_op jit(solution)/shard_map/all_to_all | solution.py:25
  91.2 2.2 %convolution_convert_fusion.1 = bf16[256,512]{1,0:T(8,128)(2,1)} fusion(bf16[512,512]{1,0:T(8,128)(2,1)S(1)} %copy-done.7, bf16[512,256]{1,0:T(8,128)(2,1)S(1)} %collective-permute-done.16, bf16[512,256]{1,0:T(8,128)(2,1)S(1)} %copy-done.4, bf16[512,256]{1,0:T(8,128)(2,1)S(1)} %copy-done.6, bf16[512,256]{1,0:T(8,128)(2,1)} %collective-permute-done.19, ...), kind=kOutput, calls=%fused_computation.2 | convolution fusion | flops 136052736 | bytes 2097155 | tf_op jit(solution)/shard_map/dot_general | solution.py:241
  93.4 2.8 %collective-permute-done.22 = bf16[512,256]{1,0:T(8,128)(2,1)S(1)} collective-permute-done((bf16[512,256]{1,0:T(8,128)(2,1)S(1)}, bf16[512,256]{1,0:T(8,128)(2,1)S(1)}, u32[]{:S(2)}, u32[]{:S(2)}) %collective-permute-start.22) | collective-permute-done | bytes 262176 | tf_op jit(solution)/shard_map/ppermute | solution.py:21
  96.2 1.1 %convolution_convert_fusion = bf16[256,512]{1,0:T(8,128)(2,1)} fusion(bf16[512,512]{1,0:T(8,128)(2,1)S(1)} %copy-done.2, bf16[512,256]{1,0:T(8,128)(2,1)S(1)} %collective-permute-done.22, bf16[2,512,256]{2,1,0:T(8,128)(2,1)S(1)} %add_convert_fusion.1), kind=kOutput, calls=%fused_computation.1 | convolution fusion | flops 134873088 | bytes 1310720 | tf_op jit(solution)/shard_map/dot_general | solution.py:241
  97.3 5.6 %collective-permute-start.23 = (bf16[512,512]{1,0:T(8,128)(2,1)S(1)}, bf16[512,512]{1,0:T(8,128)(2,1)S(1)}, u32[]{:S(2)}, u32[]{:S(2)}) collective-permute-start(bf16[512,512]{1,0:T(8,128)(2,1)S(1)} %bitcast.13), channel_id=1, source_target_pairs={{0,2},{2,0},{1,3},{3,1},{4,6},{6,4},{5,7},{7,5},{8,10},{10,8},{9,1... | collective-permute-start | bytes 1572872 | tf_op jit(solution)/shard_map/ppermute | solution.py:21
  102.8 1.5 %collective-permute-done.23 = bf16[512,512]{1,0:T(8,128)(2,1)S(1)} collective-permute-done((bf16[512,512]{1,0:T(8,128)(2,1)S(1)}, bf16[512,512]{1,0:T(8,128)(2,1)S(1)}, u32[]{:S(2)}, u32[]{:S(2)}) %collective-permute-start.23) | collective-permute-done | bytes 524320 | tf_op jit(solution)/shard_map/ppermute | solution.py:21
  104.4 1.5 %select_convert_fusion = (f32[512,512]{1,0:T(8,128)}, f32[512,512]{1,0:T(8,128)}) fusion(bf16[512,512]{1,0:T(8,128)(2,1)S(1)} %collective-permute-done.23, bf16[512,512]{1,0:T(8,128)(2,1)S(1)} %bitcast.14, pred[]{:T(512)S(6)} %eq.4), kind=kLoop, calls=%fused_computation.25 | loop fusion | flops 1048576 | bytes 3145729 | tf_op jit(solution)/shard_map/convert_element_type | solution.py:296
  (53 shorter events, 7.6 us)
Async XLA Ops:
  3.0 12.9 %collective-permute-start.2 = (bf16[272,512]{1,0:T(8,128)(2,1)S(1)}, bf16[272,512]{1,0:T(8,128)(2,1)S(1)}, u32[]{:S(2)}, u32[]{:S(2)}) collective-permute-start(bf16[272,512]{1,0:T(8,128)(2,1)S(1)} %get-tuple-element.21.refs_0_), channel_id=1, source_target_pairs={{0,32},{8,40},{16,48},{24,56},{32,64},{40,72},{48,80},{56,88},{64,... | collective-permute-start | bytes 835592 | tf_op jit(solution)/shard_map/ppermute | solution.py:21
  5.6 13.4 %collective-permute-start.8 = (bf16[272,512]{1,0:T(8,128)(2,1)S(1)}, bf16[272,512]{1,0:T(8,128)(2,1)S(1)}, u32[]{:S(2)}, u32[]{:S(2)}) collective-permute-start(bf16[272,512]{1,0:T(8,128)(2,1)S(1)} %get-tuple-element.22.refs_5_), channel_id=1, source_target_pairs={{0,224},{32,0},{64,32},{96,64},{128,96},{160,128},{192,160},{224,1... | collective-permute-start | bytes 835592 | tf_op jit(solution)/shard_map/ppermute | solution.py:21
  9.6 13.2 %collective-permute-start.5 = (bf16[272,512]{1,0:T(8,128)(2,1)S(1)}, bf16[272,512]{1,0:T(8,128)(2,1)S(1)}, u32[]{:S(2)}, u32[]{:S(2)}) collective-permute-start(bf16[272,512]{1,0:T(8,128)(2,1)S(1)} %get-tuple-element.22.refs_5_), channel_id=1, source_target_pairs={{0,4},{4,0},{1,5},{5,1},{2,6},{6,2},{3,7},{7,3},{8,12},{12,8},{9,1... | collective-permute-start | bytes 835592 | tf_op jit(solution)/shard_map/ppermute | solution.py:21
  10.9 13.7 %collective-permute-start.1 = (bf16[272,512]{1,0:T(8,128)(2,1)S(1)}, bf16[272,512]{1,0:T(8,128)(2,1)S(1)}, u32[]{:S(2)}, u32[]{:S(2)}) collective-permute-start(bf16[272,512]{1,0:T(8,128)(2,1)S(1)} %get-tuple-element.22.refs_5_), channel_id=1, source_target_pairs={{0,228},{4,224},{32,4},{36,0},{64,36},{68,32},{96,68},{100,64},{12... | collective-permute-start | bytes 835592 | tf_op jit(solution)/shard_map/ppermute | solution.py:221
  15.9 8.7 %collective-permute-start.4 = (bf16[272,512]{1,0:T(8,128)(2,1)S(1)}, bf16[272,512]{1,0:T(8,128)(2,1)S(1)}, u32[]{:S(2)}, u32[]{:S(2)}) collective-permute-start(bf16[272,512]{1,0:T(8,128)(2,1)S(1)} %get-tuple-element.40), channel_id=1, source_target_pairs={{0,24},{8,0},{16,8},{24,16},{1,25},{9,1},{17,9},{25,17},{2,26},{10... | collective-permute-start | bytes 835592 | tf_op jit(solution)/shard_map/ppermute | solution.py:21
  18.5 12.9 %collective-permute-start.3 = (bf16[272,512]{1,0:T(8,128)(2,1)S(1)}, bf16[272,512]{1,0:T(8,128)(2,1)S(1)}, u32[]{:S(2)}, u32[]{:S(2)}) collective-permute-start(bf16[272,512]{1,0:T(8,128)(2,1)S(1)} %get-tuple-element.41), channel_id=1, source_target_pairs={{0,16},{8,24},{16,0},{24,8},{1,17},{9,25},{17,1},{25,9},{2,18},{10... | collective-permute-start | bytes 835592 | tf_op jit(solution)/shard_map/ppermute | solution.py:21
  19.0 15.2 %collective-permute-start = (bf16[272,512]{1,0:T(8,128)(2,1)S(1)}, bf16[272,512]{1,0:T(8,128)(2,1)S(1)}, u32[]{:S(2)}, u32[]{:S(2)}) collective-permute-start(bf16[272,512]{1,0:T(8,128)(2,1)S(1)} %get-tuple-element.21.refs_0_), channel_id=1, source_target_pairs={{0,8},{8,16},{16,24},{24,32},{32,40},{40,48},{48,56},{56,64},{64,7... | collective-permute-start | bytes 835592 | tf_op jit(solution)/shard_map/ppermute | solution.py:21
  22.8 11.4 %collective-permute-start.6 = (bf16[272,512]{1,0:T(8,128)(2,1)S(1)}, bf16[272,512]{1,0:T(8,128)(2,1)S(1)}, u32[]{:S(2)}, u32[]{:S(2)}) collective-permute-start(bf16[272,512]{1,0:T(8,128)(2,1)S(1)} %get-tuple-element.22.refs_5_), channel_id=1, source_target_pairs={{0,2},{2,0},{1,3},{3,1},{4,6},{6,4},{5,7},{7,5},{8,10},{10,8},{9,1... | collective-permute-start | bytes 835592 | tf_op jit(solution)/shard_map/ppermute | solution.py:21
  24.6 9.6 %collective-permute-start.9 = (bf16[272,512]{1,0:T(8,128)(2,1)S(1)}, bf16[272,512]{1,0:T(8,128)(2,1)S(1)}, u32[]{:S(2)}, u32[]{:S(2)}) collective-permute-start(bf16[272,512]{1,0:T(8,128)(2,1)S(1)} %collective-permute-done.8.refs_9_), channel_id=1, source_target_pairs={{0,2},{2,0},{1,3},{3,1},{4,6},{6,4},{5,7},{7,5},{8,10},{10,8},{9,1... | collective-permute-start | bytes 835592 | tf_op jit(solution)/shard_map/ppermute | solution.py:21
  24.7 9.6 %collective-permute-start.7 = (bf16[272,512]{1,0:T(8,128)(2,1)S(1)}, bf16[272,512]{1,0:T(8,128)(2,1)S(1)}, u32[]{:S(2)}, u32[]{:S(2)}) collective-permute-start(bf16[272,512]{1,0:T(8,128)(2,1)S(1)} %collective-permute-done.5.refs_6_), channel_id=1, source_target_pairs={{0,2},{2,0},{1,3},{3,1},{4,6},{6,4},{5,7},{7,5},{8,10},{10,8},{9,1... | collective-permute-start | bytes 835592 | tf_op jit(solution)/shard_map/ppermute | solution.py:21
  31.4 4.0 %collective-permute-start.10 = (bf16[272,512]{1,0:T(8,128)(2,1)S(1)}, bf16[272,512]{1,0:T(8,128)(2,1)S(1)}, u32[]{:S(2)}, u32[]{:S(2)}) collective-permute-start(bf16[272,512]{1,0:T(8,128)(2,1)S(1)} %collective-permute-done.1.refs_10_), channel_id=1, source_target_pairs={{0,2},{2,0},{1,3},{3,1},{4,6},{6,4},{5,7},{7,5},{8,10},{10,8},{9,1... | collective-permute-start | bytes 835592 | tf_op jit(solution)/shard_map/ppermute | solution.py:21
  51.5 2.2 %collective-permute-start.11 = (bf16[512,512]{1,0:T(8,128)(2,1)S(1)}, bf16[512,512]{1,0:T(8,128)(2,1)S(1)}, u32[]{:S(2)}, u32[]{:S(2)}) collective-permute-start(bf16[512,512]{1,0:T(8,128)(2,1)S(1)} %get-tuple-element.27), channel_id=1, source_target_pairs={{0,2},{2,0},{1,3},{3,1},{4,6},{6,4},{5,7},{7,5},{8,10},{10,8},{9,1... | collective-permute-start | bytes 1572872 | tf_op jit(solution)/shard_map/ppermute | solution.py:21
  52.2 17.6 %collective-permute-start.20 = (bf16[4,512,256]{2,1,0:T(8,128)(2,1)}, bf16[4,512,256]{2,1,0:T(8,128)(2,1)}, u32[]{:S(2)}, u32[]{:S(2)}) collective-permute-start(bf16[4,512,256]{2,1,0:T(8,128)(2,1)} %get-tuple-element.34), channel_id=1, source_target_pairs={{0,2},{2,0},{1,3},{3,1},{4,6},{6,4},{5,7},{7,5},{8,10},{10,8},{9,1... | collective-permute-start | bytes 3145736 | tf_op jit(solution)/shard_map/ppermute | solution.py:21
  65.8 4.8 %collective-permute-start.14 = (bf16[64,512]{1,0:T(8,128)(2,1)S(1)}, bf16[64,512]{1,0:T(8,128)(2,1)S(1)}, u32[]{:S(2)}, u32[]{:S(2)}) collective-permute-start(bf16[64,512]{1,0:T(8,128)(2,1)S(1)} %reduce_sum.12), channel_id=1, source_target_pairs={{0,192},{32,224},{64,0},{96,32},{128,64},{160,96},{192,128},{224,1... | collective-permute-start | bytes 196616 | tf_op jit(solution)/shard_map/ppermute | solution.py:21
  67.4 10.8 %collective-permute-start.16 = (bf16[512,256]{1,0:T(8,128)(2,1)S(1)}, bf16[512,256]{1,0:T(8,128)(2,1)S(1)}, u32[]{:S(2)}, u32[]{:S(2)}) collective-permute-start(bf16[512,256]{1,0:T(8,128)(2,1)S(1)} %get-tuple-element.29), channel_id=1, source_target_pairs={{0,24},{8,0},{16,8},{24,16},{1,25},{9,1},{17,9},{25,17},{2,26},{10... | collective-permute-start | bytes 786440 | tf_op jit(solution)/shard_map/ppermute | solution.py:21
  68.4 9.8 %collective-permute-start.17 = (bf16[512,256]{1,0:T(8,128)(2,1)S(1)}, bf16[512,256]{1,0:T(8,128)(2,1)S(1)}, u32[]{:S(2)}, u32[]{:S(2)}) collective-permute-start(bf16[512,256]{1,0:T(8,128)(2,1)S(1)} %get-tuple-element.30), channel_id=1, source_target_pairs={{0,16},{8,24},{16,0},{24,8},{1,17},{9,25},{17,1},{25,9},{2,18},{10... | collective-permute-start | bytes 786440 | tf_op jit(solution)/shard_map/ppermute | solution.py:21
  69.8 13.4 %collective-permute-start.18 = (bf16[512,256]{1,0:T(8,128)(2,1)S(1)}, bf16[512,256]{1,0:T(8,128)(2,1)S(1)}, u32[]{:S(2)}, u32[]{:S(2)}) collective-permute-start(bf16[512,256]{1,0:T(8,128)(2,1)S(1)} %get-tuple-element.31), channel_id=1, source_target_pairs={{0,8},{8,16},{16,24},{24,0},{1,9},{9,17},{17,25},{25,1},{2,10},{10... | collective-permute-start | bytes 786440 | tf_op jit(solution)/shard_map/ppermute | solution.py:21
  69.8 4.2 %collective-permute-start.13 = (bf16[64,512]{1,0:T(8,128)(2,1)S(1)}, bf16[64,512]{1,0:T(8,128)(2,1)S(1)}, u32[]{:S(2)}, u32[]{:S(2)}) collective-permute-start(bf16[64,512]{1,0:T(8,128)(2,1)S(1)} %reduce_sum.12), channel_id=1, source_target_pairs={{0,224},{32,0},{64,32},{96,64},{128,96},{160,128},{192,160},{224,1... | collective-permute-start | bytes 196616 | tf_op jit(solution)/shard_map/ppermute | solution.py:21
  70.6 4.3 %collective-permute-start.12 = (bf16[64,512]{1,0:T(8,128)(2,1)S(1)}, bf16[64,512]{1,0:T(8,128)(2,1)S(1)}, u32[]{:S(2)}, u32[]{:S(2)}) collective-permute-start(bf16[64,512]{1,0:T(8,128)(2,1)S(1)} %reduce_sum.12), channel_id=1, source_target_pairs={{0,32},{32,64},{64,96},{96,128},{128,160},{160,192},{192,224},{224... | collective-permute-start | bytes 196616 | tf_op jit(solution)/shard_map/ppermute | solution.py:21
  73.0 11.0 %copy-start = (bf16[4,512,256]{2,1,0:T(8,128)(2,1)}, bf16[4,512,256]{2,1,0:T(8,128)(2,1)S(1)}, u32[]{:S(2)}) copy-start(bf16[4,512,256]{2,1,0:T(8,128)(2,1)S(1)} %add_convert_fusion) | copy-start | bytes 3145732
  74.0 15.5 %collective-permute-start.21 = (bf16[2,512,256]{2,1,0:T(8,128)(2,1)S(1)}, bf16[2,512,256]{2,1,0:T(8,128)(2,1)S(1)}, u32[]{:S(2)}, u32[]{:S(2)}) collective-permute-start(bf16[2,512,256]{2,1,0:T(8,128)(2,1)S(1)} %slice.17), channel_id=1, source_target_pairs={{0,4},{4,0},{1,5},{5,1},{2,6},{6,2},{3,7},{7,3},{8,12},{12,8},{9,1... | collective-permute-start | bytes 1572872 | tf_op jit(solution)/shard_map/ppermute | solution.py:21
  75.0 9.8 %collective-permute-start.15 = (bf16[64,512]{1,0:T(8,128)(2,1)S(1)}, bf16[64,512]{1,0:T(8,128)(2,1)S(1)}, u32[]{:S(2)}, u32[]{:S(2)}) collective-permute-start(bf16[64,512]{1,0:T(8,128)(2,1)S(1)} %add_convert_fusion.4), channel_id=1, source_target_pairs={{0,128},{32,160},{64,192},{96,224},{128,0},{160,32},{192,64},{224,... | collective-permute-start | bytes 196616 | tf_op jit(solution)/shard_map/ppermute | solution.py:21
  78.2 5.8 %copy-start.3 = (bf16[512,256]{1,0:T(8,128)(2,1)}, bf16[512,256]{1,0:T(8,128)(2,1)S(1)}, u32[]{:S(2)}) copy-start(bf16[512,256]{1,0:T(8,128)(2,1)S(1)} %collective-permute-done.17) | copy-start | bytes 786436
  84.0 7.1 %collective-permute-start.19 = (bf16[512,256]{1,0:T(8,128)(2,1)}, bf16[512,256]{1,0:T(8,128)(2,1)}, u32[]{:S(2)}, u32[]{:S(2)}) collective-permute-start(bf16[512,256]{1,0:T(8,128)(2,1)} %fusion.10), channel_id=1, source_target_pairs={{0,224},{32,0},{64,32},{96,64},{128,96},{160,128},{192,160},{224,1... | collective-permute-start | bytes 786440 | tf_op jit(solution)/shard_map/ppermute | solution.py:21
  84.8 4.7 %copy-start.1 = (bf16[4,512,256]{2,1,0:T(8,128)(2,1)S(1)}, bf16[4,512,256]{2,1,0:T(8,128)(2,1)}, u32[]{:S(2)}) copy-start(bf16[4,512,256]{2,1,0:T(8,128)(2,1)} %copy-done) | copy-start | bytes 3145732
  85.7 11.6 %all-to-all-start.1 = ((bf16[8,64,512]{2,1,0:T(8,128)(2,1)}), bf16[8,64,512]{2,1,0:T(8,128)(2,1)S(1)}, u32[]{:S(2)}, u32[]{:S(2)}) async-start(bf16[8,64,512]{2,1,0:T(8,128)(2,1)} %broadcast_in_dim.16), calls=%async_computation.1 | async-start | bytes 1048576 | tf_op jit(solution)/shard_map/all_to_all | solution.py:25
  89.5 1.7 %copy-start.4 = (bf16[512,256]{1,0:T(8,128)(2,1)S(1)}, bf16[512,256]{1,0:T(8,128)(2,1)}, u32[]{:S(2)}) copy-start(bf16[512,256]{1,0:T(8,128)(2,1)} %copy-done.3) | copy-start | bytes 786436
  89.5 1.7 %copy-start.6 = (bf16[512,256]{1,0:T(8,128)(2,1)S(1)}, bf16[512,256]{1,0:T(8,128)(2,1)}, u32[]{:S(2)}) copy-start(bf16[512,256]{1,0:T(8,128)(2,1)} %copy-done.5) | copy-start | bytes 786436
  89.5 1.7 %copy-start.7 = (bf16[512,512]{1,0:T(8,128)(2,1)S(1)}, bf16[512,512]{1,0:T(8,128)(2,1)}, u32[]{:S(2)}) copy-start(bf16[512,512]{1,0:T(8,128)(2,1)} %refs_13_.1) | copy-start | bytes 1572868
  89.7 6.5 %collective-permute-start.22 = (bf16[512,256]{1,0:T(8,128)(2,1)S(1)}, bf16[512,256]{1,0:T(8,128)(2,1)S(1)}, u32[]{:S(2)}, u32[]{:S(2)}) collective-permute-start(bf16[512,256]{1,0:T(8,128)(2,1)S(1)} %slice_bitcast_fusion), channel_id=1, source_target_pairs={{0,32},{32,64},{64,96},{96,128},{128,160},{160,192},{192,224},{224... | collective-permute-start | bytes 786440 | tf_op jit(solution)/shard_map/ppermute | solution.py:21
  91.2 5.0 %copy-start.2 = (bf16[512,512]{1,0:T(8,128)(2,1)S(1)}, bf16[512,512]{1,0:T(8,128)(2,1)}, u32[]{:S(2)}) copy-start(bf16[512,512]{1,0:T(8,128)(2,1)} %refs_14_.1) | copy-start | bytes 1572868
  97.3 7.1 %collective-permute-start.23 = (bf16[512,512]{1,0:T(8,128)(2,1)S(1)}, bf16[512,512]{1,0:T(8,128)(2,1)S(1)}, u32[]{:S(2)}, u32[]{:S(2)}) collective-permute-start(bf16[512,512]{1,0:T(8,128)(2,1)S(1)} %bitcast.13), channel_id=1, source_target_pairs={{0,2},{2,0},{1,3},{3,1},{4,6},{6,4},{5,7},{7,5},{8,10},{10,8},{9,1... | collective-permute-start | bytes 1572872 | tf_op jit(solution)/shard_map/ppermute | solution.py:21
  (1 other events, 0.9 us)
